TPU v7x, 32 devices: a whole 2x2x4 slice. The times are simulated.
32 devices in a mesh: groups: 2 (over y), space: 4 (over x, core), chan: 4 (over z).
Axes of the slice: x: 2, y: 2, z: 4, core: 2. Of those that a mesh axis runs over, the one named last changes fastest.
Arguments:
- volume: bfloat16 [32, 16, 256, 256], P(('groups', 'space'), 'chan'), parts along dimension 0, may hold values from -6 to 6
- weight: bfloat16 [8, 256, 256], P(None, 'space', 'chan'), may hold values from -0.125 to 0.125
- cotangent: bfloat16 [16, 8, 128, 256], P(('groups', 'space'), None, None, 'chan'), parts along dimension 0, may hold values from -6 to 6
Outputs:
- grad_volume: bfloat16 [32, 16, 256, 256], P(('groups', 'space'), 'chan'), parts along dimension 0
- grad_weight: float32 [16, 256, 256], P('groups', 'space', 'chan'), parts along dimension 0
There are 2 independent parts, one for each index of `groups`. A program takes and returns all parts, laid end to end along the dimension named above; an argument that names none is the same for every part. Nothing has to cross between parts.
All inputs are finite; a program needn't handle non-finite values.
Results may differ from a plain program's by a relative error of at most 0.0049.
Values may be sent and summed in bfloat16 or wider, within the bound.
No kernel may reach another device: no remote copies, remote signals or barrier semaphores. Data moves between devices by JAX's collectives and lax.ppermute only.
A program may use at most 64 MiB of HBM per device.

v0:
```python
import jax
import jax.numpy as jnp
from jax import lax
from jax.sharding import PartitionSpec as P


def patch_rows(block):
    cells_x, cells_y, cells_z, in_chan = block.shape
    shaped = block.reshape(cells_x // 2, 2, cells_y // 2, 2, cells_z // 2, 2, in_chan)
    return shaped.transpose(0, 2, 4, 1, 3, 5, 6).reshape(-1, 8, in_chan)


def unpatch(rows, cells_x, cells_y, cells_z):
    in_chan = rows.shape[2]
    shaped = rows.reshape(cells_x // 2, cells_y // 2, cells_z // 2, 2, 2, 2, in_chan)
    return shaped.transpose(0, 3, 1, 4, 2, 5, 6).reshape(cells_x, cells_y, cells_z, in_chan)


def shards(volume, weight, cotangent):
    cells_x, cells_y, cells_z, in_chan = volume.shape
    patches = patch_rows(volume)
    out_rows = patches.shape[0]
    wide_w = lax.all_gather(weight, "chan", axis=2, tiled=True)
    cot_tiles = lax.all_to_all(cotangent, "chan", split_axis=1, concat_axis=3, tiled=True)
    out_chan = cot_tiles.shape[3]
    upstream = cot_tiles.reshape(out_rows, out_chan)
    whole_w = lax.all_gather(wide_w, "space", axis=1, tiled=True)
    pre_act = jnp.einsum("mkc,kco->mo", patches, whole_w, preferred_element_type=jnp.float32)
    squash = jax.nn.sigmoid(pre_act)
    slopes = squash * (1.0 + pre_act * (1.0 - squash))
    deltas = (upstream.astype(jnp.float32) * slopes).astype(jnp.bfloat16)
    grad_rows = jnp.einsum(
        "mo,kco->mkc", deltas, whole_w, preferred_element_type=jnp.float32
    ).astype(jnp.bfloat16)
    grad_volume = unpatch(grad_rows, cells_x, cells_y, cells_z)
    partial_w = jnp.einsum("mkc,mo->kco", patches, deltas, preferred_element_type=jnp.float32)
    by_chan = lax.psum_scatter(partial_w, "chan", scatter_dimension=2, tiled=True)
    owned_sum = lax.psum_scatter(by_chan, "space", scatter_dimension=1, tiled=True)
    grad_weight = owned_sum / out_rows
    return (grad_volume, grad_weight)


def solution(mesh):
    return jax.shard_map(
        shards,
        mesh=mesh,
        in_specs=(
            P(("groups", "space"), "chan", None, None),
            P(None, "space", "chan"),
            P(("groups", "space"), None, None, "chan"),
        ),
        out_specs=(P(("groups", "space"), "chan", None, None), P("groups", "space", "chan")),
        check_vma=False,
    )
```

profile of v0, /device:TPU:0, one launch (start us, length us, event | category | flops | bytes accessed | tf_op | source)
XLA Modules:
  0.0 126.0 jit_solution(15146380185082460627)
XLA Ops:
  7.2 0.0 copy-start.2
  7.2 0.0 copy-start
  7.2 0.0 all-gather.2.cloned.1.call-start
  7.2 1.2 copy.19
  8.4 17.4 %all_gather.6 = bf16[8,64,256]{1,0,2:T(8,128)(2,1)S(1)} all-gather(bf16[8,64,64]{1,0,2:T(8,128)(2,1)S(1)} %copy.19), channel_id=1, replica_groups=mesh['groups'=2,'space'=4,'chan'=4] {'chan'}, dimensions={2}, use_global_device_ids=true | all-gather | bytes 327680 | tf_op jit(solution)/shard_map/all_gather | solution.py:23
  25.8 1.0 copy.20
  26.8 0.0 all-gather.2.cloned.1.call-update
  26.8 0.0 copy-done.2
  26.9 0.7 copy.16
  27.6 5.4 %all-to-all-start = ((bf16[2,8,128,64]{2,3,0,1:T(8,128)(2,1)}), bf16[2,8,128,64]{2,3,0,1:T(8,128)(2,1)S(1)}, u32[]{:S(2)}, u32[]{:S(2)}) async-start(bf16[2,8,128,64]{2,3,0,1:T(8,128)(2,1)} %copy.16), calls=%async_computation | async-start | bytes 524288 | tf_op jit(solution)/shard_map/all_to_all | solution.py:24
  33.0 0.0 reduce-scatter.5.cloned.1.call-start
  33.0 0.0 copy-done
  33.0 2.2 %reshape.22 = bf16[2,2,2,2,128,2,256]{6,5,4,3,2,1,0:T(2,128)(2,1)} reshape(bf16[4,4,256,256]{3,2,1,0:T(8,128)(2,1)S(1)} %copy-done) | data formatting | bytes 4194304 | tf_op jit(solution)/shard_map/reshape | solution.py:9
  35.2 2.1 %copy.18 = bf16[2,2,128,2,2,2,256]{6,2,1,0,5,4,3:T(8,128)(2,1)S(1)} copy(bf16[2,2,128,2,2,2,256]{6,5,2,4,1,3,0:T(2,128)(2,1)} %bitcast.37) | data formatting | bytes 4194304 | tf_op jit(solution)/shard_map/transpose | solution.py:10
  37.3 2.4 %all-to-all-done = bf16[2,8,128,64]{2,3,0,1:T(8,128)(2,1)S(1)} async-done(((bf16[2,8,128,64]{2,3,0,1:T(8,128)(2,1)}), bf16[2,8,128,64]{2,3,0,1:T(8,128)(2,1)S(1)}, u32[]{:S(2)}, u32[]{:S(2)}) %all-to-all-start) | async-done | bytes 262176 | tf_op jit(solution)/shard_map/all_to_all | solution.py:24
  39.7 0.3 copy.30
  40.0 0.4 reshape.26
  40.4 1.0 copy.21
  41.4 4.0 %all-gather.2.cloned.1.call-done = bf16[8,256,256]{2,1,0:T(8,128)(2,1)} async-done(((bf16[8,64,256]{2,1,0:T(8,128)(2,1)}), bf16[8,256,256]{2,1,0:T(8,128)(2,1)}) %all-gather.2.cloned.1.call-update) | async-done | bytes 1048592 | tf_op jit(solution)/shard_map/all_gather | solution.py:27
  45.5 2.1 %fusion = bf16[512,256,1]{1,0,2:T(8,128)(2,1)S(1)} fusion(f32[512,256]{1,0:T(8,128)} %copy.21, bf16[512,8,256]{2,0,1:T(8,128)(2,1)S(1)} %bitcast.34, bf16[8,256,256]{2,1,0:T(8,128)(2,1)} %all-gather.2.cloned.1.call-done), kind=kOutput, calls=%fused_computation.5 | convolution fusion | flops 538050560 | bytes 3932160 | tf_op jit(solution)/shard_map/mkc,kco->mo/dot_general | solution.py:28
  47.6 2.0 %convolution_bitcast_fusion = f32[8,256,256]{1,2,0:T(8,128)} fusion(bf16[512,256,1]{1,0,2:T(8,128)(2,1)S(1)} %fusion, bf16[512,8,256]{2,0,1:T(8,128)(2,1)S(1)} %bitcast.35), kind=kOutput, calls=%fused_computation.1 | convolution fusion | flops 536870912 | bytes 4456448 | tf_op jit(solution)/shard_map/mkc,mo->kco/dot_general | solution.py:36
  49.7 0.0 reduce-scatter.5.cloned.1.call-update
  49.7 0.0 copy-start.1
  49.7 0.0 reduce-scatter.7.cloned.1.call-start
  49.8 44.0 %reduce-scatter.5.cloned.1.call-done = f32[8,256,64]{1,2,0:T(8,128)} async-done(((f32[8,256,256]{1,2,0:T(8,128)}), f32[8,256,64]{1,2,0:T(8,128)}) %reduce-scatter.5.cloned.1.call-update) | async-done | bytes 524304 | tf_op jit(solution)/shard_map/reduce_scatter | solution.py:37
  93.7 1.5 %copy.27 = f32[8,256,64]{2,0,1:T(8,128)S(1)} copy(f32[8,256,64]{1,2,0:T(8,128)} %reduce-scatter.5.cloned.1.call-done) | data formatting | bytes 1048576
  95.2 1.1 reshape.31
  96.3 0.0 reduce-scatter.7.cloned.1.call-update
  96.3 0.0 copy-done.1
  96.3 0.7 convolution_convert_fusion
  97.1 2.2 %copy.22 = bf16[2,2,2,2,128,2,256]{6,5,4,3,2,1,0:T(2,128)(2,1)S(1)} copy(bf16[2,2,2,2,128,2,256]{6,4,2,0,5,3,1:T(8,128)(2,1)S(1)} %bitcast.36) | data formatting | bytes 4194304 | tf_op jit(solution)/shard_map/transpose | solution.py:16
  99.2 2.2 %reshape.25 = bf16[4,4,256,256]{3,2,1,0:T(8,128)(2,1)} reshape(bf16[2,2,2,2,128,2,256]{6,5,4,3,2,1,0:T(2,128)(2,1)S(1)} %copy.22) | data formatting | bytes 4194304 | tf_op jit(solution)/shard_map/reshape | solution.py:16
  101.4 16.0 %reduce-scatter.7.cloned.1.call-done = f32[64,512]{1,0:T(8,128)} async-done(((f32[256,512]{1,0:T(8,128)}), f32[64,512]{1,0:T(8,128)}) %reduce-scatter.7.cloned.1.call-update) | async-done | bytes 131088
  117.5 1.0 reshape.32
  118.5 0.1 copy.28
  118.7 0.8 copy.24
  (1 shorter events, 0.0 us)
Async XLA Ops:
  7.2 19.7 %copy-start.2 = (bf16[2,8,128,64]{2,3,1,0:T(8,128)(2,1)S(1)}, bf16[2,8,128,64]{2,3,1,0:T(8,128)(2,1)}, u32[]{:S(2)}) copy-start(bf16[2,8,128,64]{2,3,1,0:T(8,128)(2,1)} %param.5) | copy-start | bytes 786436
  7.2 25.8 %copy-start = (bf16[4,4,256,256]{3,2,1,0:T(8,128)(2,1)S(1)}, bf16[4,4,256,256]{3,2,1,0:T(8,128)(2,1)}, u32[]{:S(2)}) copy-start(bf16[4,4,256,256]{3,2,1,0:T(8,128)(2,1)} %param.3) | copy-start | bytes 6291460
  7.2 38.3 %all-gather.2.cloned.1.call-start = ((), (), s32[]{:S(2)}) async-start(), calls=%async_computation.3 | async-start | bytes 1310720 | tf_op jit(solution)/shard_map/all_gather | solution.py:27
  27.6 12.2 %all-to-all-start = ((bf16[2,8,128,64]{2,3,0,1:T(8,128)(2,1)}), bf16[2,8,128,64]{2,3,0,1:T(8,128)(2,1)S(1)}, u32[]{:S(2)}, u32[]{:S(2)}) async-start(bf16[2,8,128,64]{2,3,0,1:T(8,128)(2,1)} %copy.16), calls=%async_computation | async-start | bytes 524288 | tf_op jit(solution)/shard_map/all_to_all | solution.py:24
  33.0 60.8 %reduce-scatter.5.cloned.1.call-start = ((), (), s32[]{:S(2)}) async-start(), calls=%async_computation.4 | async-start | bytes 2621440 | tf_op jit(solution)/shard_map/reduce_scatter | solution.py:37
  49.7 46.6 %copy-start.1 = (bf16[8,256,256]{2,1,0:T(8,128)(2,1)S(1)}, bf16[8,256,256]{2,1,0:T(8,128)(2,1)}, u32[]{:S(2)}) copy-start(bf16[8,256,256]{2,1,0:T(8,128)(2,1)} %all-gather.2.cloned.1.call-done) | copy-start | bytes 3145732
  49.7 67.8 %reduce-scatter.7.cloned.1.call-start = ((), (), s32[]{:S(2)}) async-start(), calls=%async_computation.5 | async-start | bytes 655360
Sparse Core Ops, SparseCore 0:
  27.0 18.4 all-gather.1
  49.8 43.8 reduce-scatter.4
  96.4 20.9 reduce-scatter.6
where the time goes:
time: 126 us
  waiting for transfers between devices  66.5 us (53%)
  local copies, waits for them, and re-layouts  17.9 us (14%)
  blocking collectives  17.4 us (14%)
  between operations  13.9 us (11%)
  starting transfers between devices  5.46 us (4%)
  matrix products  4.92 us (4%)
    reduce_scatter x1, waiting for transfers between devices, shards(): lax.psum_scatter(partial_w, 'chan', scatter_dimension=2, tiled=True)  44 us
    all_gather x1, blocking collectives, shards(): wide_w = lax.all_gather(weight, 'chan', axis=2, tiled=True)  17.4 us
    unnamed x4, waiting for transfers between devices  16.1 us
    unnamed x13, local copies, waits for them, and re-layouts  6.45 us
    all_to_all x1, starting transfers between devices, shards(): lax.all_to_all(cotangent, 'chan', split_axis=1, concat_axis=3, tiled=True)  5.38 us
    all_gather x1, waiting for transfers between devices, shards(): whole_w = lax.all_gather(wide_w, 'space', axis=1, tiled=True)  4.05 us
  transfers between devices with their start and end apart: 4, of which 4 were waited for; matrix products, arithmetic and copies ran while one was open for 9% of the time, Pallas kernels for 0%

commit v1 on v0

v1 whole, which is shorter than its diff:
```python
import functools

import jax
import jax.numpy as jnp
from jax import lax
from jax.experimental import pallas as pl
from jax.experimental.pallas import tpu as pltpu
from jax.sharding import PartitionSpec as P

LANES = 128
BF16 = jnp.bfloat16
F32 = jnp.float32


def other(me, step):
    return me ^ step


def fetch(x, axis, pairs):
    return lax.ppermute(x, axis, pairs)


def lane_group(shape, width):
    return lax.broadcasted_iota(jnp.int32, shape, len(shape) - 1) // width


def merge(parts, width, flip):
    group = lane_group(parts[0].shape, width)
    out = parts[flip]
    for g in range(1, len(parts)):
        out = jnp.where(group == g, parts[g ^ flip], out)
    return out


def swap_groups(x, width, flip):
    if flip == 0:
        return x
    tiles = []
    for t in range(x.shape[1] // LANES):
        tile = x[:, t * LANES:(t + 1) * LANES]
        bit = 1
        while bit <= flip:
            if flip & bit:
                shift = width * bit
                up = pltpu.roll(tile, LANES - shift, 1)
                if 2 * shift == LANES:
                    tile = up
                else:
                    even = (lane_group(tile.shape, shift) % 2) == 0
                    tile = jnp.where(even, up, pltpu.roll(tile, shift, 1))
            bit *= 2
        tiles.append(tile)
    return tiles[0] if len(tiles) == 1 else jnp.concatenate(tiles, axis=1)


def whole(x):
    return pl.BlockSpec(x.shape, lambda *_: (0,) * len(x.shape))


def params():
    return pltpu.CompilerParams(vmem_limit_bytes=48 * 1024 * 1024)


def cost(flops, bytes_accessed):
    return pl.CostEstimate(flops=flops, bytes_accessed=bytes_accessed, transcendentals=0)


def spread(x, width, at):
    if width >= LANES:
        return x
    zeros = jnp.zeros((x.shape[0], LANES - width), x.dtype)
    full = jnp.concatenate([x, zeros], axis=1)
    return pltpu.roll(full, at * width, 1) if at else full


def pack_weight(weight, ratio):
    kinds, rows, width = weight.shape
    groups = kinds // ratio
    lanes = ratio * width

    def body(w_ref, *outs):
        for g in range(groups):
            for flip in range(ratio):
                acc = None
                for lane in range(ratio):
                    part = spread(w_ref[g * ratio + (lane ^ flip)].astype(F32), width, lane)
                    acc = part if acc is None else acc + part
                outs[flip][g] = acc.astype(BF16)

    return pl.pallas_call(
        body,
        out_shape=[jax.ShapeDtypeStruct((groups, rows, lanes), BF16)] * ratio,
        compiler_params=params(),
        name="pack_weight",
    )(weight)


def pack_cot(cot, chans, ratio):
    planes, cells_y, cells_z, width = cot.shape
    own_y = cells_y // chans
    cells = planes * own_y * cells_z
    sect = cells // ratio

    def body(c_ref, *outs):
        me = lax.axis_index("chan")
        for step in range(chans):
            flip = step % ratio
            target = other(me, step) * own_y
            mine = []
            for p in range(planes):
                for y in range(own_y):
                    mine.append(c_ref[p, target + y].astype(F32))
            rows = jnp.concatenate(mine, axis=0)
            acc = None
            for lane in range(ratio):
                sec = lane ^ flip
                part = spread(rows[sec * sect:(sec + 1) * sect], width, lane)
                acc = part if acc is None else acc + part
            outs[step][...] = acc.astype(BF16)

    return pl.pallas_call(
        body,
        out_shape=[jax.ShapeDtypeStruct((sect, ratio * width), BF16)] * chans,
        compiler_params=params(),
        name="pack_cot",
    )(cot)


def patch_rows(volume):
    cells_x, cells_y, cells_z, in_chan = volume.shape
    nx, ny, nz = cells_x // 2, cells_y // 2, cells_z // 2

    def body(v_ref, p_ref, t_ref):
        row = lax.broadcasted_iota(jnp.int32, (cells_z, cells_z), 0)
        col = lax.broadcasted_iota(jnp.int32, (cells_z, cells_z), 1)
        pick = (col == 2 * (row % nz) + row // nz).astype(F32).astype(BF16)
        for a in range(2):
            for b in range(2):
                k = 4 * a + 2 * b
                got = jnp.dot(pick, v_ref[a, b], preferred_element_type=F32)
                for e in range(2):
                    part = got[e * nz:(e + 1) * nz]
                    p_ref[k + e] = part.astype(BF16)
                    t_ref[k + e] = part.T.astype(BF16)

    rows = nx * ny * nz
    return pl.pallas_call(
        body,
        grid=(nx * ny,),
        in_specs=[pl.BlockSpec((2, 2, cells_z, in_chan), lambda n: (n // ny, n % ny, 0, 0))],
        out_specs=[
            pl.BlockSpec((8, nz, in_chan), lambda n: (0, n, 0)),
            pl.BlockSpec((8, in_chan, nz), lambda n: (0, 0, n)),
        ],
        out_shape=[
            jax.ShapeDtypeStruct((8, rows, in_chan), BF16),
            jax.ShapeDtypeStruct((8, in_chan, rows), BF16),
        ],
        compiler_params=params(),
        cost_estimate=cost(16 * rows * in_chan * cells_z, 6 * volume.size),
        name="patch_rows",
    )(volume)


def forward(patches, pieces, cots, spaces, chans, ratio):
    kinds, rows, in_chan = patches.shape
    groups, block, lanes = pieces[0][0].shape
    out_chan = lanes * (chans // ratio)
    width = lanes // ratio
    flat = [p for line in pieces for p in line]
    sect = rows // ratio

    def body(p_ref, *refs):
        ins = refs[:len(flat)]
        cot_refs = refs[len(flat):len(flat) + chans]
        d_ref, w_ref = refs[len(flat) + chans:]
        me = lax.axis_index("space")
        for j in range(spaces):
            at = pl.multiple_of(other(me, j) * block, block)
            for g in range(groups):
                for t in range(chans // ratio):
                    got = [ins[j * chans + t * ratio + u][g] for u in range(ratio)]
                    for q in range(ratio):
                        w_ref[g * ratio + q, pl.ds(at, block), t * lanes:(t + 1) * lanes] = merge(got, width, q)
        for sec in range(ratio):
            here = slice(sec * sect, (sec + 1) * sect)
            pre = None
            for q in range(ratio):
                acc = None
                for k in range(q, kinds, ratio):
                    part = jnp.dot(p_ref[k, here], w_ref[k], preferred_element_type=F32)
                    acc = part if acc is None else acc + part
                acc = swap_groups(acc, width, q)
                pre = acc if pre is None else pre + acc
            ups = []
            for t in range(chans // ratio):
                got = [cot_refs[t * ratio + u][...] for u in range(ratio)]
                ups.append(merge(got, width, sec).astype(F32))
            up = swap_groups(jnp.concatenate(ups, axis=1), width, sec)
            squash = 1.0 / (1.0 + jnp.exp(-pre))
            slopes = squash * (1.0 + pre * (1.0 - squash))
            delta = (up * slopes).astype(BF16)
            d_ref[0, here] = delta
            for q in range(1, ratio):
                d_ref[q, here] = swap_groups(delta.astype(F32), width, q).astype(BF16)

    return pl.pallas_call(
        body,
        out_shape=[
            jax.ShapeDtypeStruct((ratio, rows, out_chan), BF16),
            jax.ShapeDtypeStruct((kinds, in_chan, out_chan), BF16),
        ],
        compiler_params=params(),
        cost_estimate=cost(2 * patches.size * out_chan, 2 * patches.size),
        name="forward",
    )(patches, *flat, *cots)


def weight_part(turned, deltas, steps, spaces, dtype):
    kinds, in_chan, rows = turned.shape
    ratio, _, out_chan = deltas.shape
    block = in_chan // spaces

    def body(t_ref, d_ref, *outs):
        me = lax.axis_index("space")
        for n, step in enumerate(steps):
            at = pl.multiple_of(other(me, step) * block, block)
            for k in range(kinds):
                got = jnp.dot(t_ref[k, pl.ds(at, block)], d_ref[k % ratio], preferred_element_type=F32)
                outs[n][k] = got.astype(dtype)

    return pl.pallas_call(
        body,
        out_shape=[jax.ShapeDtypeStruct((kinds, block, out_chan), dtype)] * len(steps),
        compiler_params=params(),
        cost_estimate=cost(2 * turned.size * out_chan * len(steps) // spaces, 2 * turned.size),
        name="weight_part",
    )(turned, deltas)


def add_pairs(mine, theirs, dtypes):
    def body(*refs):
        n = len(mine)
        for i in range(n):
            refs[2 * n + i][...] = (refs[i][...].astype(F32) + refs[n + i][...].astype(F32)).astype(dtypes[i])

    return pl.pallas_call(
        body,
        out_shape=[jax.ShapeDtypeStruct(m.shape, d) for m, d in zip(mine, dtypes)],
        compiler_params=params(),
        name="add_pairs",
    )(*mine, *theirs)


def add_and_pack(mine, theirs, chans, ratio):
    kinds, block, out_chan = mine.shape
    width = out_chan // chans
    lanes = ratio * width
    groups = kinds // ratio

    def body(*refs):
        ins, outs = refs[:1 + len(theirs)], refs[1 + len(theirs):]
        for g in range(groups):
            for t in range(chans // ratio):
                lane = slice(t * lanes, (t + 1) * lanes)
                sums = []
                for q in range(ratio):
                    acc = ins[0][g * ratio + q, :, lane]
                    for ref in ins[1:]:
                        acc = acc + ref[g * ratio + q, :, lane].astype(F32)
                    sums.append(acc)
                for u in range(ratio):
                    packed = swap_groups(merge(sums, width, u), width, u)
                    out = outs[t * ratio + u]
                    out[g] = packed.astype(out.dtype)

    return pl.pallas_call(
        body,
        out_shape=[jax.ShapeDtypeStruct((groups, block, lanes), BF16 if i else F32) for i in range(chans)],
        compiler_params=params(),
        name="add_and_pack",
    )(mine, *theirs)


def finish(parts, kinds, width, scale):
    groups, block, lanes = parts[0].shape
    ratio = lanes // width

    def body(*refs):
        out = refs[-1]
        for g in range(groups):
            acc = refs[0][g]
            for ref in refs[1:-1]:
                acc = acc + ref[g].astype(F32)
            acc = acc * scale
            for q in range(ratio):
                moved = pltpu.roll(acc, lanes - q * width, 1) if q else acc
                out[g * ratio + q] = moved[:, :width]

    return pl.pallas_call(
        body,
        out_shape=jax.ShapeDtypeStruct((kinds, block, width), F32),
        compiler_params=params(),
        name="finish",
    )(*parts)


def volume_grad(deltas, weights, shape):
    cells_x, cells_y, cells_z, in_chan = shape
    nx, ny, nz = cells_x // 2, cells_y // 2, cells_z // 2
    ratio, rows, out_chan = deltas.shape

    def body(d_ref, w_ref, o_ref):
        row = lax.broadcasted_iota(jnp.int32, (cells_z, nz), 0)
        col = lax.broadcasted_iota(jnp.int32, (cells_z, nz), 1)
        wide = {}
        for k in range(8):
            e, q = k % 2, k % ratio
            if (e, q) not in wide:
                put = (row == 2 * col + e).astype(F32).astype(BF16)
                wide[e, q] = jnp.dot(put, d_ref[q], preferred_element_type=F32).astype(BF16)
        for a in range(2):
            for b in range(2):
                acc = None
                for e in range(2):
                    k = 4 * a + 2 * b + e
                    part = lax.dot_general(
                        wide[e, k % ratio], w_ref[k], (((1,), (1,)), ((), ())), preferred_element_type=F32
                    )
                    acc = part if acc is None else acc + part
                o_ref[a, b] = acc.astype(BF16)

    return pl.pallas_call(
        body,
        grid=(nx * ny,),
        in_specs=[pl.BlockSpec((ratio, nz, out_chan), lambda n: (0, n, 0)), whole(weights)],
        out_specs=pl.BlockSpec((2, 2, cells_z, in_chan), lambda n: (n // ny, n % ny, 0, 0)),
        out_shape=jax.ShapeDtypeStruct(shape, BF16),
        compiler_params=params(),
        cost_estimate=cost(32 * rows * in_chan * out_chan, 2 * rows * 8 * in_chan),
        name="volume_grad",
    )(deltas, weights)


def shards(spaces, chans, volume, weight, cotangent):
    kinds, block, width = weight.shape
    ratio = max(1, LANES // width)
    out_rows = volume.shape[0] * volume.shape[1] * volume.shape[2] // 8

    def pairs(count, step):
        return [(d, other(d, step)) for d in range(count)]

    packed = pack_weight(weight, ratio)
    line = [packed[0]] + [
        fetch(packed[i % ratio], "chan", pairs(chans, i)) for i in range(1, chans)
    ]
    cot_out = pack_cot(cotangent, chans, ratio)
    cots = [cot_out[0]] + [
        fetch(cot_out[i], "chan", pairs(chans, i)) for i in range(1, chans)
    ]
    pieces = [line] + [None] * (spaces - 1)
    for j in range(2, spaces, 2):
        pieces[j] = [fetch(p, "space", pairs(spaces, j)) for p in line]
    for j in range(0, spaces, 2):
        pieces[j + 1] = [fetch(p, "space", pairs(spaces, 1)) for p in pieces[j]]
    patches, turned = patch_rows(volume)
    deltas, weights = forward(patches, pieces, cots, spaces, chans, ratio)
    steps = list(range(0, spaces, 2))
    away = weight_part(turned, deltas, [s + 1 for s in steps], spaces, BF16)
    near = weight_part(turned, deltas, steps, spaces, F32)
    crossed = [fetch(p, "space", pairs(spaces, 1)) for p in away]
    sums = add_pairs(near, crossed, [F32] + [BF16] * (len(steps) - 1))
    came = [fetch(sums[n], "space", pairs(spaces, steps[n])) for n in range(1, len(steps))]
    parts = add_and_pack(sums[0], came, chans, ratio)
    got = [parts[0]] + [fetch(parts[i], "chan", pairs(chans, i)) for i in range(1, chans)]
    grad_weight = finish(got, kinds, width, 1.0 / out_rows)
    grad_volume = volume_grad(deltas, weights, volume.shape)
    return (grad_volume, grad_weight)


def solution(mesh):
    return jax.shard_map(
        functools.partial(shards, mesh.shape["space"], mesh.shape["chan"]),
        mesh=mesh,
        in_specs=(
            P(("groups", "space"), "chan", None, None),
            P(None, "space", "chan"),
            P(("groups", "space"), None, None, "chan"),
        ),
        out_specs=(P(("groups", "space"), "chan", None, None), P("groups", "space", "chan")),
        check_vma=False,
    )
```

time: 126 us -> 51.9 us (0.41)
  waiting for transfers between devices: 66.5 us -> 15.9 us
  blocking collectives: 17.4 us -> 0 us
  starting transfers between devices: 5.46 us -> 21.7 us
  local copies, waits for them, and re-layouts: 17.9 us -> 2.12 us
  between operations: 13.9 us -> 0.77 us
  Pallas kernels: 0 us -> 11.1 us
  matrix products: 4.92 us -> 0 us
    reduce_scatter x1 -> x0, waiting for transfers between devices: 44 us -> none  [shards(): lax.psum_scatter(partial_w, 'chan', scatter_dimension=2, tiled=True)]
    ppermute x0 -> x24, starting transfers between devices: none -> 21.7 us  [fetch(): return lax.ppermute(x, axis, pairs)]
    all_gather x1 -> x0, blocking collectives: 17.4 us -> none  [shards(): wide_w = lax.all_gather(weight, 'chan', axis=2, tiled=True)]
    unnamed x4 -> x0, waiting for transfers between devices: 16.1 us -> none
    ppermute x0 -> x24, waiting for transfers between devices: none -> 15.9 us  [fetch(): return lax.ppermute(x, axis, pairs)]
    pallas_call x0 -> x10, Pallas kernels: none -> 11.1 us  [the longest x1 3.73 us: patch_rows(): pl.pallas_call(body, grid=(nx * ny,), in_specs=[pl.BlockSpec((2, 2, cells...]
    all_to_all x1 -> x0, starting transfers between devices: 5.38 us -> none  [shards(): lax.all_to_all(cotangent, 'chan', split_axis=1, concat_axis=3, tiled=True)]
    dot_general x3 -> x0, matrix products: 4.92 us -> none  [the longest x1 2.13 us: shards(): jnp.einsum('mkc,kco->mo', patches, whole_w, preferred_element_type=jnp.fl...]
  transfers between devices with their start and end apart: 4 -> 24, of which waited for: 4 -> 8; matrix products, arithmetic and copies ran while one was open for 9% -> 2% of each run, Pallas kernels for 0% -> 16%
where the time goes in v1:
time: 51.9 us; the launch traced here: 51.7 us
  starting transfers between devices  21.7 us (42%)
  waiting for transfers between devices  15.9 us (31%)
  Pallas kernels  11.1 us (21%)
  local copies, waits for them, and re-layouts  2.12 us (4%)
  between operations  0.77 us (1%)
    ppermute x24, starting transfers between devices, fetch(): return lax.ppermute(x, axis, pairs)  21.7 us
    ppermute x24, waiting for transfers between devices, fetch(): return lax.ppermute(x, axis, pairs)  15.9 us
    pallas_call x1, Pallas kernels, patch_rows(): pl.pallas_call(body, grid=(nx * ny,), in_specs=[pl.BlockSpec((2, 2, cells...  3.73 us
    pallas_call x1, Pallas kernels, volume_grad(): pl.pallas_call(body, grid=(nx * ny,), in_specs=[pl.BlockSpec((ratio, nz,...  3.34 us
    unnamed x3, local copies, waits for them, and re-layouts  2.12 us
    pallas_call x2, Pallas kernels, weight_part(): pl.pallas_call(body, out_shape=[jax.ShapeDtypeStruct((kinds, block, out_c...  1.68 us
    pallas_call x1, Pallas kernels, forward(): pl.pallas_call(body, out_shape=[jax.ShapeDtypeStruct((ratio, rows, out_ch...  1.11 us
  transfers between devices with their start and end apart: 24, of which 8 were waited for; matrix products, arithmetic and copies ran while one was open for 2% of the time, Pallas kernels for 16%

profile of v1, /device:TPU:0, one launch (start us, length us, event | category | flops | bytes accessed | tf_op | source)
XLA Modules:
  0.0 51.7 jit_solution(15481449510577113325)
XLA Ops:
  0.6 0.0 copy-start
  0.6 0.9 %copy-done = bf16[8,64,64]{2,1,0:T(8,128)(2,1)S(1)} copy-done((bf16[8,64,64]{2,1,0:T(8,128)(2,1)S(1)}, bf16[8,64,64]{2,1,0:T(8,128)(2,1)}, u32[]{:S(2)}) %copy-start) | copy-done | bytes 65560
  1.5 0.1 pack_weight.1
  1.6 5.1 %collective-permute-start.2 = (bf16[4,64,128]{2,1,0:T(8,128)(2,1)S(1)}, bf16[4,64,128]{2,1,0:T(8,128)(2,1)S(1)}, u32[]{:S(2)}, u32[]{:S(2)}) collective-permute-start(bf16[4,64,128]{2,1,0:T(8,128)(2,1)S(1)} %get-tuple-element.24), channel_id=1, source_target_pairs={{0,3},{1,2},{2,1},{3,0},{4,7},{5,6},{6,5},{7,4},{8,11},{9,10},{10,... | collective-permute-start | bytes 196616 | tf_op jit(solution)/shard_map/ppermute | solution.py:20
  6.8 0.0 collective-permute-start
  6.8 1.5 %collective-permute-start.7 = (bf16[4,64,128]{2,1,0:T(8,128)(2,1)S(1)}, bf16[4,64,128]{2,1,0:T(8,128)(2,1)S(1)}, u32[]{:S(2)}, u32[]{:S(2)}) collective-permute-start(bf16[4,64,128]{2,1,0:T(8,128)(2,1)S(1)} %get-tuple-element.23.refs_0_), channel_id=1, source_target_pairs={{0,8},{4,12},{8,0},{12,4},{1,9},{5,13},{9,1},{13,5},{2,10},{6,14},... | collective-permute-start | bytes 196616 | tf_op jit(solution)/shard_map/ppermute | solution.py:20
  8.3 0.0 collective-permute-start.3
  8.3 0.8 %collective-permute-start.1 = (bf16[4,64,128]{2,1,0:T(8,128)(2,1)S(1)}, bf16[4,64,128]{2,1,0:T(8,128)(2,1)S(1)}, u32[]{:S(2)}, u32[]{:S(2)}) collective-permute-start(bf16[4,64,128]{2,1,0:T(8,128)(2,1)S(1)} %get-tuple-element.23.refs_0_), channel_id=1, source_target_pairs={{0,2},{1,3},{2,0},{3,1},{4,6},{5,7},{6,4},{7,5},{8,10},{9,11},{10,... | collective-permute-start | bytes 196616 | tf_op jit(solution)/shard_map/ppermute | solution.py:20
  9.0 1.2 %copy.5.c_ref = bf16[2,8,128,64]{3,2,1,0:T(8,128)(2,1)S(1)} copy(bf16[2,8,128,64]{2,3,1,0:T(8,128)(2,1)} %param.5) | data formatting | bytes 524288 | tf_op args[2]
  10.3 0.1 pack_cot.1
  10.4 0.0 collective-permute-done.2.refs_3_
  10.4 1.3 %collective-permute-start.15 = (bf16[256,128]{1,0:T(8,128)(2,1)S(1)}, bf16[256,128]{1,0:T(8,128)(2,1)S(1)}, u32[]{:S(2)}, u32[]{:S(2)}) collective-permute-start(bf16[256,128]{1,0:T(8,128)(2,1)S(1)} %get-tuple-element.26), channel_id=1, source_target_pairs={{0,1},{1,0},{2,3},{3,2},{4,5},{5,4},{6,7},{7,6},{8,9},{9,8},{10,11... | collective-permute-start | bytes 196616 | tf_op jit(solution)/shard_map/ppermute | solution.py:20
  11.7 0.0 collective-permute-done.refs_1_
  11.7 2.9 %collective-permute-start.16 = (bf16[256,128]{1,0:T(8,128)(2,1)S(1)}, bf16[256,128]{1,0:T(8,128)(2,1)S(1)}, u32[]{:S(2)}, u32[]{:S(2)}) collective-permute-start(bf16[256,128]{1,0:T(8,128)(2,1)S(1)} %get-tuple-element.27), channel_id=1, source_target_pairs={{0,2},{1,3},{2,0},{3,1},{4,6},{5,7},{6,4},{7,5},{8,10},{9,11},{10,... | collective-permute-start | bytes 196616 | tf_op jit(solution)/shard_map/ppermute | solution.py:20
  14.7 0.0 collective-permute-done.7.refs_8_
  14.7 0.2 collective-permute-start.17
  14.9 0.0 collective-permute-done.3.refs_4_
  14.9 1.7 %collective-permute-start.10 = (bf16[4,64,128]{2,1,0:T(8,128)(2,1)S(1)}, bf16[4,64,128]{2,1,0:T(8,128)(2,1)S(1)}, u32[]{:S(2)}, u32[]{:S(2)}) collective-permute-start(bf16[4,64,128]{2,1,0:T(8,128)(2,1)S(1)} %collective-permute-done.2.refs_3_), channel_id=1, source_target_pairs={{0,8},{4,12},{8,0},{12,4},{1,9},{5,13},{9,1},{13,5},{2,10},{6,14},... | collective-permute-start | bytes 196616 | tf_op jit(solution)/shard_map/ppermute | solution.py:20
  16.6 0.0 collective-permute-done.1.refs_2_
  16.6 0.0 collective-permute-start.6
  16.6 0.0 collective-permute-done.15.refs_17_
  16.6 0.4 collective-permute-start.8
  17.0 1.8 %collective-permute-done.16.refs_18_ = bf16[256,128]{1,0:T(8,128)(2,1)S(1)} collective-permute-done((bf16[256,128]{1,0:T(8,128)(2,1)S(1)}, bf16[256,128]{1,0:T(8,128)(2,1)S(1)}, u32[]{:S(2)}, u32[]{:S(2)}) %collective-permute-start.16) | collective-permute-done | bytes 65568 | tf_op jit(solution)/shard_map/ppermute | solution.py:20
  18.8 0.0 collective-permute-start.4
  18.8 2.1 %collective-permute-done.17.refs_19_ = bf16[256,128]{1,0:T(8,128)(2,1)S(1)} collective-permute-done((bf16[256,128]{1,0:T(8,128)(2,1)S(1)}, bf16[256,128]{1,0:T(8,128)(2,1)S(1)}, u32[]{:S(2)}, u32[]{:S(2)}) %collective-permute-start.17) | collective-permute-done | bytes 65568 | tf_op jit(solution)/shard_map/ppermute | solution.py:20
  20.8 0.8 %collective-permute-start.9 = (bf16[4,64,128]{2,1,0:T(8,128)(2,1)S(1)}, bf16[4,64,128]{2,1,0:T(8,128)(2,1)S(1)}, u32[]{:S(2)}, u32[]{:S(2)}) collective-permute-start(bf16[4,64,128]{2,1,0:T(8,128)(2,1)S(1)} %collective-permute-done.1.refs_2_), channel_id=1, source_target_pairs={{0,8},{4,12},{8,0},{12,4},{1,9},{5,13},{9,1},{13,5},{2,10},{6,14},... | collective-permute-start | bytes 196616 | tf_op jit(solution)/shard_map/ppermute | solution.py:20
  21.6 0.0 collective-permute-done.10.refs_11_
  21.6 0.0 collective-permute-start.5
  21.6 0.0 collective-permute-done.6.refs_7_
  21.6 0.5 collective-permute-start.11
  22.2 0.0 collective-permute-done.8.refs_9_
  22.2 0.1 collective-permute-start.14
  22.2 0.0 collective-permute-done.4.refs_5_
  22.2 0.4 collective-permute-start.12
  22.7 2.4 %collective-permute-done.9.refs_10_ = bf16[4,64,128]{2,1,0:T(8,128)(2,1)S(1)} collective-permute-done((bf16[4,64,128]{2,1,0:T(8,128)(2,1)S(1)}, bf16[4,64,128]{2,1,0:T(8,128)(2,1)S(1)}, u32[]{:S(2)}, u32[]{:S(2)}) %collective-permute-start.9) | collective-permute-done | bytes 65568 | tf_op jit(solution)/shard_map/ppermute | solution.py:20
  25.1 0.0 collective-permute-start.13
  25.1 3.7 %patch_rows.1 = (bf16[8,512,256]{2,1,0:T(8,128)(2,1)S(1)}, bf16[8,256,512]{2,1,0:T(8,128)(2,1)S(1)}) custom-call(bf16[4,4,256,256]{3,2,1,0:T(8,128)(2,1)} %v_ref.1), custom_call_target="tpu_custom_call" | custom-call | flops 536870912 | bytes 6291456 | tf_op jit(solution)/shard_map/patch_rows/pallas_call | solution.py:147
  28.9 0.0 collective-permute-done.11.refs_12_
  28.9 0.0 collective-permute-done.5.refs_6_
  28.9 0.0 collective-permute-done.14.refs_15_
  28.9 0.0 collective-permute-done.12.refs_13_
  28.9 0.0 collective-permute-done.13.refs_14_
  28.9 1.1 %forward.1 = (bf16[2,512,256]{2,1,0:T(8,128)(2,1)S(1)}, bf16[8,256,256]{2,1,0:T(8,128)(2,1)S(1)}) custom-call(bf16[8,512,256]{2,1,0:T(8,128)(2,1)S(1)} %get-tuple-element.22.p_ref, bf16[4,64,128]{2,1,0:T(8,128)(2,1)S(1)} %get-tuple-element.23.refs_0_, bf16[4,64,128]{2,1,0:T(8,128)(2,1)S(1)} %collective-permute-done.refs_1_, ...), custom_call_target="tpu_custom_call" | custom-call | flops 536870912 | bytes 2097152 | tf_op jit(solution)/shard_map/forward/pallas_call | solution.py:207
  30.0 0.8 %weight_part.3 = (bf16[8,64,256]{2,1,0:T(8,128)(2,1)S(1)}, bf16[8,64,256]{2,1,0:T(8,128)(2,1)S(1)}) custom-call(bf16[8,256,512]{2,1,0:T(8,128)(2,1)S(1)} %get-tuple-element.31.t_ref, bf16[2,512,256]{2,1,0:T(8,128)(2,1)S(1)} %get-tuple-element.29.d_ref), custom_call_target="tpu_custom_call" | custom-call | flops 268435456 | bytes 2097152 | tf_op jit(solution)/shard_map/weight_part/pallas_call | solution.py:232
  30.9 0.6 %collective-permute-start.18 = (bf16[8,64,256]{2,1,0:T(8,128)(2,1)S(1)}, bf16[8,64,256]{2,1,0:T(8,128)(2,1)S(1)}, u32[]{:S(2)}, u32[]{:S(2)}) collective-permute-start(bf16[8,64,256]{2,1,0:T(8,128)(2,1)S(1)} %get-tuple-element.34), channel_id=1, source_target_pairs={{0,4},{4,0},{8,12},{12,8},{1,5},{5,1},{9,13},{13,9},{2,6},{6,2},{1... | collective-permute-start | bytes 786440 | tf_op jit(solution)/shard_map/ppermute | solution.py:20
  31.4 0.1 collective-permute-start.19
  31.5 0.8 %weight_part.2 = (f32[8,64,256]{2,1,0:T(8,128)S(1)}, f32[8,64,256]{2,1,0:T(8,128)S(1)}) custom-call(bf16[8,256,512]{2,1,0:T(8,128)(2,1)S(1)} %get-tuple-element.31.t_ref, bf16[2,512,256]{2,1,0:T(8,128)(2,1)S(1)} %get-tuple-element.29.d_ref), custom_call_target="tpu_custom_call" | custom-call | flops 268435456 | bytes 2097152 | tf_op jit(solution)/shard_map/weight_part/pallas_call | solution.py:232
  32.4 0.2 collective-permute-done.18.refs_2_
  32.6 0.4 collective-permute-done.19.refs_3_
  33.0 0.1 add_pairs.1
  33.1 0.9 %collective-permute-start.20 = (bf16[8,64,256]{2,1,0:T(8,128)(2,1)S(1)}, bf16[8,64,256]{2,1,0:T(8,128)(2,1)S(1)}, u32[]{:S(2)}, u32[]{:S(2)}) collective-permute-start(bf16[8,64,256]{2,1,0:T(8,128)(2,1)S(1)} %get-tuple-element.37), channel_id=1, source_target_pairs={{0,8},{4,12},{8,0},{12,4},{1,9},{5,13},{9,1},{13,5},{2,10},{6,14},... | collective-permute-start | bytes 786440 | tf_op jit(solution)/shard_map/ppermute | solution.py:20
  33.9 7.8 %collective-permute-done.20.refs_1_ = bf16[8,64,256]{2,1,0:T(8,128)(2,1)S(1)} collective-permute-done((bf16[8,64,256]{2,1,0:T(8,128)(2,1)S(1)}, bf16[8,64,256]{2,1,0:T(8,128)(2,1)S(1)}, u32[]{:S(2)}, u32[]{:S(2)}) %collective-permute-start.20) | collective-permute-done | bytes 262176 | tf_op jit(solution)/shard_map/ppermute | solution.py:20
  41.7 0.1 add_and_pack.1
  41.9 0.9 %collective-permute-start.21 = (bf16[4,64,128]{2,1,0:T(8,128)(2,1)S(1)}, bf16[4,64,128]{2,1,0:T(8,128)(2,1)S(1)}, u32[]{:S(2)}, u32[]{:S(2)}) collective-permute-start(bf16[4,64,128]{2,1,0:T(8,128)(2,1)S(1)} %get-tuple-element.39), channel_id=1, source_target_pairs={{0,1},{1,0},{2,3},{3,2},{4,5},{5,4},{6,7},{7,6},{8,9},{9,8},{10,11... | collective-permute-start | bytes 196616 | tf_op jit(solution)/shard_map/ppermute | solution.py:20
  42.8 2.0 %collective-permute-start.22 = (bf16[4,64,128]{2,1,0:T(8,128)(2,1)S(1)}, bf16[4,64,128]{2,1,0:T(8,128)(2,1)S(1)}, u32[]{:S(2)}, u32[]{:S(2)}) collective-permute-start(bf16[4,64,128]{2,1,0:T(8,128)(2,1)S(1)} %get-tuple-element.40), channel_id=1, source_target_pairs={{0,2},{1,3},{2,0},{3,1},{4,6},{5,7},{6,4},{7,5},{8,10},{9,11},{10,... | collective-permute-start | bytes 196616 | tf_op jit(solution)/shard_map/ppermute | solution.py:20
  44.7 1.6 %collective-permute-start.23 = (bf16[4,64,128]{2,1,0:T(8,128)(2,1)S(1)}, bf16[4,64,128]{2,1,0:T(8,128)(2,1)S(1)}, u32[]{:S(2)}, u32[]{:S(2)}) collective-permute-start(bf16[4,64,128]{2,1,0:T(8,128)(2,1)S(1)} %get-tuple-element.41), channel_id=1, source_target_pairs={{0,3},{1,2},{2,1},{3,0},{4,7},{5,6},{6,5},{7,4},{8,11},{9,10},{10,... | collective-permute-start | bytes 196616 | tf_op jit(solution)/shard_map/ppermute | solution.py:20
  46.3 3.3 %volume_grad.1 = bf16[4,4,256,256]{3,2,1,0:T(8,128)(2,1)} custom-call(bf16[2,512,256]{2,1,0:T(8,128)(2,1)S(1)} %get-tuple-element.29.d_ref, bf16[8,256,256]{2,1,0:T(8,128)(2,1)S(1)} %get-tuple-element.30.w_ref), custom_call_target="tpu_custom_call" | custom-call | flops 1073741824 | bytes 2097152 | tf_op jit(solution)/shard_map/volume_grad/pallas_call | solution.py:333
  49.6 0.0 collective-permute-done.21.refs_1_
  49.7 0.1 collective-permute-done.22.refs_2_
  49.7 1.1 %collective-permute-done.23.refs_3_ = bf16[4,64,128]{2,1,0:T(8,128)(2,1)S(1)} collective-permute-done((bf16[4,64,128]{2,1,0:T(8,128)(2,1)S(1)}, bf16[4,64,128]{2,1,0:T(8,128)(2,1)S(1)}, u32[]{:S(2)}, u32[]{:S(2)}) %collective-permute-start.23) | collective-permute-done | bytes 65568 | tf_op jit(solution)/shard_map/ppermute | solution.py:20
  50.9 0.8 %finish.1 = f32[8,64,64]{2,1,0:T(8,128)} custom-call(f32[4,64,128]{2,1,0:T(8,128)S(1)} %get-tuple-element.38.refs_0_, bf16[4,64,128]{2,1,0:T(8,128)(2,1)S(1)} %collective-permute-done.21.refs_1_, bf16[4,64,128]{2,1,0:T(8,128)(2,1)S(1)} %collective-permute-done.22.refs_2_, bf16[4,64,128]{2,1,0:T(8,128)(2,1)S(1)} %collective-permute-done.23.refs_3_), custom_call_target="tpu_custom_call" | custom-call | tf_op jit(solution)/shard_map/finish/pallas_call | solution.py:300
Async XLA Ops:
  0.6 0.9 %copy-start = (bf16[8,64,64]{2,1,0:T(8,128)(2,1)S(1)}, bf16[8,64,64]{2,1,0:T(8,128)(2,1)}, u32[]{:S(2)}) copy-start(bf16[8,64,64]{2,1,0:T(8,128)(2,1)} %w_ref.1) | copy-start | bytes 196612
  1.6 8.8 %collective-permute-start.2 = (bf16[4,64,128]{2,1,0:T(8,128)(2,1)S(1)}, bf16[4,64,128]{2,1,0:T(8,128)(2,1)S(1)}, u32[]{:S(2)}, u32[]{:S(2)}) collective-permute-start(bf16[4,64,128]{2,1,0:T(8,128)(2,1)S(1)} %get-tuple-element.24), channel_id=1, source_target_pairs={{0,3},{1,2},{2,1},{3,0},{4,7},{5,6},{6,5},{7,4},{8,11},{9,10},{10,... | collective-permute-start | bytes 196616 | tf_op jit(solution)/shard_map/ppermute | solution.py:20
  6.8 5.0 %collective-permute-start = (bf16[4,64,128]{2,1,0:T(8,128)(2,1)S(1)}, bf16[4,64,128]{2,1,0:T(8,128)(2,1)S(1)}, u32[]{:S(2)}, u32[]{:S(2)}) collective-permute-start(bf16[4,64,128]{2,1,0:T(8,128)(2,1)S(1)} %get-tuple-element.24), channel_id=1, source_target_pairs={{0,1},{1,0},{2,3},{3,2},{4,5},{5,4},{6,7},{7,6},{8,9},{9,8},{10,11... | collective-permute-start | bytes 196616 | tf_op jit(solution)/shard_map/ppermute | solution.py:20
  6.8 7.9 %collective-permute-start.7 = (bf16[4,64,128]{2,1,0:T(8,128)(2,1)S(1)}, bf16[4,64,128]{2,1,0:T(8,128)(2,1)S(1)}, u32[]{:S(2)}, u32[]{:S(2)}) collective-permute-start(bf16[4,64,128]{2,1,0:T(8,128)(2,1)S(1)} %get-tuple-element.23.refs_0_), channel_id=1, source_target_pairs={{0,8},{4,12},{8,0},{12,4},{1,9},{5,13},{9,1},{13,5},{2,10},{6,14},... | collective-permute-start | bytes 196616 | tf_op jit(solution)/shard_map/ppermute | solution.py:20
  8.3 6.6 %collective-permute-start.3 = (bf16[4,64,128]{2,1,0:T(8,128)(2,1)S(1)}, bf16[4,64,128]{2,1,0:T(8,128)(2,1)S(1)}, u32[]{:S(2)}, u32[]{:S(2)}) collective-permute-start(bf16[4,64,128]{2,1,0:T(8,128)(2,1)S(1)} %get-tuple-element.23.refs_0_), channel_id=1, source_target_pairs={{0,4},{4,0},{8,12},{12,8},{1,5},{5,1},{9,13},{13,9},{2,6},{6,2},{1... | collective-permute-start | bytes 196616 | tf_op jit(solution)/shard_map/ppermute | solution.py:20
  8.3 8.3 %collective-permute-start.1 = (bf16[4,64,128]{2,1,0:T(8,128)(2,1)S(1)}, bf16[4,64,128]{2,1,0:T(8,128)(2,1)S(1)}, u32[]{:S(2)}, u32[]{:S(2)}) collective-permute-start(bf16[4,64,128]{2,1,0:T(8,128)(2,1)S(1)} %get-tuple-element.23.refs_0_), channel_id=1, source_target_pairs={{0,2},{1,3},{2,0},{3,1},{4,6},{5,7},{6,4},{7,5},{8,10},{9,11},{10,... | collective-permute-start | bytes 196616 | tf_op jit(solution)/shard_map/ppermute | solution.py:20
  10.4 6.1 %collective-permute-start.15 = (bf16[256,128]{1,0:T(8,128)(2,1)S(1)}, bf16[256,128]{1,0:T(8,128)(2,1)S(1)}, u32[]{:S(2)}, u32[]{:S(2)}) collective-permute-start(bf16[256,128]{1,0:T(8,128)(2,1)S(1)} %get-tuple-element.26), channel_id=1, source_target_pairs={{0,1},{1,0},{2,3},{3,2},{4,5},{5,4},{6,7},{7,6},{8,9},{9,8},{10,11... | collective-permute-start | bytes 196616 | tf_op jit(solution)/shard_map/ppermute | solution.py:20
  11.7 7.0 %collective-permute-start.16 = (bf16[256,128]{1,0:T(8,128)(2,1)S(1)}, bf16[256,128]{1,0:T(8,128)(2,1)S(1)}, u32[]{:S(2)}, u32[]{:S(2)}) collective-permute-start(bf16[256,128]{1,0:T(8,128)(2,1)S(1)} %get-tuple-element.27), channel_id=1, source_target_pairs={{0,2},{1,3},{2,0},{3,1},{4,6},{5,7},{6,4},{7,5},{8,10},{9,11},{10,... | collective-permute-start | bytes 196616 | tf_op jit(solution)/shard_map/ppermute | solution.py:20
  14.7 6.2 %collective-permute-start.17 = (bf16[256,128]{1,0:T(8,128)(2,1)S(1)}, bf16[256,128]{1,0:T(8,128)(2,1)S(1)}, u32[]{:S(2)}, u32[]{:S(2)}) collective-permute-start(bf16[256,128]{1,0:T(8,128)(2,1)S(1)} %get-tuple-element.28), channel_id=1, source_target_pairs={{0,3},{1,2},{2,1},{3,0},{4,7},{5,6},{6,5},{7,4},{8,11},{9,10},{10,... | collective-permute-start | bytes 196616 | tf_op jit(solution)/shard_map/ppermute | solution.py:20
  14.9 6.7 %collective-permute-start.10 = (bf16[4,64,128]{2,1,0:T(8,128)(2,1)S(1)}, bf16[4,64,128]{2,1,0:T(8,128)(2,1)S(1)}, u32[]{:S(2)}, u32[]{:S(2)}) collective-permute-start(bf16[4,64,128]{2,1,0:T(8,128)(2,1)S(1)} %collective-permute-done.2.refs_3_), channel_id=1, source_target_pairs={{0,8},{4,12},{8,0},{12,4},{1,9},{5,13},{9,1},{13,5},{2,10},{6,14},... | collective-permute-start | bytes 196616 | tf_op jit(solution)/shard_map/ppermute | solution.py:20
  16.6 5.1 %collective-permute-start.6 = (bf16[4,64,128]{2,1,0:T(8,128)(2,1)S(1)}, bf16[4,64,128]{2,1,0:T(8,128)(2,1)S(1)}, u32[]{:S(2)}, u32[]{:S(2)}) collective-permute-start(bf16[4,64,128]{2,1,0:T(8,128)(2,1)S(1)} %collective-permute-done.2.refs_3_), channel_id=1, source_target_pairs={{0,4},{4,0},{8,12},{12,8},{1,5},{5,1},{9,13},{13,9},{2,6},{6,2},{1... | collective-permute-start | bytes 196616 | tf_op jit(solution)/shard_map/ppermute | solution.py:20
  16.6 5.6 %collective-permute-start.8 = (bf16[4,64,128]{2,1,0:T(8,128)(2,1)S(1)}, bf16[4,64,128]{2,1,0:T(8,128)(2,1)S(1)}, u32[]{:S(2)}, u32[]{:S(2)}) collective-permute-start(bf16[4,64,128]{2,1,0:T(8,128)(2,1)S(1)} %collective-permute-done.refs_1_), channel_id=1, source_target_pairs={{0,8},{4,12},{8,0},{12,4},{1,9},{5,13},{9,1},{13,5},{2,10},{6,14},... | collective-permute-start | bytes 196616 | tf_op jit(solution)/shard_map/ppermute | solution.py:20
  18.8 3.5 %collective-permute-start.4 = (bf16[4,64,128]{2,1,0:T(8,128)(2,1)S(1)}, bf16[4,64,128]{2,1,0:T(8,128)(2,1)S(1)}, u32[]{:S(2)}, u32[]{:S(2)}) collective-permute-start(bf16[4,64,128]{2,1,0:T(8,128)(2,1)S(1)} %collective-permute-done.refs_1_), channel_id=1, source_target_pairs={{0,4},{4,0},{8,12},{12,8},{1,5},{5,1},{9,13},{13,9},{2,6},{6,2},{1... | collective-permute-start | bytes 196616 | tf_op jit(solution)/shard_map/ppermute | solution.py:20
  20.8 4.3 %collective-permute-start.9 = (bf16[4,64,128]{2,1,0:T(8,128)(2,1)S(1)}, bf16[4,64,128]{2,1,0:T(8,128)(2,1)S(1)}, u32[]{:S(2)}, u32[]{:S(2)}) collective-permute-start(bf16[4,64,128]{2,1,0:T(8,128)(2,1)S(1)} %collective-permute-done.1.refs_2_), channel_id=1, source_target_pairs={{0,8},{4,12},{8,0},{12,4},{1,9},{5,13},{9,1},{13,5},{2,10},{6,14},... | collective-permute-start | bytes 196616 | tf_op jit(solution)/shard_map/ppermute | solution.py:20
  21.6 7.2 %collective-permute-start.5 = (bf16[4,64,128]{2,1,0:T(8,128)(2,1)S(1)}, bf16[4,64,128]{2,1,0:T(8,128)(2,1)S(1)}, u32[]{:S(2)}, u32[]{:S(2)}) collective-permute-start(bf16[4,64,128]{2,1,0:T(8,128)(2,1)S(1)} %collective-permute-done.1.refs_2_), channel_id=1, source_target_pairs={{0,4},{4,0},{8,12},{12,8},{1,5},{5,1},{9,13},{13,9},{2,6},{6,2},{1... | collective-permute-start | bytes 196616 | tf_op jit(solution)/shard_map/ppermute | solution.py:20
  21.6 7.2 %collective-permute-start.11 = (bf16[4,64,128]{2,1,0:T(8,128)(2,1)S(1)}, bf16[4,64,128]{2,1,0:T(8,128)(2,1)S(1)}, u32[]{:S(2)}, u32[]{:S(2)}) collective-permute-start(bf16[4,64,128]{2,1,0:T(8,128)(2,1)S(1)} %collective-permute-done.7.refs_8_), channel_id=1, source_target_pairs={{0,4},{4,0},{8,12},{12,8},{1,5},{5,1},{9,13},{13,9},{2,6},{6,2},{1... | collective-permute-start | bytes 196616 | tf_op jit(solution)/shard_map/ppermute | solution.py:20
  22.2 6.7 %collective-permute-start.14 = (bf16[4,64,128]{2,1,0:T(8,128)(2,1)S(1)}, bf16[4,64,128]{2,1,0:T(8,128)(2,1)S(1)}, u32[]{:S(2)}, u32[]{:S(2)}) collective-permute-start(bf16[4,64,128]{2,1,0:T(8,128)(2,1)S(1)} %collective-permute-done.10.refs_11_), channel_id=1, source_target_pairs={{0,4},{4,0},{8,12},{12,8},{1,5},{5,1},{9,13},{13,9},{2,6},{6,2},{1... | collective-permute-start | bytes 196616 | tf_op jit(solution)/shard_map/ppermute | solution.py:20
  22.2 6.7 %collective-permute-start.12 = (bf16[4,64,128]{2,1,0:T(8,128)(2,1)S(1)}, bf16[4,64,128]{2,1,0:T(8,128)(2,1)S(1)}, u32[]{:S(2)}, u32[]{:S(2)}) collective-permute-start(bf16[4,64,128]{2,1,0:T(8,128)(2,1)S(1)} %collective-permute-done.8.refs_9_), channel_id=1, source_target_pairs={{0,4},{4,0},{8,12},{12,8},{1,5},{5,1},{9,13},{13,9},{2,6},{6,2},{1... | collective-permute-start | bytes 196616 | tf_op jit(solution)/shard_map/ppermute | solution.py:20
  25.1 3.8 %collective-permute-start.13 = (bf16[4,64,128]{2,1,0:T(8,128)(2,1)S(1)}, bf16[4,64,128]{2,1,0:T(8,128)(2,1)S(1)}, u32[]{:S(2)}, u32[]{:S(2)}) collective-permute-start(bf16[4,64,128]{2,1,0:T(8,128)(2,1)S(1)} %collective-permute-done.9.refs_10_), channel_id=1, source_target_pairs={{0,4},{4,0},{8,12},{12,8},{1,5},{5,1},{9,13},{13,9},{2,6},{6,2},{1... | collective-permute-start | bytes 196616 | tf_op jit(solution)/shard_map/ppermute | solution.py:20
  30.9 1.7 %collective-permute-start.18 = (bf16[8,64,256]{2,1,0:T(8,128)(2,1)S(1)}, bf16[8,64,256]{2,1,0:T(8,128)(2,1)S(1)}, u32[]{:S(2)}, u32[]{:S(2)}) collective-permute-start(bf16[8,64,256]{2,1,0:T(8,128)(2,1)S(1)} %get-tuple-element.34), channel_id=1, source_target_pairs={{0,4},{4,0},{8,12},{12,8},{1,5},{5,1},{9,13},{13,9},{2,6},{6,2},{1... | collective-permute-start | bytes 786440 | tf_op jit(solution)/shard_map/ppermute | solution.py:20
  31.4 1.5 %collective-permute-start.19 = (bf16[8,64,256]{2,1,0:T(8,128)(2,1)S(1)}, bf16[8,64,256]{2,1,0:T(8,128)(2,1)S(1)}, u32[]{:S(2)}, u32[]{:S(2)}) collective-permute-start(bf16[8,64,256]{2,1,0:T(8,128)(2,1)S(1)} %get-tuple-element.35), channel_id=1, source_target_pairs={{0,4},{4,0},{8,12},{12,8},{1,5},{5,1},{9,13},{13,9},{2,6},{6,2},{1... | collective-permute-start | bytes 786440 | tf_op jit(solution)/shard_map/ppermute | solution.py:20
  33.1 8.7 %collective-permute-start.20 = (bf16[8,64,256]{2,1,0:T(8,128)(2,1)S(1)}, bf16[8,64,256]{2,1,0:T(8,128)(2,1)S(1)}, u32[]{:S(2)}, u32[]{:S(2)}) collective-permute-start(bf16[8,64,256]{2,1,0:T(8,128)(2,1)S(1)} %get-tuple-element.37), channel_id=1, source_target_pairs={{0,8},{4,12},{8,0},{12,4},{1,9},{5,13},{9,1},{13,5},{2,10},{6,14},... | collective-permute-start | bytes 786440 | tf_op jit(solution)/shard_map/ppermute | solution.py:20
  41.9 7.8 %collective-permute-start.21 = (bf16[4,64,128]{2,1,0:T(8,128)(2,1)S(1)}, bf16[4,64,128]{2,1,0:T(8,128)(2,1)S(1)}, u32[]{:S(2)}, u32[]{:S(2)}) collective-permute-start(bf16[4,64,128]{2,1,0:T(8,128)(2,1)S(1)} %get-tuple-element.39), channel_id=1, source_target_pairs={{0,1},{1,0},{2,3},{3,2},{4,5},{5,4},{6,7},{7,6},{8,9},{9,8},{10,11... | collective-permute-start | bytes 196616 | tf_op jit(solution)/shard_map/ppermute | solution.py:20
  42.8 7.0 %collective-permute-start.22 = (bf16[4,64,128]{2,1,0:T(8,128)(2,1)S(1)}, bf16[4,64,128]{2,1,0:T(8,128)(2,1)S(1)}, u32[]{:S(2)}, u32[]{:S(2)}) collective-permute-start(bf16[4,64,128]{2,1,0:T(8,128)(2,1)S(1)} %get-tuple-element.40), channel_id=1, source_target_pairs={{0,2},{1,3},{2,0},{3,1},{4,6},{5,7},{6,4},{7,5},{8,10},{9,11},{10,... | collective-permute-start | bytes 196616 | tf_op jit(solution)/shard_map/ppermute | solution.py:20
  44.7 6.2 %collective-permute-start.23 = (bf16[4,64,128]{2,1,0:T(8,128)(2,1)S(1)}, bf16[4,64,128]{2,1,0:T(8,128)(2,1)S(1)}, u32[]{:S(2)}, u32[]{:S(2)}) collective-permute-start(bf16[4,64,128]{2,1,0:T(8,128)(2,1)S(1)} %get-tuple-element.41), channel_id=1, source_target_pairs={{0,3},{1,2},{2,1},{3,0},{4,7},{5,6},{6,5},{7,4},{8,11},{9,10},{10,... | collective-permute-start | bytes 196616 | tf_op jit(solution)/shard_map/ppermute | solution.py:20

commit v2 on v1

v2 whole, which is shorter than its diff:
```python
import functools

import jax
import jax.numpy as jnp
from jax import lax
from jax.experimental import pallas as pl
from jax.experimental.pallas import tpu as pltpu
from jax.sharding import PartitionSpec as P

LANES = 128
TURN_FLOPS = 4 * 10**9
BF16 = jnp.bfloat16
F32 = jnp.float32


def other(me, step):
    return me ^ step


def fetch(x, axis, pairs):
    return lax.ppermute(x, axis, pairs)


def lane_group(shape, width):
    return lax.broadcasted_iota(jnp.int32, shape, len(shape) - 1) // width


def merge(parts, width, flip):
    group = lane_group(parts[0].shape, width)
    out = parts[flip]
    for g in range(1, len(parts)):
        out = jnp.where(group == g, parts[g ^ flip], out)
    return out


def swap_groups(x, width, flip):
    if flip == 0:
        return x
    tiles = []
    for t in range(x.shape[1] // LANES):
        tile = x[:, t * LANES:(t + 1) * LANES]
        bit = 1
        while bit <= flip:
            if flip & bit:
                shift = width * bit
                up = pltpu.roll(tile, LANES - shift, 1)
                if 2 * shift == LANES:
                    tile = up
                else:
                    even = (lane_group(tile.shape, shift) % 2) == 0
                    tile = jnp.where(even, up, pltpu.roll(tile, shift, 1))
            bit *= 2
        tiles.append(tile)
    return tiles[0] if len(tiles) == 1 else jnp.concatenate(tiles, axis=1)


def whole(x):
    return pl.BlockSpec(x.shape, lambda *_: (0,) * len(x.shape))


def params():
    return pltpu.CompilerParams(vmem_limit_bytes=48 * 1024 * 1024)


def cost(flops, bytes_accessed):
    return pl.CostEstimate(flops=flops, bytes_accessed=bytes_accessed, transcendentals=0)


def spread(x, width, at):
    if width >= LANES:
        return x
    zeros = jnp.zeros((x.shape[0], LANES - width), x.dtype)
    full = jnp.concatenate([x, zeros], axis=1)
    return pltpu.roll(full, at * width, 1) if at else full


def pack_weight(weight, ratio):
    kinds, rows, width = weight.shape
    groups = kinds // ratio
    lanes = ratio * width

    def body(w_ref, *outs):
        for g in range(groups):
            for flip in range(ratio):
                acc = None
                for lane in range(ratio):
                    part = spread(w_ref[g * ratio + (lane ^ flip)].astype(F32), width, lane)
                    acc = part if acc is None else acc + part
                outs[flip][g] = acc.astype(BF16)

    return pl.pallas_call(
        body,
        out_shape=[jax.ShapeDtypeStruct((groups, rows, lanes), BF16)] * ratio,
        compiler_params=params(),
        name="pack_weight",
    )(weight)


def pack_cot(cot, chans):
    planes, cells_y, width, cells_z = cot.shape
    own_y = cells_y // chans

    def body(c_ref, *outs):
        me = lax.axis_index("chan")
        for step in range(chans):
            target = other(me, step) * own_y
            for p in range(planes):
                for y in range(own_y):
                    outs[step][p * own_y + y] = c_ref[p, target + y]

    return pl.pallas_call(
        body,
        out_shape=[jax.ShapeDtypeStruct((planes * own_y, width, cells_z), BF16)] * chans,
        compiler_params=params(),
        name="pack_cot",
    )(cot)


def merge_tile(parts, width, after=()):
    groups, block, lanes = parts[0].shape
    ratio = len(parts)

    def body(*refs):
        out = refs[-1]
        for g in range(groups):
            got = [refs[u][g] for u in range(ratio)]
            for q in range(ratio):
                out[g * ratio + q] = merge(got, width, q)

    return pl.pallas_call(
        body,
        in_specs=[pl.BlockSpec(memory_space=pltpu.VMEM)] * ratio + [pl.BlockSpec(memory_space=pl.ANY)] * len(after),
        out_shape=jax.ShapeDtypeStruct((groups * ratio, block, lanes), BF16),
        compiler_params=params(),
        name="merge_tile",
    )(*parts, *after)


def gate(tile, after):
    def body(t_ref, *refs):
        refs[-1][...] = t_ref[...]

    return pl.pallas_call(
        body,
        in_specs=[pl.BlockSpec(memory_space=pltpu.VMEM)] + [pl.BlockSpec(memory_space=pl.ANY)] * len(after),
        out_shape=jax.ShapeDtypeStruct(tile.shape, tile.dtype),
        compiler_params=params(),
        name="gate",
    )(tile, *after)


def patch_rows(volume, after=()):
    cells_x, cells_y, cells_z, in_chan = volume.shape
    nx, ny, nz = cells_x // 2, cells_y // 2, cells_z // 2
    rows = nx * ny * nz

    def body(v_ref, *refs):
        p_ref, t_ref = refs[-2:]
        row = lax.broadcasted_iota(jnp.int32, (cells_z, cells_z), 0)
        col = lax.broadcasted_iota(jnp.int32, (cells_z, cells_z), 1)
        pick = (col == 2 * (row % nz) + row // nz).astype(F32).astype(BF16)
        for n in range(nx * ny):
            here = slice(n * nz, (n + 1) * nz)
            for a in range(2):
                for b in range(2):
                    k = 4 * a + 2 * b
                    got = jnp.dot(pick, v_ref[2 * (n // ny) + a, 2 * (n % ny) + b], preferred_element_type=F32)
                    got = got.astype(BF16)
                    for e in range(2):
                        part = got[e * nz:(e + 1) * nz]
                        p_ref[k + e, here] = part
                        t_ref[k + e, :, here] = part.T

    return pl.pallas_call(
        body,
        in_specs=[pl.BlockSpec(memory_space=pltpu.VMEM)] + [pl.BlockSpec(memory_space=pl.ANY)] * len(after),
        out_shape=[
            jax.ShapeDtypeStruct((8, rows, in_chan), BF16),
            jax.ShapeDtypeStruct((8, in_chan, rows), BF16),
        ],
        compiler_params=params(),
        cost_estimate=cost(16 * rows * in_chan * cells_z, 6 * volume.size),
        name="patch_rows",
    )(volume, *after)


def turn_cot(cots):
    tiles, width, cells = cots[0].shape
    out_chan = width * len(cots)

    def body(*refs):
        out = refs[-1]
        for n in range(tiles):
            column = jnp.concatenate([ref[n] for ref in refs[:-1]], axis=0)
            out[n * cells:(n + 1) * cells] = column.T

    return pl.pallas_call(
        body,
        out_shape=jax.ShapeDtypeStruct((tiles * cells, out_chan), BF16),
        compiler_params=params(),
        cost_estimate=cost(TURN_FLOPS, 4 * tiles * cells * out_chan),
        name="turn_cot",
    )(*cots)


def forward(patches, lines, upstream, width, ratio):
    kinds, rows, in_chan = patches.shape
    _, block, lanes = lines[0][0].shape
    spaces, lane_tiles = len(lines), len(lines[0])
    out_chan = lane_tiles * lanes
    flat = [tile for line in lines for tile in line]

    def body(p_ref, u_ref, *refs):
        ins = refs[:len(flat)]
        d_ref, w_ref = refs[-2:]
        me = lax.axis_index("space")
        for j in range(spaces):
            at = pl.multiple_of(other(me, j) * block, block)
            for t in range(lane_tiles):
                for k in range(kinds):
                    w_ref[k, pl.ds(at, block), t * lanes:(t + 1) * lanes] = ins[j * lane_tiles + t][k]
        part_rows = rows // 2
        for first in range(0, rows, part_rows):
            here = slice(first, first + part_rows)
            pre = None
            for q in range(ratio):
                acc = None
                for k in range(q, kinds, ratio):
                    part = jnp.dot(p_ref[k, here], w_ref[k], preferred_element_type=F32)
                    acc = part if acc is None else acc + part
                acc = swap_groups(acc, width, q)
                pre = acc if pre is None else pre + acc
            up = u_ref[here].astype(F32)
            squash = 1.0 / (1.0 + jnp.exp(-pre))
            slopes = squash * (1.0 + pre * (1.0 - squash))
            delta = (up * slopes).astype(BF16)
            d_ref[0, here] = delta
            for q in range(1, ratio):
                d_ref[q, here] = swap_groups(delta.astype(F32), width, q).astype(BF16)

    return pl.pallas_call(
        body,
        out_shape=[
            jax.ShapeDtypeStruct((ratio, rows, out_chan), BF16),
            jax.ShapeDtypeStruct((kinds, in_chan, out_chan), BF16),
        ],
        compiler_params=params(),
        cost_estimate=cost(2 * patches.size * out_chan, 2 * patches.size),
        name="forward",
    )(patches, upstream, *flat)


def weight_part(turned, deltas, steps, spaces, lanes, dtype):
    kinds, in_chan, rows = turned.shape
    ratio, _, out_chan = deltas.shape
    block = in_chan // spaces
    tiles = out_chan // lanes

    def body(t_ref, d_ref, *outs):
        me = lax.axis_index("space")
        ats = [pl.multiple_of(other(me, step) * block, block) for step in steps]
        for q in range(ratio):
            ks = range(q, kinds, ratio)
            for n, at in enumerate(ats):
                left = jnp.concatenate([t_ref[k, pl.ds(at, block)] for k in ks], axis=0)
                got = jnp.dot(left, d_ref[q], preferred_element_type=F32).astype(dtype)
                for i, k in enumerate(ks):
                    for t in range(tiles):
                        outs[t][n, k] = got[i * block:(i + 1) * block, t * lanes:(t + 1) * lanes]

    return pl.pallas_call(
        body,
        out_shape=[jax.ShapeDtypeStruct((len(steps), kinds, block, lanes), dtype)] * tiles,
        compiler_params=params(),
        cost_estimate=cost(2 * turned.size * out_chan * len(steps) // spaces, 2 * turned.size),
        name="weight_part",
    )(turned, deltas)


def add_core(mine, theirs):
    count, kinds, block, lanes = mine.shape

    def body(a_ref, b_ref, *outs):
        for n in range(count):
            outs[n][...] = (a_ref[n] + b_ref[n].astype(F32)).astype(outs[n].dtype)

    return pl.pallas_call(
        body,
        out_shape=[jax.ShapeDtypeStruct((kinds, block, lanes), BF16 if n else F32) for n in range(count)],
        compiler_params=params(),
        name="add_core",
    )(mine, theirs)


def add_and_pack(mine, theirs, width, own):
    kinds, block, lanes = mine.shape
    ratio = lanes // width
    groups = kinds // ratio

    def body(*refs):
        ins, outs = refs[:1 + len(theirs)], refs[1 + len(theirs):]
        for g in range(groups):
            sums = []
            for q in range(ratio):
                acc = ins[0][g * ratio + q]
                for ref in ins[1:]:
                    acc = acc + ref[g * ratio + q].astype(F32)
                sums.append(acc)
            for u in range(ratio):
                packed = swap_groups(merge(sums, width, u), width, u)
                outs[u][g] = packed.astype(outs[u].dtype)

    return pl.pallas_call(
        body,
        out_shape=[
            jax.ShapeDtypeStruct((groups, block, lanes), F32 if own and u == 0 else BF16) for u in range(ratio)
        ],
        compiler_params=params(),
        name="add_and_pack",
    )(mine, *theirs)


def finish(parts, kinds, width, scale):
    groups, block, lanes = parts[0].shape
    ratio = lanes // width

    def body(*refs):
        out = refs[-1]
        for g in range(groups):
            acc = refs[0][g]
            for ref in refs[1:-1]:
                acc = acc + ref[g].astype(F32)
            acc = acc * scale
            for q in range(ratio):
                moved = pltpu.roll(acc, lanes - q * width, 1) if q else acc
                out[g * ratio + q] = moved[:, :width]

    return pl.pallas_call(
        body,
        out_shape=jax.ShapeDtypeStruct((kinds, block, width), F32),
        compiler_params=params(),
        name="finish",
    )(*parts)


def volume_grad(deltas, weights, shape):
    cells_x, cells_y, cells_z, in_chan = shape
    nx, ny, nz = cells_x // 2, cells_y // 2, cells_z // 2
    ratio, rows, out_chan = deltas.shape

    def body(d_ref, w_ref, o_ref):
        row = lax.broadcasted_iota(jnp.int32, (cells_z, nz), 0)
        col = lax.broadcasted_iota(jnp.int32, (cells_z, nz), 1)
        wide = {}
        for k in range(8):
            e, q = k % 2, k % ratio
            if (e, q) not in wide:
                put = (row == 2 * col + e).astype(F32).astype(BF16)
                wide[e, q] = jnp.dot(put, d_ref[q], preferred_element_type=F32).astype(BF16)
        for a in range(2):
            for b in range(2):
                acc = None
                for e in range(2):
                    k = 4 * a + 2 * b + e
                    part = lax.dot_general(
                        wide[e, k % ratio], w_ref[k], (((1,), (1,)), ((), ())), preferred_element_type=F32
                    )
                    acc = part if acc is None else acc + part
                o_ref[a, b] = acc.astype(BF16)

    return pl.pallas_call(
        body,
        grid=(nx * ny,),
        in_specs=[pl.BlockSpec((ratio, nz, out_chan), lambda n: (0, n, 0)), whole(weights)],
        out_specs=pl.BlockSpec((2, 2, cells_z, in_chan), lambda n: (n // ny, n % ny, 0, 0)),
        out_shape=jax.ShapeDtypeStruct(shape, BF16),
        compiler_params=params(),
        cost_estimate=cost(32 * rows * in_chan * out_chan, 2 * rows * 8 * in_chan),
        name="volume_grad",
    )(deltas, weights)


def shards(spaces, chans, volume, weight, cotangent):
    kinds, block, width = weight.shape
    ratio = max(1, LANES // width)
    out_rows = volume.shape[0] * volume.shape[1] * volume.shape[2] // 8

    def pairs(count, step):
        return [(d, other(d, step)) for d in range(count)]

    packed = pack_weight(weight, ratio)
    tiles = pack_cot(cotangent.transpose(0, 1, 3, 2), chans)
    line = [packed[0]] + [fetch(packed[i % ratio], "chan", pairs(chans, i)) for i in range(1, chans)]
    cots = [tiles[0]] + [fetch(tiles[i], "chan", pairs(chans, i)) for i in range(1, chans)]
    lane_tiles = chans // ratio
    own = [merge_tile(line[t * ratio:(t + 1) * ratio], width) for t in range(lane_tiles)]
    upstream = turn_cot(cots)
    patches, turned = patch_rows(volume, own[1:])
    lines = []
    for j in range(0, spaces, 2):
        lines.append([fetch(tile, "space", pairs(spaces, j)) for tile in own] if j else own)
        lines.append([fetch(gate(tile, (upstream,)) if not j else tile, "space", pairs(spaces, 1)) for t, tile in enumerate(lines[-1])])
    deltas, weights = forward(patches, lines, upstream, width, ratio)
    steps = list(range(0, spaces, 2))
    lanes = ratio * width
    away = weight_part(turned, deltas, [s + 1 for s in steps], spaces, lanes, BF16)
    crossed = [fetch(tile, "space", pairs(spaces, 1)) for tile in away]
    near = weight_part(turned, deltas, steps, spaces, lanes, F32)
    got = [None] * chans
    for t in reversed(range(lane_tiles)):
        sums = add_core(near[t], crossed[t])
        came = [fetch(sums[n], "space", pairs(spaces, steps[n])) for n in range(1, len(steps))]
        parts = add_and_pack(sums[0], came, width, t == 0)
        for u in range(ratio):
            i = t * ratio + u
            got[i] = fetch(parts[u], "chan", pairs(chans, i)) if i else parts[u]
    grad_weight = finish(got, kinds, width, 1.0 / out_rows)
    grad_volume = volume_grad(deltas, weights, volume.shape)
    return (grad_volume, grad_weight)


def solution(mesh):
    return jax.shard_map(
        functools.partial(shards, mesh.shape["space"], mesh.shape["chan"]),
        mesh=mesh,
        in_specs=(
            P(("groups", "space"), "chan", None, None),
            P(None, "space", "chan"),
            P(("groups", "space"), None, None, "chan"),
        ),
        out_specs=(P(("groups", "space"), "chan", None, None), P("groups", "space", "chan")),
        check_vma=False,
    )
```

time: 51.9 us -> 44 us (0.85)
  waiting for transfers between devices: 15.9 us -> 12.4 us
  starting transfers between devices: 21.7 us -> 19.6 us
  Pallas kernels: 11.1 us -> 9.11 us
    ppermute x24 -> x19, waiting for transfers between devices: 15.9 us -> 12.4 us  [fetch(): return lax.ppermute(x, axis, pairs)]
    pallas_call x5 -> x11, Pallas kernels: 5.64 us -> 3.55 us  [the longest x1 2.37 us: patch_rows(): pl.pallas_call(body, in_specs=[pl.BlockSpec(memory_space=pltpu.VMEM)] + [...]
    ppermute x24 -> x19, starting transfers between devices: 21.7 us -> 19.6 us  [fetch(): return lax.ppermute(x, axis, pairs)]
    unnamed x3 -> x4, local copies, waits for them, and re-layouts: 2.12 us -> 1.85 us
  transfers between devices with their start and end apart: 24 -> 19, of which waited for: 8 -> 9; matrix products, arithmetic and copies ran while one was open for 2% -> 0% of each run, Pallas kernels for 16% -> 15%
where the time goes in v2:
time: 44 us; the launch traced here: 43.8 us
  starting transfers between devices  19.6 us (45%)
  waiting for transfers between devices  12.4 us (28%)
  Pallas kernels  9.11 us (21%)
  local copies, waits for them, and re-layouts  1.85 us (4%)
  between operations  0.77 us (2%)
    ppermute x19, starting transfers between devices, fetch(): return lax.ppermute(x, axis, pairs)  19.6 us
    ppermute x19, waiting for transfers between devices, fetch(): return lax.ppermute(x, axis, pairs)  12.4 us
    pallas_call x1, Pallas kernels, volume_grad(): pl.pallas_call(body, grid=(nx * ny,), in_specs=[pl.BlockSpec((ratio, nz,...  3.35 us
    pallas_call x1, Pallas kernels, patch_rows(): pl.pallas_call(body, in_specs=[pl.BlockSpec(memory_space=pltpu.VMEM)] + [...  2.37 us
    unnamed x4, local copies, waits for them, and re-layouts  1.85 us
    pallas_call x1, Pallas kernels, forward(): pl.pallas_call(body, out_shape=[jax.ShapeDtypeStruct((ratio, rows, out_ch...  1.1 us
  transfers between devices with their start and end apart: 19, of which 9 were waited for; matrix products, arithmetic and copies ran while one was open for 0% of the time, Pallas kernels for 15%

profile of v2, /device:TPU:0, one launch (start us, length us, event | category | flops | bytes accessed | tf_op | source)
XLA Modules:
  0.0 43.8 jit_solution(15076567037572090586)
XLA Ops:
  0.6 0.0 copy-start.1
  0.6 0.9 %copy-done.1 = bf16[8,64,64]{2,1,0:T(8,128)(2,1)S(1)} copy-done((bf16[8,64,64]{2,1,0:T(8,128)(2,1)S(1)}, bf16[8,64,64]{2,1,0:T(8,128)(2,1)}, u32[]{:S(2)}) %copy-start.1) | copy-done | bytes 65560
  1.5 0.1 pack_weight.1
  1.6 4.1 %collective-permute-start = (bf16[4,64,128]{2,1,0:T(8,128)(2,1)S(1)}, bf16[4,64,128]{2,1,0:T(8,128)(2,1)S(1)}, u32[]{:S(2)}, u32[]{:S(2)}) collective-permute-start(bf16[4,64,128]{2,1,0:T(8,128)(2,1)S(1)} %get-tuple-element.24.refs_0_), channel_id=1, source_target_pairs={{0,2},{1,3},{2,0},{3,1},{4,6},{5,7},{6,4},{7,5},{8,10},{9,11},{10,... | collective-permute-start | bytes 196616 | tf_op jit(solution)/shard_map/ppermute | solution.py:21
  5.7 1.6 %collective-permute-start.5 = (bf16[4,64,128]{2,1,0:T(8,128)(2,1)S(1)}, bf16[4,64,128]{2,1,0:T(8,128)(2,1)S(1)}, u32[]{:S(2)}, u32[]{:S(2)}) collective-permute-start(bf16[4,64,128]{2,1,0:T(8,128)(2,1)S(1)} %get-tuple-element.25), channel_id=1, source_target_pairs={{0,1},{1,0},{2,3},{3,2},{4,5},{5,4},{6,7},{7,6},{8,9},{9,8},{10,11... | collective-permute-start | bytes 196616 | tf_op jit(solution)/shard_map/ppermute | solution.py:21
  7.3 0.0 collective-permute-start.1
  7.3 0.0 copy-start
  7.3 0.9 %copy-done = bf16[2,8,128,64]{2,3,1,0:T(8,128)(2,1)S(1)} copy-done((bf16[2,8,128,64]{2,3,1,0:T(8,128)(2,1)S(1)}, bf16[2,8,128,64]{2,3,1,0:T(8,128)(2,1)}, u32[]{:S(2)}) %copy-start) | copy-done | bytes 262168
  8.3 1.0 %collective-permute-start.2 = (bf16[4,64,128]{2,1,0:T(8,128)(2,1)S(1)}, bf16[4,64,128]{2,1,0:T(8,128)(2,1)S(1)}, u32[]{:S(2)}, u32[]{:S(2)}) collective-permute-start(bf16[4,64,128]{2,1,0:T(8,128)(2,1)S(1)} %get-tuple-element.28), channel_id=1, source_target_pairs={{0,1},{1,0},{2,3},{3,2},{4,5},{5,4},{6,7},{7,6},{8,9},{9,8},{10,11... | collective-permute-start | bytes 196616 | tf_op jit(solution)/shard_map/ppermute | solution.py:21
  9.3 3.5 %collective-permute-start.3 = (bf16[4,64,128]{2,1,0:T(8,128)(2,1)S(1)}, bf16[4,64,128]{2,1,0:T(8,128)(2,1)S(1)}, u32[]{:S(2)}, u32[]{:S(2)}) collective-permute-start(bf16[4,64,128]{2,1,0:T(8,128)(2,1)S(1)} %get-tuple-element.29), channel_id=1, source_target_pairs={{0,2},{1,3},{2,0},{3,1},{4,6},{5,7},{6,4},{7,5},{8,10},{9,11},{10,... | collective-permute-start | bytes 196616 | tf_op jit(solution)/shard_map/ppermute | solution.py:21
  12.7 0.0 collective-permute-done.refs_0_
  12.8 1.2 %collective-permute-start.4 = (bf16[4,64,128]{2,1,0:T(8,128)(2,1)S(1)}, bf16[4,64,128]{2,1,0:T(8,128)(2,1)S(1)}, u32[]{:S(2)}, u32[]{:S(2)}) collective-permute-start(bf16[4,64,128]{2,1,0:T(8,128)(2,1)S(1)} %get-tuple-element.30), channel_id=1, source_target_pairs={{0,3},{1,2},{2,1},{3,0},{4,7},{5,6},{6,5},{7,4},{8,11},{9,10},{10,... | collective-permute-start | bytes 196616 | tf_op jit(solution)/shard_map/ppermute | solution.py:21
  13.9 0.2 collective-permute-done.1.refs_1_
  14.1 1.6 %collective-permute-start.9 = (bf16[8,64,128]{2,1,0:T(8,128)(2,1)S(1)}, bf16[8,64,128]{2,1,0:T(8,128)(2,1)S(1)}, u32[]{:S(2)}, u32[]{:S(2)}) collective-permute-start(bf16[8,64,128]{2,1,0:T(8,128)(2,1)S(1)} %merge_tile.2.refs_0_.t_ref.refs_1_), channel_id=1, source_target_pairs={{0,8},{4,12},{8,0},{12,4},{1,9},{5,13},{9,1},{13,5},{2,10},{6,14},... | collective-permute-start | bytes 393224 | tf_op jit(solution)/shard_map/ppermute | solution.py:21
  15.7 0.0 collective-permute-done.5.refs_1_
  15.7 0.6 %collective-permute-start.8 = (bf16[8,64,128]{2,1,0:T(8,128)(2,1)S(1)}, bf16[8,64,128]{2,1,0:T(8,128)(2,1)S(1)}, u32[]{:S(2)}, u32[]{:S(2)}) collective-permute-start(bf16[8,64,128]{2,1,0:T(8,128)(2,1)S(1)} %merge_tile.3.t_ref.refs_0_), channel_id=1, source_target_pairs={{0,8},{4,12},{8,0},{12,4},{1,9},{5,13},{9,1},{13,5},{2,10},{6,14},... | collective-permute-start | bytes 393224 | tf_op jit(solution)/shard_map/ppermute | solution.py:21
  16.3 0.0 collective-permute-done.2.refs_1_
  16.3 0.9 %collective-permute-done.3.refs_2_ = bf16[4,64,128]{2,1,0:T(8,128)(2,1)S(1)} collective-permute-done((bf16[4,64,128]{2,1,0:T(8,128)(2,1)S(1)}, bf16[4,64,128]{2,1,0:T(8,128)(2,1)S(1)}, u32[]{:S(2)}, u32[]{:S(2)}) %collective-permute-start.3) | collective-permute-done | bytes 65568 | tf_op jit(solution)/shard_map/ppermute | solution.py:21
  17.2 1.7 %collective-permute-done.4.refs_3_ = bf16[4,64,128]{2,1,0:T(8,128)(2,1)S(1)} collective-permute-done((bf16[4,64,128]{2,1,0:T(8,128)(2,1)S(1)}, bf16[4,64,128]{2,1,0:T(8,128)(2,1)S(1)}, u32[]{:S(2)}, u32[]{:S(2)}) %collective-permute-start.4) | collective-permute-done | bytes 65568 | tf_op jit(solution)/shard_map/ppermute | solution.py:21
  18.8 0.1 turn_cot.1.refs_0_.u_ref
  19.0 0.1 collective-permute-start.6
  19.1 0.5 %collective-permute-start.7 = (bf16[8,64,128]{2,1,0:T(8,128)(2,1)S(1)}, bf16[8,64,128]{2,1,0:T(8,128)(2,1)S(1)}, u32[]{:S(2)}, u32[]{:S(2)}) collective-permute-start(bf16[8,64,128]{2,1,0:T(8,128)(2,1)S(1)} %gate.3), channel_id=1, source_target_pairs={{0,4},{4,0},{8,12},{12,8},{1,5},{5,1},{9,13},{13,9},{2,6},{6,2},{1... | collective-permute-start | bytes 393224 | tf_op jit(solution)/shard_map/ppermute | solution.py:21
  19.6 0.0 collective-permute-done.9.refs_5_
  19.6 0.1 collective-permute-start.11
  19.6 1.1 %collective-permute-done.8.refs_4_ = bf16[8,64,128]{2,1,0:T(8,128)(2,1)S(1)} collective-permute-done((bf16[8,64,128]{2,1,0:T(8,128)(2,1)S(1)}, bf16[8,64,128]{2,1,0:T(8,128)(2,1)S(1)}, u32[]{:S(2)}, u32[]{:S(2)}) %collective-permute-start.8) | collective-permute-done | bytes 131104 | tf_op jit(solution)/shard_map/ppermute | solution.py:21
  20.7 0.0 collective-permute-start.10
  20.7 2.4 %patch_rows.1 = (bf16[8,512,256]{2,1,0:T(8,128)(2,1)S(1)}, bf16[8,256,512]{2,1,0:T(8,128)(2,1)S(1)}) custom-call(bf16[4,4,256,256]{3,2,1,0:T(8,128)(2,1)} %v_ref.1, bf16[8,64,128]{2,1,0:T(8,128)(2,1)S(1)} %merge_tile.2.refs_0_.t_ref.refs_1_), custom_call_target="tpu_custom_call" | custom-call | flops 536870912 | bytes 6291456 | tf_op jit(solution)/shard_map/patch_rows/pallas_call | solution.py:174
  23.1 0.0 collective-permute-done.6.refs_2_
  23.1 0.0 collective-permute-done.7.refs_3_
  23.1 0.0 collective-permute-done.11.refs_7_
  23.2 0.0 collective-permute-done.10.refs_6_
  23.2 1.1 %forward.1 = (bf16[2,512,256]{2,1,0:T(8,128)(2,1)S(1)}, bf16[8,256,256]{2,1,0:T(8,128)(2,1)S(1)}) custom-call(bf16[8,512,256]{2,1,0:T(8,128)(2,1)S(1)} %get-tuple-element.26.p_ref, bf16[512,256]{1,0:T(8,128)(2,1)S(1)} %turn_cot.1.refs_0_.u_ref, bf16[8,64,128]{2,1,0:T(8,128)(2,1)S(1)} %merge_tile.3.t_ref.refs_0_, ...), custom_call_target="tpu_custom_call" | custom-call | flops 536870912 | bytes 2097152 | tf_op jit(solution)/shard_map/forward/pallas_call | solution.py:241
  24.3 0.4 %weight_part.3 = (bf16[2,8,64,128]{3,2,1,0:T(8,128)(2,1)S(1)}, bf16[2,8,64,128]{3,2,1,0:T(8,128)(2,1)S(1)}) custom-call(bf16[8,256,512]{2,1,0:T(8,128)(2,1)S(1)} %get-tuple-element.33.t_ref, bf16[2,512,256]{2,1,0:T(8,128)(2,1)S(1)} %get-tuple-element.31.d_ref), custom_call_target="tpu_custom_call" | custom-call | flops 268435456 | bytes 2097152 | tf_op jit(solution)/shard_map/weight_part/pallas_call | solution.py:271
  24.7 0.6 %collective-permute-start.12 = (bf16[2,8,64,128]{3,2,1,0:T(8,128)(2,1)S(1)}, bf16[2,8,64,128]{3,2,1,0:T(8,128)(2,1)S(1)}, u32[]{:S(2)}, u32[]{:S(2)}) collective-permute-start(bf16[2,8,64,128]{3,2,1,0:T(8,128)(2,1)S(1)} %get-tuple-element.35), channel_id=1, source_target_pairs={{0,4},{4,0},{8,12},{12,8},{1,5},{5,1},{9,13},{13,9},{2,6},{6,2},{1... | collective-permute-start | bytes 786440 | tf_op jit(solution)/shard_map/ppermute | solution.py:21
  25.3 0.1 collective-permute-start.15
  25.4 0.4 weight_part.2
  25.8 0.6 %collective-permute-done.12.b_ref = bf16[2,8,64,128]{3,2,1,0:T(8,128)(2,1)S(1)} collective-permute-done((bf16[2,8,64,128]{3,2,1,0:T(8,128)(2,1)S(1)}, bf16[2,8,64,128]{3,2,1,0:T(8,128)(2,1)S(1)}, u32[]{:S(2)}, u32[]{:S(2)}) %collective-permute-start.12) | collective-permute-done | bytes 262176 | tf_op jit(solution)/shard_map/ppermute | solution.py:21
  26.5 1.4 %collective-permute-start.13 = (bf16[8,64,128]{2,1,0:T(8,128)(2,1)S(1)}, bf16[8,64,128]{2,1,0:T(8,128)(2,1)S(1)}, u32[]{:S(2)}, u32[]{:S(2)}) collective-permute-start(bf16[8,64,128]{2,1,0:T(8,128)(2,1)S(1)} %get-tuple-element.37), channel_id=1, source_target_pairs={{0,8},{4,12},{8,0},{12,4},{1,9},{5,13},{9,1},{13,5},{2,10},{6,14},... | collective-permute-start | bytes 393224 | tf_op jit(solution)/shard_map/ppermute | solution.py:21
  27.9 0.0 collective-permute-done.15.b_ref
  27.9 0.8 %collective-permute-start.16 = (bf16[8,64,128]{2,1,0:T(8,128)(2,1)S(1)}, bf16[8,64,128]{2,1,0:T(8,128)(2,1)S(1)}, u32[]{:S(2)}, u32[]{:S(2)}) collective-permute-start(bf16[8,64,128]{2,1,0:T(8,128)(2,1)S(1)} %get-tuple-element.43), channel_id=1, source_target_pairs={{0,8},{4,12},{8,0},{12,4},{1,9},{5,13},{9,1},{13,5},{2,10},{6,14},... | collective-permute-start | bytes 393224 | tf_op jit(solution)/shard_map/ppermute | solution.py:21
  28.7 4.2 %collective-permute-done.13.refs_1_ = bf16[8,64,128]{2,1,0:T(8,128)(2,1)S(1)} collective-permute-done((bf16[8,64,128]{2,1,0:T(8,128)(2,1)S(1)}, bf16[8,64,128]{2,1,0:T(8,128)(2,1)S(1)}, u32[]{:S(2)}, u32[]{:S(2)}) %collective-permute-start.13) | collective-permute-done | bytes 131104 | tf_op jit(solution)/shard_map/ppermute | solution.py:21
  32.9 0.1 add_and_pack.2
  33.0 0.1 collective-permute-start.14
  33.1 2.1 %collective-permute-done.16.refs_1_ = bf16[8,64,128]{2,1,0:T(8,128)(2,1)S(1)} collective-permute-done((bf16[8,64,128]{2,1,0:T(8,128)(2,1)S(1)}, bf16[8,64,128]{2,1,0:T(8,128)(2,1)S(1)}, u32[]{:S(2)}, u32[]{:S(2)}) %collective-permute-start.16) | collective-permute-done | bytes 131104 | tf_op jit(solution)/shard_map/ppermute | solution.py:21
  35.1 0.1 add_and_pack.3
  35.3 1.6 %collective-permute-start.17 = (bf16[4,64,128]{2,1,0:T(8,128)(2,1)S(1)}, bf16[4,64,128]{2,1,0:T(8,128)(2,1)S(1)}, u32[]{:S(2)}, u32[]{:S(2)}) collective-permute-start(bf16[4,64,128]{2,1,0:T(8,128)(2,1)S(1)} %get-tuple-element.44), channel_id=1, source_target_pairs={{0,2},{1,3},{2,0},{3,1},{4,6},{5,7},{6,4},{7,5},{8,10},{9,11},{10,... | collective-permute-start | bytes 196616 | tf_op jit(solution)/shard_map/ppermute | solution.py:21
  36.8 1.1 %collective-permute-start.18 = (bf16[4,64,128]{2,1,0:T(8,128)(2,1)S(1)}, bf16[4,64,128]{2,1,0:T(8,128)(2,1)S(1)}, u32[]{:S(2)}, u32[]{:S(2)}) collective-permute-start(bf16[4,64,128]{2,1,0:T(8,128)(2,1)S(1)} %get-tuple-element.45), channel_id=1, source_target_pairs={{0,3},{1,2},{2,1},{3,0},{4,7},{5,6},{6,5},{7,4},{8,11},{9,10},{10,... | collective-permute-start | bytes 196616 | tf_op jit(solution)/shard_map/ppermute | solution.py:21
  37.9 3.3 %volume_grad.1 = bf16[4,4,256,256]{3,2,1,0:T(8,128)(2,1)} custom-call(bf16[2,512,256]{2,1,0:T(8,128)(2,1)S(1)} %get-tuple-element.31.d_ref, bf16[8,256,256]{2,1,0:T(8,128)(2,1)S(1)} %get-tuple-element.32.w_ref), custom_call_target="tpu_custom_call" | custom-call | flops 1073741824 | bytes 2097152 | tf_op jit(solution)/shard_map/volume_grad/pallas_call | solution.py:371
  41.2 0.0 collective-permute-done.14.refs_1_
  41.2 1.0 %collective-permute-done.17.refs_2_ = bf16[4,64,128]{2,1,0:T(8,128)(2,1)S(1)} collective-permute-done((bf16[4,64,128]{2,1,0:T(8,128)(2,1)S(1)}, bf16[4,64,128]{2,1,0:T(8,128)(2,1)S(1)}, u32[]{:S(2)}, u32[]{:S(2)}) %collective-permute-start.17) | collective-permute-done | bytes 65568 | tf_op jit(solution)/shard_map/ppermute | solution.py:21
  42.2 0.8 %collective-permute-done.18.refs_3_ = bf16[4,64,128]{2,1,0:T(8,128)(2,1)S(1)} collective-permute-done((bf16[4,64,128]{2,1,0:T(8,128)(2,1)S(1)}, bf16[4,64,128]{2,1,0:T(8,128)(2,1)S(1)}, u32[]{:S(2)}, u32[]{:S(2)}) %collective-permute-start.18) | collective-permute-done | bytes 65568 | tf_op jit(solution)/shard_map/ppermute | solution.py:21
  43.0 0.8 %finish.1 = f32[8,64,64]{2,1,0:T(8,128)} custom-call(f32[4,64,128]{2,1,0:T(8,128)S(1)} %get-tuple-element.38.refs_0_, bf16[4,64,128]{2,1,0:T(8,128)(2,1)S(1)} %collective-permute-done.14.refs_1_, bf16[4,64,128]{2,1,0:T(8,128)(2,1)S(1)} %collective-permute-done.17.refs_2_, bf16[4,64,128]{2,1,0:T(8,128)(2,1)S(1)} %collective-permute-done.18.refs_3_), custom_call_target="tpu_custom_call" | custom-call | tf_op jit(solution)/shard_map/finish/pallas_call | solution.py:338
  (7 shorter events, 0.2 us)
Async XLA Ops:
  0.6 0.9 %copy-start.1 = (bf16[8,64,64]{2,1,0:T(8,128)(2,1)S(1)}, bf16[8,64,64]{2,1,0:T(8,128)(2,1)}, u32[]{:S(2)}) copy-start(bf16[8,64,64]{2,1,0:T(8,128)(2,1)} %w_ref.1) | copy-start | bytes 196612
  1.6 11.1 %collective-permute-start = (bf16[4,64,128]{2,1,0:T(8,128)(2,1)S(1)}, bf16[4,64,128]{2,1,0:T(8,128)(2,1)S(1)}, u32[]{:S(2)}, u32[]{:S(2)}) collective-permute-start(bf16[4,64,128]{2,1,0:T(8,128)(2,1)S(1)} %get-tuple-element.24.refs_0_), channel_id=1, source_target_pairs={{0,2},{1,3},{2,0},{3,1},{4,6},{5,7},{6,4},{7,5},{8,10},{9,11},{10,... | collective-permute-start | bytes 196616 | tf_op jit(solution)/shard_map/ppermute | solution.py:21
  5.7 9.9 %collective-permute-start.5 = (bf16[4,64,128]{2,1,0:T(8,128)(2,1)S(1)}, bf16[4,64,128]{2,1,0:T(8,128)(2,1)S(1)}, u32[]{:S(2)}, u32[]{:S(2)}) collective-permute-start(bf16[4,64,128]{2,1,0:T(8,128)(2,1)S(1)} %get-tuple-element.25), channel_id=1, source_target_pairs={{0,1},{1,0},{2,3},{3,2},{4,5},{5,4},{6,7},{7,6},{8,9},{9,8},{10,11... | collective-permute-start | bytes 196616 | tf_op jit(solution)/shard_map/ppermute | solution.py:21
  7.3 6.8 %collective-permute-start.1 = (bf16[4,64,128]{2,1,0:T(8,128)(2,1)S(1)}, bf16[4,64,128]{2,1,0:T(8,128)(2,1)S(1)}, u32[]{:S(2)}, u32[]{:S(2)}) collective-permute-start(bf16[4,64,128]{2,1,0:T(8,128)(2,1)S(1)} %get-tuple-element.25), channel_id=1, source_target_pairs={{0,3},{1,2},{2,1},{3,0},{4,7},{5,6},{6,5},{7,4},{8,11},{9,10},{10,... | collective-permute-start | bytes 196616 | tf_op jit(solution)/shard_map/ppermute | solution.py:21
  7.3 1.0 %copy-start = (bf16[2,8,128,64]{2,3,1,0:T(8,128)(2,1)S(1)}, bf16[2,8,128,64]{2,3,1,0:T(8,128)(2,1)}, u32[]{:S(2)}) copy-start(bf16[2,8,128,64]{2,3,1,0:T(8,128)(2,1)} %param.5) | copy-start | bytes 786436
  8.3 8.0 %collective-permute-start.2 = (bf16[4,64,128]{2,1,0:T(8,128)(2,1)S(1)}, bf16[4,64,128]{2,1,0:T(8,128)(2,1)S(1)}, u32[]{:S(2)}, u32[]{:S(2)}) collective-permute-start(bf16[4,64,128]{2,1,0:T(8,128)(2,1)S(1)} %get-tuple-element.28), channel_id=1, source_target_pairs={{0,1},{1,0},{2,3},{3,2},{4,5},{5,4},{6,7},{7,6},{8,9},{9,8},{10,11... | collective-permute-start | bytes 196616 | tf_op jit(solution)/shard_map/ppermute | solution.py:21
  9.3 7.9 %collective-permute-start.3 = (bf16[4,64,128]{2,1,0:T(8,128)(2,1)S(1)}, bf16[4,64,128]{2,1,0:T(8,128)(2,1)S(1)}, u32[]{:S(2)}, u32[]{:S(2)}) collective-permute-start(bf16[4,64,128]{2,1,0:T(8,128)(2,1)S(1)} %get-tuple-element.29), channel_id=1, source_target_pairs={{0,2},{1,3},{2,0},{3,1},{4,6},{5,7},{6,4},{7,5},{8,10},{9,11},{10,... | collective-permute-start | bytes 196616 | tf_op jit(solution)/shard_map/ppermute | solution.py:21
  12.8 6.1 %collective-permute-start.4 = (bf16[4,64,128]{2,1,0:T(8,128)(2,1)S(1)}, bf16[4,64,128]{2,1,0:T(8,128)(2,1)S(1)}, u32[]{:S(2)}, u32[]{:S(2)}) collective-permute-start(bf16[4,64,128]{2,1,0:T(8,128)(2,1)S(1)} %get-tuple-element.30), channel_id=1, source_target_pairs={{0,3},{1,2},{2,1},{3,0},{4,7},{5,6},{6,5},{7,4},{8,11},{9,10},{10,... | collective-permute-start | bytes 196616 | tf_op jit(solution)/shard_map/ppermute | solution.py:21
  14.1 5.4 %collective-permute-start.9 = (bf16[8,64,128]{2,1,0:T(8,128)(2,1)S(1)}, bf16[8,64,128]{2,1,0:T(8,128)(2,1)S(1)}, u32[]{:S(2)}, u32[]{:S(2)}) collective-permute-start(bf16[8,64,128]{2,1,0:T(8,128)(2,1)S(1)} %merge_tile.2.refs_0_.t_ref.refs_1_), channel_id=1, source_target_pairs={{0,8},{4,12},{8,0},{12,4},{1,9},{5,13},{9,1},{13,5},{2,10},{6,14},... | collective-permute-start | bytes 393224 | tf_op jit(solution)/shard_map/ppermute | solution.py:21
  15.7 5.0 %collective-permute-start.8 = (bf16[8,64,128]{2,1,0:T(8,128)(2,1)S(1)}, bf16[8,64,128]{2,1,0:T(8,128)(2,1)S(1)}, u32[]{:S(2)}, u32[]{:S(2)}) collective-permute-start(bf16[8,64,128]{2,1,0:T(8,128)(2,1)S(1)} %merge_tile.3.t_ref.refs_0_), channel_id=1, source_target_pairs={{0,8},{4,12},{8,0},{12,4},{1,9},{5,13},{9,1},{13,5},{2,10},{6,14},... | collective-permute-start | bytes 393224 | tf_op jit(solution)/shard_map/ppermute | solution.py:21
  19.0 4.2 %collective-permute-start.6 = (bf16[8,64,128]{2,1,0:T(8,128)(2,1)S(1)}, bf16[8,64,128]{2,1,0:T(8,128)(2,1)S(1)}, u32[]{:S(2)}, u32[]{:S(2)}) collective-permute-start(bf16[8,64,128]{2,1,0:T(8,128)(2,1)S(1)} %gate.2), channel_id=1, source_target_pairs={{0,4},{4,0},{8,12},{12,8},{1,5},{5,1},{9,13},{13,9},{2,6},{6,2},{1... | collective-permute-start | bytes 393224 | tf_op jit(solution)/shard_map/ppermute | solution.py:21
  19.1 4.1 %collective-permute-start.7 = (bf16[8,64,128]{2,1,0:T(8,128)(2,1)S(1)}, bf16[8,64,128]{2,1,0:T(8,128)(2,1)S(1)}, u32[]{:S(2)}, u32[]{:S(2)}) collective-permute-start(bf16[8,64,128]{2,1,0:T(8,128)(2,1)S(1)} %gate.3), channel_id=1, source_target_pairs={{0,4},{4,0},{8,12},{12,8},{1,5},{5,1},{9,13},{13,9},{2,6},{6,2},{1... | collective-permute-start | bytes 393224 | tf_op jit(solution)/shard_map/ppermute | solution.py:21
  19.6 3.6 %collective-permute-start.11 = (bf16[8,64,128]{2,1,0:T(8,128)(2,1)S(1)}, bf16[8,64,128]{2,1,0:T(8,128)(2,1)S(1)}, u32[]{:S(2)}, u32[]{:S(2)}) collective-permute-start(bf16[8,64,128]{2,1,0:T(8,128)(2,1)S(1)} %collective-permute-done.9.refs_5_), channel_id=1, source_target_pairs={{0,4},{4,0},{8,12},{12,8},{1,5},{5,1},{9,13},{13,9},{2,6},{6,2},{1... | collective-permute-start | bytes 393224 | tf_op jit(solution)/shard_map/ppermute | solution.py:21
  20.7 2.4 %collective-permute-start.10 = (bf16[8,64,128]{2,1,0:T(8,128)(2,1)S(1)}, bf16[8,64,128]{2,1,0:T(8,128)(2,1)S(1)}, u32[]{:S(2)}, u32[]{:S(2)}) collective-permute-start(bf16[8,64,128]{2,1,0:T(8,128)(2,1)S(1)} %collective-permute-done.8.refs_4_), channel_id=1, source_target_pairs={{0,4},{4,0},{8,12},{12,8},{1,5},{5,1},{9,13},{13,9},{2,6},{6,2},{1... | collective-permute-start | bytes 393224 | tf_op jit(solution)/shard_map/ppermute | solution.py:21
  24.7 1.7 %collective-permute-start.12 = (bf16[2,8,64,128]{3,2,1,0:T(8,128)(2,1)S(1)}, bf16[2,8,64,128]{3,2,1,0:T(8,128)(2,1)S(1)}, u32[]{:S(2)}, u32[]{:S(2)}) collective-permute-start(bf16[2,8,64,128]{3,2,1,0:T(8,128)(2,1)S(1)} %get-tuple-element.35), channel_id=1, source_target_pairs={{0,4},{4,0},{8,12},{12,8},{1,5},{5,1},{9,13},{13,9},{2,6},{6,2},{1... | collective-permute-start | bytes 786440 | tf_op jit(solution)/shard_map/ppermute | solution.py:21
  25.3 2.6 %collective-permute-start.15 = (bf16[2,8,64,128]{3,2,1,0:T(8,128)(2,1)S(1)}, bf16[2,8,64,128]{3,2,1,0:T(8,128)(2,1)S(1)}, u32[]{:S(2)}, u32[]{:S(2)}) collective-permute-start(bf16[2,8,64,128]{3,2,1,0:T(8,128)(2,1)S(1)} %get-tuple-element.41), channel_id=1, source_target_pairs={{0,4},{4,0},{8,12},{12,8},{1,5},{5,1},{9,13},{13,9},{2,6},{6,2},{1... | collective-permute-start | bytes 786440 | tf_op jit(solution)/shard_map/ppermute | solution.py:21
  26.5 6.4 %collective-permute-start.13 = (bf16[8,64,128]{2,1,0:T(8,128)(2,1)S(1)}, bf16[8,64,128]{2,1,0:T(8,128)(2,1)S(1)}, u32[]{:S(2)}, u32[]{:S(2)}) collective-permute-start(bf16[8,64,128]{2,1,0:T(8,128)(2,1)S(1)} %get-tuple-element.37), channel_id=1, source_target_pairs={{0,8},{4,12},{8,0},{12,4},{1,9},{5,13},{9,1},{13,5},{2,10},{6,14},... | collective-permute-start | bytes 393224 | tf_op jit(solution)/shard_map/ppermute | solution.py:21
  27.9 7.2 %collective-permute-start.16 = (bf16[8,64,128]{2,1,0:T(8,128)(2,1)S(1)}, bf16[8,64,128]{2,1,0:T(8,128)(2,1)S(1)}, u32[]{:S(2)}, u32[]{:S(2)}) collective-permute-start(bf16[8,64,128]{2,1,0:T(8,128)(2,1)S(1)} %get-tuple-element.43), channel_id=1, source_target_pairs={{0,8},{4,12},{8,0},{12,4},{1,9},{5,13},{9,1},{13,5},{2,10},{6,14},... | collective-permute-start | bytes 393224 | tf_op jit(solution)/shard_map/ppermute | solution.py:21
  33.0 8.2 %collective-permute-start.14 = (bf16[4,64,128]{2,1,0:T(8,128)(2,1)S(1)}, bf16[4,64,128]{2,1,0:T(8,128)(2,1)S(1)}, u32[]{:S(2)}, u32[]{:S(2)}) collective-permute-start(bf16[4,64,128]{2,1,0:T(8,128)(2,1)S(1)} %get-tuple-element.39), channel_id=1, source_target_pairs={{0,1},{1,0},{2,3},{3,2},{4,5},{5,4},{6,7},{7,6},{8,9},{9,8},{10,11... | collective-permute-start | bytes 196616 | tf_op jit(solution)/shard_map/ppermute | solution.py:21
  35.3 7.0 %collective-permute-start.17 = (bf16[4,64,128]{2,1,0:T(8,128)(2,1)S(1)}, bf16[4,64,128]{2,1,0:T(8,128)(2,1)S(1)}, u32[]{:S(2)}, u32[]{:S(2)}) collective-permute-start(bf16[4,64,128]{2,1,0:T(8,128)(2,1)S(1)} %get-tuple-element.44), channel_id=1, source_target_pairs={{0,2},{1,3},{2,0},{3,1},{4,6},{5,7},{6,4},{7,5},{8,10},{9,11},{10,... | collective-permute-start | bytes 196616 | tf_op jit(solution)/shard_map/ppermute | solution.py:21
  36.8 6.2 %collective-permute-start.18 = (bf16[4,64,128]{2,1,0:T(8,128)(2,1)S(1)}, bf16[4,64,128]{2,1,0:T(8,128)(2,1)S(1)}, u32[]{:S(2)}, u32[]{:S(2)}) collective-permute-start(bf16[4,64,128]{2,1,0:T(8,128)(2,1)S(1)} %get-tuple-element.45), channel_id=1, source_target_pairs={{0,3},{1,2},{2,1},{3,0},{4,7},{5,6},{6,5},{7,4},{8,11},{9,10},{10,... | collective-permute-start | bytes 196616 | tf_op jit(solution)/shard_map/ppermute | solution.py:21

commit v3 on v2

--- a/solution.py
+++ b/solution.py
@@ -96,11 +96,12 @@
     )(weight)
 
 
-def pack_cot(cot, chans):
+def pack_cot(cot, chans, after=()):
     planes, cells_y, width, cells_z = cot.shape
     own_y = cells_y // chans
 
-    def body(c_ref, *outs):
+    def body(c_ref, *refs):
+        outs = refs[len(after):]
         me = lax.axis_index("chan")
         for step in range(chans):
             target = other(me, step) * own_y
@@ -110,10 +111,11 @@
 
     return pl.pallas_call(
         body,
+        in_specs=[pl.BlockSpec(memory_space=pltpu.VMEM)] + [pl.BlockSpec(memory_space=pl.ANY)] * len(after),
         out_shape=[jax.ShapeDtypeStruct((planes * own_y, width, cells_z), BF16)] * chans,
         compiler_params=params(),
         name="pack_cot",
-    )(cot)
+    )(cot, *after)
 
 
 def merge_tile(parts, width, after=()):
@@ -292,13 +294,13 @@
     )(mine, theirs)
 
 
-def add_and_pack(mine, theirs, width, own):
+def add_and_pack(mine, theirs, width, after=()):
     kinds, block, lanes = mine.shape
     ratio = lanes // width
     groups = kinds // ratio
 
     def body(*refs):
-        ins, outs = refs[:1 + len(theirs)], refs[1 + len(theirs):]
+        ins, outs = refs[:1 + len(theirs)], refs[1 + len(theirs) + len(after):]
         for g in range(groups):
             sums = []
             for q in range(ratio):
@@ -307,17 +309,81 @@
                     acc = acc + ref[g * ratio + q].astype(F32)
                 sums.append(acc)
             for u in range(ratio):
-                packed = swap_groups(merge(sums, width, u), width, u)
-                outs[u][g] = packed.astype(outs[u].dtype)
-
-    return pl.pallas_call(
-        body,
+                outs[u][g] = swap_groups(merge(sums, width, u), width, u).astype(BF16)
+
+    return pl.pallas_call(
+        body,
+        in_specs=[pl.BlockSpec(memory_space=pltpu.VMEM)] * (1 + len(theirs))
+        + [pl.BlockSpec(memory_space=pl.ANY)] * len(after),
+        out_shape=[jax.ShapeDtypeStruct((groups, block, lanes), BF16)] * ratio,
+        compiler_params=params(),
+        name="add_and_pack",
+    )(mine, *theirs, *after)
+
+
+def add_core_near(mine, theirs, width, after=()):
+    count, kinds, block, lanes = mine.shape
+    ratio = lanes // width
+    groups = kinds // ratio
+
+    def body(a_ref, b_ref, *refs):
+        outs = refs[len(after):]
+        for n in range(count):
+            for g in range(groups):
+                at = n * groups + g
+                sums = [
+                    a_ref[n, g * ratio + q] + b_ref[n, g * ratio + q].astype(F32) for q in range(ratio)
+                ]
+                for u in range(ratio):
+                    outs[u][at] = swap_groups(merge(sums, width, u), width, u).astype(outs[u].dtype)
+
+    return pl.pallas_call(
+        body,
+        in_specs=[pl.BlockSpec(memory_space=pltpu.VMEM)] * 2 + [pl.BlockSpec(memory_space=pl.ANY)] * len(after),
         out_shape=[
-            jax.ShapeDtypeStruct((groups, block, lanes), F32 if own and u == 0 else BF16) for u in range(ratio)
+            jax.ShapeDtypeStruct((count * groups, block, lanes), BF16 if u else F32) for u in range(ratio)
         ],
         compiler_params=params(),
-        name="add_and_pack",
-    )(mine, *theirs)
+        name="add_core_near",
+    )(mine, theirs, *after)
+
+
+def add_near(mine, theirs, groups, after=()):
+    total, block, lanes = mine.shape
+    count = total // groups
+
+    def body(*refs):
+        ins, outs = refs[:1 + len(theirs)], refs[1 + len(theirs) + len(after):]
+        for n in range(count):
+            here = slice(n * groups, (n + 1) * groups)
+            acc = ins[0][here]
+            for ref in ins[1:]:
+                acc = acc + ref[here].astype(F32)
+            outs[n][...] = acc.astype(outs[n].dtype)
+
+    return pl.pallas_call(
+        body,
+        in_specs=[pl.BlockSpec(memory_space=pltpu.VMEM)] * (1 + len(theirs))
+        + [pl.BlockSpec(memory_space=pl.ANY)] * len(after),
+        out_shape=[jax.ShapeDtypeStruct((groups, block, lanes), BF16 if n else F32) for n in range(count)],
+        compiler_params=params(),
+        name="add_near",
+    )(mine, *theirs, *after)
+
+
+def fold(parts):
+    def body(*refs):
+        acc = refs[0][...].astype(F32)
+        for ref in refs[1:-1]:
+            acc = acc + ref[...].astype(F32)
+        refs[-1][...] = acc
+
+    return pl.pallas_call(
+        body,
+        out_shape=jax.ShapeDtypeStruct(parts[0].shape, F32),
+        compiler_params=params(),
+        name="fold",
+    )(*parts)
 
 
 def finish(parts, kinds, width, scale):
@@ -348,7 +414,8 @@
     nx, ny, nz = cells_x // 2, cells_y // 2, cells_z // 2
     ratio, rows, out_chan = deltas.shape
 
-    def body(d_ref, w_ref, o_ref):
+    def body(d_ref, w_ref, o_ref, mark_ref):
+        mark_ref[...] = jnp.zeros_like(mark_ref)
         row = lax.broadcasted_iota(jnp.int32, (cells_z, nz), 0)
         col = lax.broadcasted_iota(jnp.int32, (cells_z, nz), 1)
         wide = {}
@@ -372,8 +439,11 @@
         body,
         grid=(nx * ny,),
         in_specs=[pl.BlockSpec((ratio, nz, out_chan), lambda n: (0, n, 0)), whole(weights)],
-        out_specs=pl.BlockSpec((2, 2, cells_z, in_chan), lambda n: (n // ny, n % ny, 0, 0)),
-        out_shape=jax.ShapeDtypeStruct(shape, BF16),
+        out_specs=[
+            pl.BlockSpec((2, 2, cells_z, in_chan), lambda n: (n // ny, n % ny, 0, 0)),
+            pl.BlockSpec((8, LANES), lambda n: (0, 0)),
+        ],
+        out_shape=[jax.ShapeDtypeStruct(shape, BF16), jax.ShapeDtypeStruct((8, LANES), F32)],
         compiler_params=params(),
         cost_estimate=cost(32 * rows * in_chan * out_chan, 2 * rows * 8 * in_chan),
         name="volume_grad",
@@ -389,33 +459,37 @@
         return [(d, other(d, step)) for d in range(count)]
 
     packed = pack_weight(weight, ratio)
-    tiles = pack_cot(cotangent.transpose(0, 1, 3, 2), chans)
     line = [packed[0]] + [fetch(packed[i % ratio], "chan", pairs(chans, i)) for i in range(1, chans)]
-    cots = [tiles[0]] + [fetch(tiles[i], "chan", pairs(chans, i)) for i in range(1, chans)]
     lane_tiles = chans // ratio
     own = [merge_tile(line[t * ratio:(t + 1) * ratio], width) for t in range(lane_tiles)]
+    tiles = pack_cot(cotangent.transpose(0, 1, 3, 2), chans, own[:1])
+    cots = [tiles[0]] + [fetch(tiles[i], "chan", pairs(chans, i)) for i in range(1, chans)]
     upstream = turn_cot(cots)
     patches, turned = patch_rows(volume, own[1:])
     lines = []
     for j in range(0, spaces, 2):
         lines.append([fetch(tile, "space", pairs(spaces, j)) for tile in own] if j else own)
-        lines.append([fetch(gate(tile, (upstream,)) if not j else tile, "space", pairs(spaces, 1)) for t, tile in enumerate(lines[-1])])
+        lines.append([fetch(gate(tile, (upstream,)) if not j and t else gate(tile, (patches,)) if not j else tile, "space", pairs(spaces, 1)) for t, tile in enumerate(lines[-1])])
     deltas, weights = forward(patches, lines, upstream, width, ratio)
     steps = list(range(0, spaces, 2))
     lanes = ratio * width
     away = weight_part(turned, deltas, [s + 1 for s in steps], spaces, lanes, BF16)
     crossed = [fetch(tile, "space", pairs(spaces, 1)) for tile in away]
     near = weight_part(turned, deltas, steps, spaces, lanes, F32)
-    got = [None] * chans
-    for t in reversed(range(lane_tiles)):
+    grad_volume, mark = volume_grad(deltas, weights, volume.shape)
+    far, outs = [], []
+    for t in reversed(range(1, lane_tiles)):
         sums = add_core(near[t], crossed[t])
+        far = list(sums[1:]) + far
         came = [fetch(sums[n], "space", pairs(spaces, steps[n])) for n in range(1, len(steps))]
-        parts = add_and_pack(sums[0], came, width, t == 0)
-        for u in range(ratio):
-            i = t * ratio + u
-            got[i] = fetch(parts[u], "chan", pairs(chans, i)) if i else parts[u]
+        outs += [(t * ratio + u, part) for u, part in enumerate(add_and_pack(sums[0], came, width, (mark,)))]
+    parts = add_core_near(near[0], crossed[0], width, far[:1])
+    got = [fetch(parts[u], "chan", pairs(chans, u)) for u in range(1, ratio)]
+    sums = add_near(parts[0], got, kinds // ratio, [part for _, part in outs[-1:]])
+    got = [sums[0]] + [fetch(sums[n], "space", pairs(spaces, steps[n])) for n in range(1, len(steps))]
+    spread_out = [fetch(part, "chan", pairs(chans, i)) for i, part in outs]
+    got += [fold(spread_out)] if spread_out else []
     grad_weight = finish(got, kinds, width, 1.0 / out_rows)
-    grad_volume = volume_grad(deltas, weights, volume.shape)
     return (grad_volume, grad_weight)
 
 

time: 44 us -> 41.3 us (0.939)
  waiting for transfers between devices: 12.4 us -> 7.74 us
  starting transfers between devices: 19.6 us -> 21.6 us
    ppermute x19, waiting for transfers between devices: 12.4 us -> 7.74 us  [fetch(): return lax.ppermute(x, axis, pairs)]
    ppermute x19, starting transfers between devices: 19.6 us -> 21.6 us  [fetch(): return lax.ppermute(x, axis, pairs)]
  transfers between devices with their start and end apart: 19 -> 19, of which waited for: 9 -> 9; matrix products, arithmetic and copies ran while one was open for 0% -> 0% of each run, Pallas kernels for 15% -> 16%
where the time goes in v3:
time: 41.3 us; the launch traced here: 41.1 us
  starting transfers between devices  21.6 us (52%)
  Pallas kernels  9.12 us (22%)
  waiting for transfers between devices  7.74 us (19%)
  local copies, waits for them, and re-layouts  1.84 us (4%)
  between operations  0.78 us (2%)
    ppermute x19, starting transfers between devices, fetch(): return lax.ppermute(x, axis, pairs)  21.6 us
    ppermute x19, waiting for transfers between devices, fetch(): return lax.ppermute(x, axis, pairs)  7.74 us
    pallas_call x1, Pallas kernels, volume_grad(): pl.pallas_call(body, grid=(nx * ny,), in_specs=[pl.BlockSpec((ratio, nz,...  3.35 us
    pallas_call x1, Pallas kernels, patch_rows(): pl.pallas_call(body, in_specs=[pl.BlockSpec(memory_space=pltpu.VMEM)] + [...  2.37 us
    unnamed x4, local copies, waits for them, and re-layouts  1.84 us
    pallas_call x1, Pallas kernels, forward(): pl.pallas_call(body, out_shape=[jax.ShapeDtypeStruct((ratio, rows, out_ch...  1.09 us
    pallas_call x2, Pallas kernels, weight_part(): pl.pallas_call(body, out_shape=[jax.ShapeDtypeStruct((len(steps), kinds,...  0.87 us
  transfers between devices with their start and end apart: 19, of which 9 were waited for; matrix products, arithmetic and copies ran while one was open for 0% of the time, Pallas kernels for 16%

profile of v3, /device:TPU:0, one launch (start us, length us, event | category | flops | bytes accessed | tf_op | source)
XLA Modules:
  0.0 41.1 jit_solution(9040949391015208252)
XLA Ops:
  0.6 0.0 copy-start.1
  0.6 0.9 %copy-done.1 = bf16[8,64,64]{2,1,0:T(8,128)(2,1)S(1)} copy-done((bf16[8,64,64]{2,1,0:T(8,128)(2,1)S(1)}, bf16[8,64,64]{2,1,0:T(8,128)(2,1)}, u32[]{:S(2)}) %copy-start.1) | copy-done | bytes 65560
  1.5 0.1 pack_weight.1
  1.6 3.1 %collective-permute-start.2 = (bf16[4,64,128]{2,1,0:T(8,128)(2,1)S(1)}, bf16[4,64,128]{2,1,0:T(8,128)(2,1)S(1)}, u32[]{:S(2)}, u32[]{:S(2)}) collective-permute-start(bf16[4,64,128]{2,1,0:T(8,128)(2,1)S(1)} %get-tuple-element.27), channel_id=1, source_target_pairs={{0,1},{1,0},{2,3},{3,2},{4,5},{5,4},{6,7},{7,6},{8,9},{9,8},{10,11... | collective-permute-start | bytes 196616 | tf_op jit(solution)/shard_map/ppermute | solution.py:21
  4.7 2.6 %collective-permute-start = (bf16[4,64,128]{2,1,0:T(8,128)(2,1)S(1)}, bf16[4,64,128]{2,1,0:T(8,128)(2,1)S(1)}, u32[]{:S(2)}, u32[]{:S(2)}) collective-permute-start(bf16[4,64,128]{2,1,0:T(8,128)(2,1)S(1)} %get-tuple-element.26.refs_0_), channel_id=1, source_target_pairs={{0,2},{1,3},{2,0},{3,1},{4,6},{5,7},{6,4},{7,5},{8,10},{9,11},{10,... | collective-permute-start | bytes 196616 | tf_op jit(solution)/shard_map/ppermute | solution.py:21
  7.3 0.0 collective-permute-start.1
  7.3 0.0 collective-permute-done.2.refs_1_
  7.4 0.0 copy-start
  7.4 0.9 %copy-done = bf16[2,8,128,64]{2,3,1,0:T(8,128)(2,1)S(1)} copy-done((bf16[2,8,128,64]{2,3,1,0:T(8,128)(2,1)S(1)}, bf16[2,8,128,64]{2,3,1,0:T(8,128)(2,1)}, u32[]{:S(2)}) %copy-start) | copy-done | bytes 262168
  8.3 1.7 %collective-permute-start.3 = (bf16[4,64,128]{2,1,0:T(8,128)(2,1)S(1)}, bf16[4,64,128]{2,1,0:T(8,128)(2,1)S(1)}, u32[]{:S(2)}, u32[]{:S(2)}) collective-permute-start(bf16[4,64,128]{2,1,0:T(8,128)(2,1)S(1)} %get-tuple-element.30), channel_id=1, source_target_pairs={{0,1},{1,0},{2,3},{3,2},{4,5},{5,4},{6,7},{7,6},{8,9},{9,8},{10,11... | collective-permute-start | bytes 196616 | tf_op jit(solution)/shard_map/ppermute | solution.py:21
  10.1 3.2 %collective-permute-start.4 = (bf16[4,64,128]{2,1,0:T(8,128)(2,1)S(1)}, bf16[4,64,128]{2,1,0:T(8,128)(2,1)S(1)}, u32[]{:S(2)}, u32[]{:S(2)}) collective-permute-start(bf16[4,64,128]{2,1,0:T(8,128)(2,1)S(1)} %get-tuple-element.31), channel_id=1, source_target_pairs={{0,2},{1,3},{2,0},{3,1},{4,6},{5,7},{6,4},{7,5},{8,10},{9,11},{10,... | collective-permute-start | bytes 196616 | tf_op jit(solution)/shard_map/ppermute | solution.py:21
  13.3 0.0 collective-permute-start.5
  13.3 0.0 collective-permute-done.refs_0_
  13.3 1.5 %collective-permute-start.8 = (bf16[8,64,128]{2,1,0:T(8,128)(2,1)S(1)}, bf16[8,64,128]{2,1,0:T(8,128)(2,1)S(1)}, u32[]{:S(2)}, u32[]{:S(2)}) collective-permute-start(bf16[8,64,128]{2,1,0:T(8,128)(2,1)S(1)} %merge_tile.3.refs_0_.t_ref), channel_id=1, source_target_pairs={{0,8},{4,12},{8,0},{12,4},{1,9},{5,13},{9,1},{13,5},{2,10},{6,14},... | collective-permute-start | bytes 393224 | tf_op jit(solution)/shard_map/ppermute | solution.py:21
  14.8 0.0 collective-permute-done.1.refs_1_
  14.8 0.8 %collective-permute-start.9 = (bf16[8,64,128]{2,1,0:T(8,128)(2,1)S(1)}, bf16[8,64,128]{2,1,0:T(8,128)(2,1)S(1)}, u32[]{:S(2)}, u32[]{:S(2)}) collective-permute-start(bf16[8,64,128]{2,1,0:T(8,128)(2,1)S(1)} %merge_tile.2.refs_0_.t_ref.refs_1_), channel_id=1, source_target_pairs={{0,8},{4,12},{8,0},{12,4},{1,9},{5,13},{9,1},{13,5},{2,10},{6,14},... | collective-permute-start | bytes 393224 | tf_op jit(solution)/shard_map/ppermute | solution.py:21
  15.6 2.4 %patch_rows.1 = (bf16[8,512,256]{2,1,0:T(8,128)(2,1)S(1)}, bf16[8,256,512]{2,1,0:T(8,128)(2,1)S(1)}) custom-call(bf16[4,4,256,256]{3,2,1,0:T(8,128)(2,1)} %v_ref.1, bf16[8,64,128]{2,1,0:T(8,128)(2,1)S(1)} %merge_tile.2.refs_0_.t_ref.refs_1_), custom_call_target="tpu_custom_call" | custom-call | flops 536870912 | bytes 6291456 | tf_op jit(solution)/shard_map/patch_rows/pallas_call | solution.py:176
  18.0 0.0 collective-permute-done.3.refs_1_
  18.0 0.1 collective-permute-start.6
  18.1 0.0 collective-permute-done.4.refs_2_
  18.1 1.2 %collective-permute-done.5.refs_3_ = bf16[4,64,128]{2,1,0:T(8,128)(2,1)S(1)} collective-permute-done((bf16[4,64,128]{2,1,0:T(8,128)(2,1)S(1)}, bf16[4,64,128]{2,1,0:T(8,128)(2,1)S(1)}, u32[]{:S(2)}, u32[]{:S(2)}) %collective-permute-start.5) | collective-permute-done | bytes 65568 | tf_op jit(solution)/shard_map/ppermute | solution.py:21
  19.4 0.1 turn_cot.1.refs_0_.u_ref
  19.5 0.1 collective-permute-start.7
  19.6 0.3 collective-permute-done.9.refs_5_
  19.9 0.2 collective-permute-start.11
  20.1 0.0 collective-permute-done.8.refs_4_
  20.1 0.3 collective-permute-start.10
  20.4 0.0 collective-permute-done.6.refs_2_
  20.4 0.5 %collective-permute-done.7.refs_3_ = bf16[8,64,128]{2,1,0:T(8,128)(2,1)S(1)} collective-permute-done((bf16[8,64,128]{2,1,0:T(8,128)(2,1)S(1)}, bf16[8,64,128]{2,1,0:T(8,128)(2,1)S(1)}, u32[]{:S(2)}, u32[]{:S(2)}) %collective-permute-start.7) | collective-permute-done | bytes 131104 | tf_op jit(solution)/shard_map/ppermute | solution.py:21
  20.9 0.3 collective-permute-done.11.refs_7_
  21.2 0.2 collective-permute-done.10.refs_6_
  21.4 1.1 %forward.1 = (bf16[2,512,256]{2,1,0:T(8,128)(2,1)S(1)}, bf16[8,256,256]{2,1,0:T(8,128)(2,1)S(1)}) custom-call(bf16[8,512,256]{2,1,0:T(8,128)(2,1)S(1)} %get-tuple-element.28.refs_0_.p_ref, bf16[512,256]{1,0:T(8,128)(2,1)S(1)} %turn_cot.1.refs_0_.u_ref, bf16[8,64,128]{2,1,0:T(8,128)(2,1)S(1)} %merge_tile.3.refs_0_.t_ref, ...), custom_call_target="tpu_custom_call" | custom-call | flops 536870912 | bytes 2097152 | tf_op jit(solution)/shard_map/forward/pallas_call | solution.py:243
  22.5 0.4 %weight_part.3 = (bf16[2,8,64,128]{3,2,1,0:T(8,128)(2,1)S(1)}, bf16[2,8,64,128]{3,2,1,0:T(8,128)(2,1)S(1)}) custom-call(bf16[8,256,512]{2,1,0:T(8,128)(2,1)S(1)} %get-tuple-element.36.t_ref, bf16[2,512,256]{2,1,0:T(8,128)(2,1)S(1)} %get-tuple-element.33.d_ref), custom_call_target="tpu_custom_call" | custom-call | flops 268435456 | bytes 2097152 | tf_op jit(solution)/shard_map/weight_part/pallas_call | solution.py:273
  23.0 0.4 collective-permute-start.13
  23.3 0.2 collective-permute-start.12
  23.5 0.4 %weight_part.2 = (f32[2,8,64,128]{3,2,1,0:T(8,128)S(1)}, f32[2,8,64,128]{3,2,1,0:T(8,128)S(1)}) custom-call(bf16[8,256,512]{2,1,0:T(8,128)(2,1)S(1)} %get-tuple-element.36.t_ref, bf16[2,512,256]{2,1,0:T(8,128)(2,1)S(1)} %get-tuple-element.33.d_ref), custom_call_target="tpu_custom_call" | custom-call | flops 268435456 | bytes 2097152 | tf_op jit(solution)/shard_map/weight_part/pallas_call | solution.py:273
  24.0 0.6 %collective-permute-done.13.b_ref = bf16[2,8,64,128]{3,2,1,0:T(8,128)(2,1)S(1)} collective-permute-done((bf16[2,8,64,128]{3,2,1,0:T(8,128)(2,1)S(1)}, bf16[2,8,64,128]{3,2,1,0:T(8,128)(2,1)S(1)}, u32[]{:S(2)}, u32[]{:S(2)}) %collective-permute-start.13) | collective-permute-done | bytes 262176 | tf_op jit(solution)/shard_map/ppermute | solution.py:21
  24.6 1.6 %collective-permute-start.15 = (bf16[8,64,128]{2,1,0:T(8,128)(2,1)S(1)}, bf16[8,64,128]{2,1,0:T(8,128)(2,1)S(1)}, u32[]{:S(2)}, u32[]{:S(2)}) collective-permute-start(bf16[8,64,128]{2,1,0:T(8,128)(2,1)S(1)} %get-tuple-element.41.refs_0_), channel_id=1, source_target_pairs={{0,8},{4,12},{8,0},{12,4},{1,9},{5,13},{9,1},{13,5},{2,10},{6,14},... | collective-permute-start | bytes 393224 | tf_op jit(solution)/shard_map/ppermute | solution.py:21
  26.2 0.0 collective-permute-done.12.b_ref
  26.2 0.1 add_core_near.1
  26.3 0.5 %collective-permute-start.14 = (bf16[8,64,128]{2,1,0:T(8,128)(2,1)S(1)}, bf16[8,64,128]{2,1,0:T(8,128)(2,1)S(1)}, u32[]{:S(2)}, u32[]{:S(2)}) collective-permute-start(bf16[8,64,128]{2,1,0:T(8,128)(2,1)S(1)} %get-tuple-element.43), channel_id=1, source_target_pairs={{0,1},{1,0},{2,3},{3,2},{4,5},{5,4},{6,7},{7,6},{8,9},{9,8},{10,11... | collective-permute-start | bytes 393224 | tf_op jit(solution)/shard_map/ppermute | solution.py:21
  26.8 3.3 %volume_grad.1 = (bf16[4,4,256,256]{3,2,1,0:T(8,128)(2,1)}, f32[8,128]{1,0:T(8,128)S(1)}) custom-call(bf16[2,512,256]{2,1,0:T(8,128)(2,1)S(1)} %get-tuple-element.33.d_ref, bf16[8,256,256]{2,1,0:T(8,128)(2,1)S(1)} %get-tuple-element.34.w_ref), custom_call_target="tpu_custom_call" | custom-call | flops 1073741824 | bytes 2097152 | tf_op jit(solution)/shard_map/volume_grad/pallas_call | solution.py:438
  30.2 0.2 collective-permute-done.15.refs_1_
  30.4 0.1 add_and_pack.1
  30.5 3.6 %collective-permute-start.17 = (bf16[4,64,128]{2,1,0:T(8,128)(2,1)S(1)}, bf16[4,64,128]{2,1,0:T(8,128)(2,1)S(1)}, u32[]{:S(2)}, u32[]{:S(2)}) collective-permute-start(bf16[4,64,128]{2,1,0:T(8,128)(2,1)S(1)} %get-tuple-element.49), channel_id=1, source_target_pairs={{0,2},{1,3},{2,0},{3,1},{4,6},{5,7},{6,4},{7,5},{8,10},{9,11},{10,... | collective-permute-start | bytes 196616 | tf_op jit(solution)/shard_map/ppermute | solution.py:21
  34.1 0.4 collective-permute-start.18
  34.5 0.0 collective-permute-done.14.refs_1_
  34.5 1.4 %collective-permute-start.16 = (bf16[4,64,128]{2,1,0:T(8,128)(2,1)S(1)}, bf16[4,64,128]{2,1,0:T(8,128)(2,1)S(1)}, u32[]{:S(2)}, u32[]{:S(2)}) collective-permute-start(bf16[4,64,128]{2,1,0:T(8,128)(2,1)S(1)} %get-tuple-element.48), channel_id=1, source_target_pairs={{0,8},{4,12},{8,0},{12,4},{1,9},{5,13},{9,1},{13,5},{2,10},{6,14},... | collective-permute-start | bytes 196616 | tf_op jit(solution)/shard_map/ppermute | solution.py:21
  35.9 1.9 %collective-permute-done.17.refs_0_ = bf16[4,64,128]{2,1,0:T(8,128)(2,1)S(1)} collective-permute-done((bf16[4,64,128]{2,1,0:T(8,128)(2,1)S(1)}, bf16[4,64,128]{2,1,0:T(8,128)(2,1)S(1)}, u32[]{:S(2)}, u32[]{:S(2)}) %collective-permute-start.17) | collective-permute-done | bytes 65568 | tf_op jit(solution)/shard_map/ppermute | solution.py:21
  37.7 2.5 %collective-permute-done.18.refs_1_ = bf16[4,64,128]{2,1,0:T(8,128)(2,1)S(1)} collective-permute-done((bf16[4,64,128]{2,1,0:T(8,128)(2,1)S(1)}, bf16[4,64,128]{2,1,0:T(8,128)(2,1)S(1)}, u32[]{:S(2)}, u32[]{:S(2)}) %collective-permute-start.18) | collective-permute-done | bytes 65568 | tf_op jit(solution)/shard_map/ppermute | solution.py:21
  40.3 0.0 collective-permute-done.16.refs_1_
  40.3 0.8 %finish.1 = f32[8,64,64]{2,1,0:T(8,128)} custom-call(f32[4,64,128]{2,1,0:T(8,128)S(1)} %get-tuple-element.47.refs_0_, bf16[4,64,128]{2,1,0:T(8,128)(2,1)S(1)} %collective-permute-done.16.refs_1_, f32[4,64,128]{2,1,0:T(8,128)S(1)} %fold.1.refs_2_), custom_call_target="tpu_custom_call" | custom-call | tf_op jit(solution)/shard_map/finish/pallas_call | solution.py:404
  (8 shorter events, 0.2 us)
Async XLA Ops:
  0.6 0.9 %copy-start.1 = (bf16[8,64,64]{2,1,0:T(8,128)(2,1)S(1)}, bf16[8,64,64]{2,1,0:T(8,128)(2,1)}, u32[]{:S(2)}) copy-start(bf16[8,64,64]{2,1,0:T(8,128)(2,1)} %w_ref.1) | copy-start | bytes 196612
  1.6 5.7 %collective-permute-start.2 = (bf16[4,64,128]{2,1,0:T(8,128)(2,1)S(1)}, bf16[4,64,128]{2,1,0:T(8,128)(2,1)S(1)}, u32[]{:S(2)}, u32[]{:S(2)}) collective-permute-start(bf16[4,64,128]{2,1,0:T(8,128)(2,1)S(1)} %get-tuple-element.27), channel_id=1, source_target_pairs={{0,1},{1,0},{2,3},{3,2},{4,5},{5,4},{6,7},{7,6},{8,9},{9,8},{10,11... | collective-permute-start | bytes 196616 | tf_op jit(solution)/shard_map/ppermute | solution.py:21
  4.7 8.6 %collective-permute-start = (bf16[4,64,128]{2,1,0:T(8,128)(2,1)S(1)}, bf16[4,64,128]{2,1,0:T(8,128)(2,1)S(1)}, u32[]{:S(2)}, u32[]{:S(2)}) collective-permute-start(bf16[4,64,128]{2,1,0:T(8,128)(2,1)S(1)} %get-tuple-element.26.refs_0_), channel_id=1, source_target_pairs={{0,2},{1,3},{2,0},{3,1},{4,6},{5,7},{6,4},{7,5},{8,10},{9,11},{10,... | collective-permute-start | bytes 196616 | tf_op jit(solution)/shard_map/ppermute | solution.py:21
  7.3 7.5 %collective-permute-start.1 = (bf16[4,64,128]{2,1,0:T(8,128)(2,1)S(1)}, bf16[4,64,128]{2,1,0:T(8,128)(2,1)S(1)}, u32[]{:S(2)}, u32[]{:S(2)}) collective-permute-start(bf16[4,64,128]{2,1,0:T(8,128)(2,1)S(1)} %get-tuple-element.27), channel_id=1, source_target_pairs={{0,3},{1,2},{2,1},{3,0},{4,7},{5,6},{6,5},{7,4},{8,11},{9,10},{10,... | collective-permute-start | bytes 196616 | tf_op jit(solution)/shard_map/ppermute | solution.py:21
  7.4 1.0 %copy-start = (bf16[2,8,128,64]{2,3,1,0:T(8,128)(2,1)S(1)}, bf16[2,8,128,64]{2,3,1,0:T(8,128)(2,1)}, u32[]{:S(2)}) copy-start(bf16[2,8,128,64]{2,3,1,0:T(8,128)(2,1)} %param.5) | copy-start | bytes 786436
  8.3 9.7 %collective-permute-start.3 = (bf16[4,64,128]{2,1,0:T(8,128)(2,1)S(1)}, bf16[4,64,128]{2,1,0:T(8,128)(2,1)S(1)}, u32[]{:S(2)}, u32[]{:S(2)}) collective-permute-start(bf16[4,64,128]{2,1,0:T(8,128)(2,1)S(1)} %get-tuple-element.30), channel_id=1, source_target_pairs={{0,1},{1,0},{2,3},{3,2},{4,5},{5,4},{6,7},{7,6},{8,9},{9,8},{10,11... | collective-permute-start | bytes 196616 | tf_op jit(solution)/shard_map/ppermute | solution.py:21
  10.1 8.1 %collective-permute-start.4 = (bf16[4,64,128]{2,1,0:T(8,128)(2,1)S(1)}, bf16[4,64,128]{2,1,0:T(8,128)(2,1)S(1)}, u32[]{:S(2)}, u32[]{:S(2)}) collective-permute-start(bf16[4,64,128]{2,1,0:T(8,128)(2,1)S(1)} %get-tuple-element.31), channel_id=1, source_target_pairs={{0,2},{1,3},{2,0},{3,1},{4,6},{5,7},{6,4},{7,5},{8,10},{9,11},{10,... | collective-permute-start | bytes 196616 | tf_op jit(solution)/shard_map/ppermute | solution.py:21
  13.3 6.1 %collective-permute-start.5 = (bf16[4,64,128]{2,1,0:T(8,128)(2,1)S(1)}, bf16[4,64,128]{2,1,0:T(8,128)(2,1)S(1)}, u32[]{:S(2)}, u32[]{:S(2)}) collective-permute-start(bf16[4,64,128]{2,1,0:T(8,128)(2,1)S(1)} %get-tuple-element.32), channel_id=1, source_target_pairs={{0,3},{1,2},{2,1},{3,0},{4,7},{5,6},{6,5},{7,4},{8,11},{9,10},{10,... | collective-permute-start | bytes 196616 | tf_op jit(solution)/shard_map/ppermute | solution.py:21
  13.3 6.8 %collective-permute-start.8 = (bf16[8,64,128]{2,1,0:T(8,128)(2,1)S(1)}, bf16[8,64,128]{2,1,0:T(8,128)(2,1)S(1)}, u32[]{:S(2)}, u32[]{:S(2)}) collective-permute-start(bf16[8,64,128]{2,1,0:T(8,128)(2,1)S(1)} %merge_tile.3.refs_0_.t_ref), channel_id=1, source_target_pairs={{0,8},{4,12},{8,0},{12,4},{1,9},{5,13},{9,1},{13,5},{2,10},{6,14},... | collective-permute-start | bytes 393224 | tf_op jit(solution)/shard_map/ppermute | solution.py:21
  14.8 5.0 %collective-permute-start.9 = (bf16[8,64,128]{2,1,0:T(8,128)(2,1)S(1)}, bf16[8,64,128]{2,1,0:T(8,128)(2,1)S(1)}, u32[]{:S(2)}, u32[]{:S(2)}) collective-permute-start(bf16[8,64,128]{2,1,0:T(8,128)(2,1)S(1)} %merge_tile.2.refs_0_.t_ref.refs_1_), channel_id=1, source_target_pairs={{0,8},{4,12},{8,0},{12,4},{1,9},{5,13},{9,1},{13,5},{2,10},{6,14},... | collective-permute-start | bytes 393224 | tf_op jit(solution)/shard_map/ppermute | solution.py:21
  18.0 2.3 %collective-permute-start.6 = (bf16[8,64,128]{2,1,0:T(8,128)(2,1)S(1)}, bf16[8,64,128]{2,1,0:T(8,128)(2,1)S(1)}, u32[]{:S(2)}, u32[]{:S(2)}) collective-permute-start(bf16[8,64,128]{2,1,0:T(8,128)(2,1)S(1)} %gate.2), channel_id=1, source_target_pairs={{0,4},{4,0},{8,12},{12,8},{1,5},{5,1},{9,13},{13,9},{2,6},{6,2},{1... | collective-permute-start | bytes 393224 | tf_op jit(solution)/shard_map/ppermute | solution.py:21
  19.5 1.4 %collective-permute-start.7 = (bf16[8,64,128]{2,1,0:T(8,128)(2,1)S(1)}, bf16[8,64,128]{2,1,0:T(8,128)(2,1)S(1)}, u32[]{:S(2)}, u32[]{:S(2)}) collective-permute-start(bf16[8,64,128]{2,1,0:T(8,128)(2,1)S(1)} %gate.3), channel_id=1, source_target_pairs={{0,4},{4,0},{8,12},{12,8},{1,5},{5,1},{9,13},{13,9},{2,6},{6,2},{1... | collective-permute-start | bytes 393224 | tf_op jit(solution)/shard_map/ppermute | solution.py:21
  19.9 1.3 %collective-permute-start.11 = (bf16[8,64,128]{2,1,0:T(8,128)(2,1)S(1)}, bf16[8,64,128]{2,1,0:T(8,128)(2,1)S(1)}, u32[]{:S(2)}, u32[]{:S(2)}) collective-permute-start(bf16[8,64,128]{2,1,0:T(8,128)(2,1)S(1)} %collective-permute-done.9.refs_5_), channel_id=1, source_target_pairs={{0,4},{4,0},{8,12},{12,8},{1,5},{5,1},{9,13},{13,9},{2,6},{6,2},{1... | collective-permute-start | bytes 393224 | tf_op jit(solution)/shard_map/ppermute | solution.py:21
  20.1 1.3 %collective-permute-start.10 = (bf16[8,64,128]{2,1,0:T(8,128)(2,1)S(1)}, bf16[8,64,128]{2,1,0:T(8,128)(2,1)S(1)}, u32[]{:S(2)}, u32[]{:S(2)}) collective-permute-start(bf16[8,64,128]{2,1,0:T(8,128)(2,1)S(1)} %collective-permute-done.8.refs_4_), channel_id=1, source_target_pairs={{0,4},{4,0},{8,12},{12,8},{1,5},{5,1},{9,13},{13,9},{2,6},{6,2},{1... | collective-permute-start | bytes 393224 | tf_op jit(solution)/shard_map/ppermute | solution.py:21
  23.0 1.6 %collective-permute-start.13 = (bf16[2,8,64,128]{3,2,1,0:T(8,128)(2,1)S(1)}, bf16[2,8,64,128]{3,2,1,0:T(8,128)(2,1)S(1)}, u32[]{:S(2)}, u32[]{:S(2)}) collective-permute-start(bf16[2,8,64,128]{3,2,1,0:T(8,128)(2,1)S(1)} %get-tuple-element.40), channel_id=1, source_target_pairs={{0,4},{4,0},{8,12},{12,8},{1,5},{5,1},{9,13},{13,9},{2,6},{6,2},{1... | collective-permute-start | bytes 786440 | tf_op jit(solution)/shard_map/ppermute | solution.py:21
  23.3 2.9 %collective-permute-start.12 = (bf16[2,8,64,128]{3,2,1,0:T(8,128)(2,1)S(1)}, bf16[2,8,64,128]{3,2,1,0:T(8,128)(2,1)S(1)}, u32[]{:S(2)}, u32[]{:S(2)}) collective-permute-start(bf16[2,8,64,128]{3,2,1,0:T(8,128)(2,1)S(1)} %get-tuple-element.38), channel_id=1, source_target_pairs={{0,4},{4,0},{8,12},{12,8},{1,5},{5,1},{9,13},{13,9},{2,6},{6,2},{1... | collective-permute-start | bytes 786440 | tf_op jit(solution)/shard_map/ppermute | solution.py:21
  24.6 5.8 %collective-permute-start.15 = (bf16[8,64,128]{2,1,0:T(8,128)(2,1)S(1)}, bf16[8,64,128]{2,1,0:T(8,128)(2,1)S(1)}, u32[]{:S(2)}, u32[]{:S(2)}) collective-permute-start(bf16[8,64,128]{2,1,0:T(8,128)(2,1)S(1)} %get-tuple-element.41.refs_0_), channel_id=1, source_target_pairs={{0,8},{4,12},{8,0},{12,4},{1,9},{5,13},{9,1},{13,5},{2,10},{6,14},... | collective-permute-start | bytes 393224 | tf_op jit(solution)/shard_map/ppermute | solution.py:21
  26.3 8.1 %collective-permute-start.14 = (bf16[8,64,128]{2,1,0:T(8,128)(2,1)S(1)}, bf16[8,64,128]{2,1,0:T(8,128)(2,1)S(1)}, u32[]{:S(2)}, u32[]{:S(2)}) collective-permute-start(bf16[8,64,128]{2,1,0:T(8,128)(2,1)S(1)} %get-tuple-element.43), channel_id=1, source_target_pairs={{0,1},{1,0},{2,3},{3,2},{4,5},{5,4},{6,7},{7,6},{8,9},{9,8},{10,11... | collective-permute-start | bytes 393224 | tf_op jit(solution)/shard_map/ppermute | solution.py:21
  30.5 7.2 %collective-permute-start.17 = (bf16[4,64,128]{2,1,0:T(8,128)(2,1)S(1)}, bf16[4,64,128]{2,1,0:T(8,128)(2,1)S(1)}, u32[]{:S(2)}, u32[]{:S(2)}) collective-permute-start(bf16[4,64,128]{2,1,0:T(8,128)(2,1)S(1)} %get-tuple-element.49), channel_id=1, source_target_pairs={{0,2},{1,3},{2,0},{3,1},{4,6},{5,7},{6,4},{7,5},{8,10},{9,11},{10,... | collective-permute-start | bytes 196616 | tf_op jit(solution)/shard_map/ppermute | solution.py:21
  34.1 6.2 %collective-permute-start.18 = (bf16[4,64,128]{2,1,0:T(8,128)(2,1)S(1)}, bf16[4,64,128]{2,1,0:T(8,128)(2,1)S(1)}, u32[]{:S(2)}, u32[]{:S(2)}) collective-permute-start(bf16[4,64,128]{2,1,0:T(8,128)(2,1)S(1)} %get-tuple-element.46.refs_2_), channel_id=1, source_target_pairs={{0,3},{1,2},{2,1},{3,0},{4,7},{5,6},{6,5},{7,4},{8,11},{9,10},{10,... | collective-permute-start | bytes 196616 | tf_op jit(solution)/shard_map/ppermute | solution.py:21
  34.5 5.8 %collective-permute-start.16 = (bf16[4,64,128]{2,1,0:T(8,128)(2,1)S(1)}, bf16[4,64,128]{2,1,0:T(8,128)(2,1)S(1)}, u32[]{:S(2)}, u32[]{:S(2)}) collective-permute-start(bf16[4,64,128]{2,1,0:T(8,128)(2,1)S(1)} %get-tuple-element.48), channel_id=1, source_target_pairs={{0,8},{4,12},{8,0},{12,4},{1,9},{5,13},{9,1},{13,5},{2,10},{6,14},... | collective-permute-start | bytes 196616 | tf_op jit(solution)/shard_map/ppermute | solution.py:21

commit v4 on v3

--- a/solution.py
+++ b/solution.py
@@ -205,31 +205,88 @@
     )(*cots)
 
 
-def forward(patches, lines, upstream, width, ratio):
+def place(w_ref, ins, me, first, tiles):
+    kinds, block, lanes = ins[0].shape
+    for n in range(len(ins) // tiles):
+        at = pl.multiple_of(other(me, first + n) * block, block)
+        for t in range(tiles):
+            for k in range(kinds):
+                w_ref[k, pl.ds(at, block), t * lanes:(t + 1) * lanes] = ins[n * tiles + t][k]
+
+
+def chip_part(p_ref, w_ref, here, me, chip, block, ratio, q):
+    kinds = w_ref.shape[0]
+    span = 2 * block
+    at = pl.multiple_of(other(me, chip) // 2 * span, span)
+    ks = range(q, kinds, ratio)
+    per = max(1, min(len(ks), w_ref.shape[1] // span))
+    acc = None
+    for first in range(0, len(ks), per):
+        some = ks[first:first + per]
+        left = jnp.concatenate([p_ref[k, here, pl.ds(at, span)] for k in some], axis=1)
+        right = jnp.concatenate([w_ref[k, pl.ds(at, span)] for k in some], axis=0)
+        part = jnp.dot(left, right, preferred_element_type=F32)
+        acc = part if acc is None else acc + part
+    return acc
+
+
+def forward_own(patches, lines, spaces, width, ratio):
     kinds, rows, in_chan = patches.shape
     _, block, lanes = lines[0][0].shape
-    spaces, lane_tiles = len(lines), len(lines[0])
-    out_chan = lane_tiles * lanes
+    tiles = len(lines[0])
+    out_chan = tiles * lanes
     flat = [tile for line in lines for tile in line]
 
+    def body(p_ref, *refs):
+        pre_ref, w_ref = refs[-2:]
+        me = lax.axis_index("space")
+        place(w_ref, refs[:-2], me, 0, tiles)
+        for first in range(0, rows, rows // 2):
+            here = slice(first, first + rows // 2)
+            pre = None
+            for q in range(ratio):
+                acc = swap_groups(chip_part(p_ref, w_ref, here, me, 0, block, ratio, q), width, q)
+                pre = acc if pre is None else pre + acc
+            pre_ref[here] = pre
+
+    return pl.pallas_call(
+        body,
+        out_shape=[
+            jax.ShapeDtypeStruct((rows, out_chan), F32),
+            jax.ShapeDtypeStruct((kinds, in_chan, out_chan), BF16),
+        ],
+        compiler_params=params(),
+        cost_estimate=cost(4 * patches.size * out_chan // spaces, 2 * patches.size),
+        name="forward_own",
+    )(patches, *flat)
+
+
+def forward(patches, own, lines, upstream, width, ratio):
+    kinds, rows, in_chan = patches.shape
+    tiles = len(lines[0])
+    _, block, lanes = lines[0][0].shape
+    out_chan = tiles * lanes
+    spaces = len(lines)
+    start = 0 if own is None else 2
+    flat = [tile for line in lines[start:] for tile in line]
+
     def body(p_ref, u_ref, *refs):
-        ins = refs[:len(flat)]
         d_ref, w_ref = refs[-2:]
         me = lax.axis_index("space")
-        for j in range(spaces):
-            at = pl.multiple_of(other(me, j) * block, block)
-            for t in range(lane_tiles):
-                for k in range(kinds):
-                    w_ref[k, pl.ds(at, block), t * lanes:(t + 1) * lanes] = ins[j * lane_tiles + t][k]
-        part_rows = rows // 2
-        for first in range(0, rows, part_rows):
-            here = slice(first, first + part_rows)
-            pre = None
+        place(w_ref, refs[:len(flat)], me, start, tiles)
+        for first in range(0, rows, rows // 2):
+            here = slice(first, first + rows // 2)
+            pre = None if own is None else refs[len(flat)][here]
             for q in range(ratio):
                 acc = None
-                for k in range(q, kinds, ratio):
-                    part = jnp.dot(p_ref[k, here], w_ref[k], preferred_element_type=F32)
-                    acc = part if acc is None else acc + part
+                if own is None:
+                    for k in range(q, kinds, ratio):
+                        part = jnp.dot(p_ref[k, here], w_ref[k], preferred_element_type=F32)
+                        acc = part if acc is None else acc + part
+                else:
+                    for chip in range(start, spaces, 2):
+                        part = chip_part(p_ref, w_ref, here, me, chip, block, ratio, q)
+                        acc = part if acc is None else acc + part
                 acc = swap_groups(acc, width, q)
                 pre = acc if pre is None else pre + acc
             up = u_ref[here].astype(F32)
@@ -240,16 +297,18 @@
             for q in range(1, ratio):
                 d_ref[q, here] = swap_groups(delta.astype(F32), width, q).astype(BF16)
 
+    extra = () if own is None else own
     return pl.pallas_call(
         body,
         out_shape=[
             jax.ShapeDtypeStruct((ratio, rows, out_chan), BF16),
             jax.ShapeDtypeStruct((kinds, in_chan, out_chan), BF16),
         ],
+        input_output_aliases={} if own is None else {2 + len(flat) + 1: 1},
         compiler_params=params(),
         cost_estimate=cost(2 * patches.size * out_chan, 2 * patches.size),
         name="forward",
-    )(patches, upstream, *flat)
+    )(patches, upstream, *flat, *extra)
 
 
 def weight_part(turned, deltas, steps, spaces, lanes, dtype):
@@ -413,37 +472,50 @@
     cells_x, cells_y, cells_z, in_chan = shape
     nx, ny, nz = cells_x // 2, cells_y // 2, cells_z // 2
     ratio, rows, out_chan = deltas.shape
-
-    def body(d_ref, w_ref, o_ref, mark_ref):
+    planes = cells_x * cells_y
+
+    def body(d_ref, w_ref, o_hbm, mark_ref, wide_ref, plane_ref, sem):
         mark_ref[...] = jnp.zeros_like(mark_ref)
         row = lax.broadcasted_iota(jnp.int32, (cells_z, nz), 0)
         col = lax.broadcasted_iota(jnp.int32, (cells_z, nz), 1)
-        wide = {}
-        for k in range(8):
-            e, q = k % 2, k % ratio
-            if (e, q) not in wide:
-                put = (row == 2 * col + e).astype(F32).astype(BF16)
-                wide[e, q] = jnp.dot(put, d_ref[q], preferred_element_type=F32).astype(BF16)
+        places = sorted({(k % 2, k % ratio) for k in range(8)})
+        for n, (e, q) in enumerate(places):
+            put = (row == 2 * col + e).astype(F32).astype(BF16)
+            for m in range(nx * ny):
+                got = jnp.dot(put, d_ref[q, m * nz:(m + 1) * nz], preferred_element_type=F32)
+                wide_ref[n, m * cells_z:(m + 1) * cells_z] = got.astype(BF16)
+        moves = []
         for a in range(2):
             for b in range(2):
                 acc = None
                 for e in range(2):
                     k = 4 * a + 2 * b + e
                     part = lax.dot_general(
-                        wide[e, k % ratio], w_ref[k], (((1,), (1,)), ((), ())), preferred_element_type=F32
+                        wide_ref[places.index((e, k % ratio))], w_ref[k], (((1,), (1,)), ((), ())),
+                        preferred_element_type=F32,
                     )
                     acc = part if acc is None else acc + part
-                o_ref[a, b] = acc.astype(BF16)
-
-    return pl.pallas_call(
-        body,
-        grid=(nx * ny,),
-        in_specs=[pl.BlockSpec((ratio, nz, out_chan), lambda n: (0, n, 0)), whole(weights)],
-        out_specs=[
-            pl.BlockSpec((2, 2, cells_z, in_chan), lambda n: (n // ny, n % ny, 0, 0)),
-            pl.BlockSpec((8, LANES), lambda n: (0, 0)),
+                out = acc.astype(BF16)
+                for m in range(nx * ny):
+                    x, y = 2 * (m // ny) + a, 2 * (m % ny) + b
+                    at = len(moves)
+                    plane_ref[at] = out[m * cells_z:(m + 1) * cells_z]
+                    move = pltpu.make_async_copy(plane_ref.at[at], o_hbm.at[x, y], sem.at[at])
+                    move.start()
+                    moves.append(move)
+        for move in moves:
+            move.wait()
+
+    return pl.pallas_call(
+        body,
+        in_specs=[pl.BlockSpec(memory_space=pltpu.VMEM)] * 2,
+        out_specs=[pl.BlockSpec(memory_space=pl.ANY), pl.BlockSpec(memory_space=pltpu.VMEM)],
+        out_shape=[jax.ShapeDtypeStruct(shape, BF16), jax.ShapeDtypeStruct((8, LANES), F32)],
+        scratch_shapes=[
+            pltpu.VMEM((max(2, ratio), 4 * rows // 2, out_chan), BF16),
+            pltpu.VMEM((planes, cells_z, in_chan), BF16),
+            pltpu.SemaphoreType.DMA((planes,)),
         ],
-        out_shape=[jax.ShapeDtypeStruct(shape, BF16), jax.ShapeDtypeStruct((8, LANES), F32)],
         compiler_params=params(),
         cost_estimate=cost(32 * rows * in_chan * out_chan, 2 * rows * 8 * in_chan),
         name="volume_grad",
@@ -469,8 +541,11 @@
     lines = []
     for j in range(0, spaces, 2):
         lines.append([fetch(tile, "space", pairs(spaces, j)) for tile in own] if j else own)
-        lines.append([fetch(gate(tile, (upstream,)) if not j and t else gate(tile, (patches,)) if not j else tile, "space", pairs(spaces, 1)) for t, tile in enumerate(lines[-1])])
-    deltas, weights = forward(patches, lines, upstream, width, ratio)
+        lines.append([fetch(gate(tile, (patches,)) if not j and not t else gate(tile, (patches,)) if not j else gate(tile, (upstream,)) if not t else gate(tile, (upstream,)), "space", pairs(spaces, 1)) for t, tile in enumerate(lines[-1])])
+    own_part = None
+    if 2 * block % LANES == 0 and spaces > 2:
+        own_part = forward_own(patches, lines[:2], spaces, width, ratio)
+    deltas, weights = forward(patches, own_part, lines, upstream, width, ratio)
     steps = list(range(0, spaces, 2))
     lanes = ratio * width
     away = weight_part(turned, deltas, [s + 1 for s in steps], spaces, lanes, BF16)

time: 41.3 us -> 39.9 us (0.966)
  waiting for transfers between devices: 7.74 us -> 6.66 us
  Pallas kernels: 9.12 us -> 8.63 us
    ppermute x19, waiting for transfers between devices: 7.74 us -> 6.66 us  [fetch(): return lax.ppermute(x, axis, pairs)]
    pallas_call x1 -> x2, Pallas kernels: 3.35 us -> 3.12 us  [the longest x1 2.52 us: volume_grad(): pl.pallas_call(body, in_specs=[pl.BlockSpec(memory_space=pltpu.VMEM)] * 2...]
  transfers between devices with their start and end apart: 19 -> 19, of which waited for: 9 -> 8; matrix products, arithmetic and copies ran while one was open for 0% -> 0% of each run, Pallas kernels for 16% -> 16%
where the time goes in v4:
time: 39.9 us; the launch traced here: 39.8 us
  starting transfers between devices  21.8 us (55%)
  Pallas kernels  8.63 us (22%)
  waiting for transfers between devices  6.66 us (17%)
  local copies, waits for them, and re-layouts  1.84 us (5%)
  between operations  0.81 us (2%)
    ppermute x19, starting transfers between devices, fetch(): return lax.ppermute(x, axis, pairs)  21.8 us
    ppermute x19, waiting for transfers between devices, fetch(): return lax.ppermute(x, axis, pairs)  6.66 us
    pallas_call x1, Pallas kernels, volume_grad(): pl.pallas_call(body, in_specs=[pl.BlockSpec(memory_space=pltpu.VMEM)] * 2...  2.52 us
    pallas_call x1, Pallas kernels, patch_rows(): pl.pallas_call(body, in_specs=[pl.BlockSpec(memory_space=pltpu.VMEM)] + [...  2.37 us
    unnamed x4, local copies, waits for them, and re-layouts  1.84 us
    pallas_call x2, Pallas kernels, weight_part(): pl.pallas_call(body, out_shape=[jax.ShapeDtypeStruct((len(steps), kinds,...  0.87 us
    pallas_call x1, Pallas kernels, finish(): pl.pallas_call(body, out_shape=jax.ShapeDtypeStruct((kinds, block, width)...  0.81 us
  transfers between devices with their start and end apart: 19, of which 8 were waited for; matrix products, arithmetic and copies ran while one was open for 0% of the time, Pallas kernels for 16%

profile of v4, /device:TPU:0, one launch (start us, length us, event | category | flops | bytes accessed | tf_op | source)
XLA Modules:
  0.0 39.8 jit_solution(13830985549588681968)
XLA Ops:
  0.6 0.0 copy-start.1
  0.6 0.9 %copy-done.1 = bf16[8,64,64]{2,1,0:T(8,128)(2,1)S(1)} copy-done((bf16[8,64,64]{2,1,0:T(8,128)(2,1)S(1)}, bf16[8,64,64]{2,1,0:T(8,128)(2,1)}, u32[]{:S(2)}) %copy-start.1) | copy-done | bytes 65560
  1.5 0.1 pack_weight.1
  1.6 3.1 %collective-permute-start.2 = (bf16[4,64,128]{2,1,0:T(8,128)(2,1)S(1)}, bf16[4,64,128]{2,1,0:T(8,128)(2,1)S(1)}, u32[]{:S(2)}, u32[]{:S(2)}) collective-permute-start(bf16[4,64,128]{2,1,0:T(8,128)(2,1)S(1)} %get-tuple-element.29), channel_id=1, source_target_pairs={{0,1},{1,0},{2,3},{3,2},{4,5},{5,4},{6,7},{7,6},{8,9},{9,8},{10,11... | collective-permute-start | bytes 196616 | tf_op jit(solution)/shard_map/ppermute | solution.py:21
  4.7 2.6 %collective-permute-start = (bf16[4,64,128]{2,1,0:T(8,128)(2,1)S(1)}, bf16[4,64,128]{2,1,0:T(8,128)(2,1)S(1)}, u32[]{:S(2)}, u32[]{:S(2)}) collective-permute-start(bf16[4,64,128]{2,1,0:T(8,128)(2,1)S(1)} %get-tuple-element.28.refs_0_), channel_id=1, source_target_pairs={{0,2},{1,3},{2,0},{3,1},{4,6},{5,7},{6,4},{7,5},{8,10},{9,11},{10,... | collective-permute-start | bytes 196616 | tf_op jit(solution)/shard_map/ppermute | solution.py:21
  7.3 0.0 collective-permute-start.1
  7.3 0.0 collective-permute-done.2.refs_1_
  7.4 0.0 copy-start
  7.4 0.9 %copy-done = bf16[2,8,128,64]{2,3,1,0:T(8,128)(2,1)S(1)} copy-done((bf16[2,8,128,64]{2,3,1,0:T(8,128)(2,1)S(1)}, bf16[2,8,128,64]{2,3,1,0:T(8,128)(2,1)}, u32[]{:S(2)}) %copy-start) | copy-done | bytes 262168
  8.3 1.7 %collective-permute-start.3 = (bf16[4,64,128]{2,1,0:T(8,128)(2,1)S(1)}, bf16[4,64,128]{2,1,0:T(8,128)(2,1)S(1)}, u32[]{:S(2)}, u32[]{:S(2)}) collective-permute-start(bf16[4,64,128]{2,1,0:T(8,128)(2,1)S(1)} %get-tuple-element.32), channel_id=1, source_target_pairs={{0,1},{1,0},{2,3},{3,2},{4,5},{5,4},{6,7},{7,6},{8,9},{9,8},{10,11... | collective-permute-start | bytes 196616 | tf_op jit(solution)/shard_map/ppermute | solution.py:21
  10.1 3.2 %collective-permute-start.4 = (bf16[4,64,128]{2,1,0:T(8,128)(2,1)S(1)}, bf16[4,64,128]{2,1,0:T(8,128)(2,1)S(1)}, u32[]{:S(2)}, u32[]{:S(2)}) collective-permute-start(bf16[4,64,128]{2,1,0:T(8,128)(2,1)S(1)} %get-tuple-element.33), channel_id=1, source_target_pairs={{0,2},{1,3},{2,0},{3,1},{4,6},{5,7},{6,4},{7,5},{8,10},{9,11},{10,... | collective-permute-start | bytes 196616 | tf_op jit(solution)/shard_map/ppermute | solution.py:21
  13.3 0.0 collective-permute-start.5
  13.3 0.0 collective-permute-done.refs_0_
  13.3 1.5 %collective-permute-start.6 = (bf16[8,64,128]{2,1,0:T(8,128)(2,1)S(1)}, bf16[8,64,128]{2,1,0:T(8,128)(2,1)S(1)}, u32[]{:S(2)}, u32[]{:S(2)}) collective-permute-start(bf16[8,64,128]{2,1,0:T(8,128)(2,1)S(1)} %merge_tile.3.refs_0_.t_ref), channel_id=1, source_target_pairs={{0,8},{4,12},{8,0},{12,4},{1,9},{5,13},{9,1},{13,5},{2,10},{6,14},... | collective-permute-start | bytes 393224 | tf_op jit(solution)/shard_map/ppermute | solution.py:21
  14.8 0.0 collective-permute-done.1.refs_1_
  14.8 0.8 %collective-permute-start.7 = (bf16[8,64,128]{2,1,0:T(8,128)(2,1)S(1)}, bf16[8,64,128]{2,1,0:T(8,128)(2,1)S(1)}, u32[]{:S(2)}, u32[]{:S(2)}) collective-permute-start(bf16[8,64,128]{2,1,0:T(8,128)(2,1)S(1)} %merge_tile.2.refs_0_.t_ref.refs_1_), channel_id=1, source_target_pairs={{0,8},{4,12},{8,0},{12,4},{1,9},{5,13},{9,1},{13,5},{2,10},{6,14},... | collective-permute-start | bytes 393224 | tf_op jit(solution)/shard_map/ppermute | solution.py:21
  15.6 2.4 %patch_rows.1 = (bf16[8,512,256]{2,1,0:T(8,128)(2,1)S(1)}, bf16[8,256,512]{2,1,0:T(8,128)(2,1)S(1)}) custom-call(bf16[4,4,256,256]{3,2,1,0:T(8,128)(2,1)} %v_ref.1, bf16[8,64,128]{2,1,0:T(8,128)(2,1)S(1)} %merge_tile.2.refs_0_.t_ref.refs_1_), custom_call_target="tpu_custom_call" | custom-call | flops 536870912 | bytes 6291456 | tf_op jit(solution)/shard_map/patch_rows/pallas_call | solution.py:176
  18.1 0.0 collective-permute-done.3.refs_1_
  18.1 0.1 collective-permute-start.10
  18.1 0.0 collective-permute-done.4.refs_2_
  18.2 0.5 %collective-permute-start.11 = (bf16[8,64,128]{2,1,0:T(8,128)(2,1)S(1)}, bf16[8,64,128]{2,1,0:T(8,128)(2,1)S(1)}, u32[]{:S(2)}, u32[]{:S(2)}) collective-permute-start(bf16[8,64,128]{2,1,0:T(8,128)(2,1)S(1)} %gate.7), channel_id=1, source_target_pairs={{0,4},{4,0},{8,12},{12,8},{1,5},{5,1},{9,13},{13,9},{2,6},{6,2},{1... | collective-permute-start | bytes 393224 | tf_op jit(solution)/shard_map/ppermute | solution.py:21
  18.6 0.7 %collective-permute-done.5.refs_3_ = bf16[4,64,128]{2,1,0:T(8,128)(2,1)S(1)} collective-permute-done((bf16[4,64,128]{2,1,0:T(8,128)(2,1)S(1)}, bf16[4,64,128]{2,1,0:T(8,128)(2,1)S(1)}, u32[]{:S(2)}, u32[]{:S(2)}) %collective-permute-start.5) | collective-permute-done | bytes 65568 | tf_op jit(solution)/shard_map/ppermute | solution.py:21
  19.4 0.1 turn_cot.1.refs_0_.u_ref
  19.5 0.0 collective-permute-done.6.t_ref.refs_0_
  19.5 0.1 collective-permute-start.8
  19.6 0.3 collective-permute-done.7.t_ref.refs_1_
  19.9 0.3 collective-permute-start.9
  20.2 0.0 collective-permute-done.10.refs_2_
  20.2 0.0 collective-permute-done.11.refs_3_
  20.2 0.6 %forward_own.1 = (f32[512,256]{1,0:T(8,128)S(1)}, bf16[8,256,256]{2,1,0:T(8,128)(2,1)S(1)}) custom-call(bf16[8,512,256]{2,1,0:T(8,128)(2,1)S(1)} %get-tuple-element.30.refs_0_.p_ref, bf16[8,64,128]{2,1,0:T(8,128)(2,1)S(1)} %merge_tile.3.refs_0_.t_ref, bf16[8,64,128]{2,1,0:T(8,128)(2,1)S(1)} %merge_tile.2.refs_0_.t_ref.refs_1_, ...), custom_call_target="tpu_custom_call" | custom-call | flops 268435456 | bytes 2097152 | tf_op jit(solution)/shard_map/forward_own/pallas_call | solution.py:252
  20.8 0.1 collective-permute-done.8.refs_2_
  20.9 0.4 collective-permute-done.9.refs_3_
  21.3 0.8 %forward.1 = (bf16[2,512,256]{2,1,0:T(8,128)(2,1)S(1)}, bf16[8,256,256]{2,1,0:T(8,128)(2,1)S(1)}) custom-call(bf16[8,512,256]{2,1,0:T(8,128)(2,1)S(1)} %get-tuple-element.30.refs_0_.p_ref, bf16[512,256]{1,0:T(8,128)(2,1)S(1)} %turn_cot.1.refs_0_.u_ref, bf16[8,64,128]{2,1,0:T(8,128)(2,1)S(1)} %collective-permute-done.6.t_ref.refs_0_, ...), custom_call_target="tpu_custom_call", output_to_operand_aliasing={{1}: (7, {})} | custom-call | flops 536870912 | bytes 2097152 | tf_op jit(solution)/shard_map/forward/pallas_call | solution.py:301
  22.1 0.4 %weight_part.3 = (bf16[2,8,64,128]{3,2,1,0:T(8,128)(2,1)S(1)}, bf16[2,8,64,128]{3,2,1,0:T(8,128)(2,1)S(1)}) custom-call(bf16[8,256,512]{2,1,0:T(8,128)(2,1)S(1)} %get-tuple-element.40.t_ref, bf16[2,512,256]{2,1,0:T(8,128)(2,1)S(1)} %get-tuple-element.37.d_ref), custom_call_target="tpu_custom_call" | custom-call | flops 268435456 | bytes 2097152 | tf_op jit(solution)/shard_map/weight_part/pallas_call | solution.py:332
  22.5 0.3 collective-permute-start.13
  22.8 0.3 collective-permute-start.12
  23.1 0.4 %weight_part.2 = (f32[2,8,64,128]{3,2,1,0:T(8,128)S(1)}, f32[2,8,64,128]{3,2,1,0:T(8,128)S(1)}) custom-call(bf16[8,256,512]{2,1,0:T(8,128)(2,1)S(1)} %get-tuple-element.40.t_ref, bf16[2,512,256]{2,1,0:T(8,128)(2,1)S(1)} %get-tuple-element.37.d_ref), custom_call_target="tpu_custom_call" | custom-call | flops 268435456 | bytes 2097152 | tf_op jit(solution)/shard_map/weight_part/pallas_call | solution.py:332
  23.5 0.6 %collective-permute-done.13.b_ref = bf16[2,8,64,128]{3,2,1,0:T(8,128)(2,1)S(1)} collective-permute-done((bf16[2,8,64,128]{3,2,1,0:T(8,128)(2,1)S(1)}, bf16[2,8,64,128]{3,2,1,0:T(8,128)(2,1)S(1)}, u32[]{:S(2)}, u32[]{:S(2)}) %collective-permute-start.13) | collective-permute-done | bytes 262176 | tf_op jit(solution)/shard_map/ppermute | solution.py:21
  24.2 1.4 %collective-permute-start.15 = (bf16[8,64,128]{2,1,0:T(8,128)(2,1)S(1)}, bf16[8,64,128]{2,1,0:T(8,128)(2,1)S(1)}, u32[]{:S(2)}, u32[]{:S(2)}) collective-permute-start(bf16[8,64,128]{2,1,0:T(8,128)(2,1)S(1)} %get-tuple-element.45.refs_0_), channel_id=1, source_target_pairs={{0,8},{4,12},{8,0},{12,4},{1,9},{5,13},{9,1},{13,5},{2,10},{6,14},... | collective-permute-start | bytes 393224 | tf_op jit(solution)/shard_map/ppermute | solution.py:21
  25.6 0.0 collective-permute-done.12.b_ref
  25.6 0.1 add_core_near.1
  25.7 0.7 %collective-permute-start.14 = (bf16[8,64,128]{2,1,0:T(8,128)(2,1)S(1)}, bf16[8,64,128]{2,1,0:T(8,128)(2,1)S(1)}, u32[]{:S(2)}, u32[]{:S(2)}) collective-permute-start(bf16[8,64,128]{2,1,0:T(8,128)(2,1)S(1)} %get-tuple-element.47), channel_id=1, source_target_pairs={{0,1},{1,0},{2,3},{3,2},{4,5},{5,4},{6,7},{7,6},{8,9},{9,8},{10,11... | collective-permute-start | bytes 393224 | tf_op jit(solution)/shard_map/ppermute | solution.py:21
  26.4 2.5 %volume_grad.1 = (bf16[4,4,256,256]{3,2,1,0:T(8,128)(2,1)}, f32[8,128]{1,0:T(8,128)S(1)}) custom-call(bf16[2,512,256]{2,1,0:T(8,128)(2,1)S(1)} %get-tuple-element.37.d_ref, bf16[8,256,256]{2,1,0:T(8,128)(2,1)S(1)} %get-tuple-element.38.w_ref), custom_call_target="tpu_custom_call" | custom-call | flops 1073741824 | bytes 2097152 | tf_op jit(solution)/shard_map/volume_grad/pallas_call | solution.py:509
  29.0 0.9 %collective-permute-done.15.refs_1_ = bf16[8,64,128]{2,1,0:T(8,128)(2,1)S(1)} collective-permute-done((bf16[8,64,128]{2,1,0:T(8,128)(2,1)S(1)}, bf16[8,64,128]{2,1,0:T(8,128)(2,1)S(1)}, u32[]{:S(2)}, u32[]{:S(2)}) %collective-permute-start.15) | collective-permute-done | bytes 131104 | tf_op jit(solution)/shard_map/ppermute | solution.py:21
  29.9 0.1 add_and_pack.1
  30.0 2.9 %collective-permute-start.17 = (bf16[4,64,128]{2,1,0:T(8,128)(2,1)S(1)}, bf16[4,64,128]{2,1,0:T(8,128)(2,1)S(1)}, u32[]{:S(2)}, u32[]{:S(2)}) collective-permute-start(bf16[4,64,128]{2,1,0:T(8,128)(2,1)S(1)} %get-tuple-element.53), channel_id=1, source_target_pairs={{0,2},{1,3},{2,0},{3,1},{4,6},{5,7},{6,4},{7,5},{8,10},{9,11},{10,... | collective-permute-start | bytes 196616 | tf_op jit(solution)/shard_map/ppermute | solution.py:21
  32.8 1.0 %collective-permute-start.18 = (bf16[4,64,128]{2,1,0:T(8,128)(2,1)S(1)}, bf16[4,64,128]{2,1,0:T(8,128)(2,1)S(1)}, u32[]{:S(2)}, u32[]{:S(2)}) collective-permute-start(bf16[4,64,128]{2,1,0:T(8,128)(2,1)S(1)} %get-tuple-element.50.refs_2_), channel_id=1, source_target_pairs={{0,3},{1,2},{2,1},{3,0},{4,7},{5,6},{6,5},{7,4},{8,11},{9,10},{10,... | collective-permute-start | bytes 196616 | tf_op jit(solution)/shard_map/ppermute | solution.py:21
  33.9 0.0 collective-permute-done.14.refs_1_
  33.9 1.4 %collective-permute-start.16 = (bf16[4,64,128]{2,1,0:T(8,128)(2,1)S(1)}, bf16[4,64,128]{2,1,0:T(8,128)(2,1)S(1)}, u32[]{:S(2)}, u32[]{:S(2)}) collective-permute-start(bf16[4,64,128]{2,1,0:T(8,128)(2,1)S(1)} %get-tuple-element.52), channel_id=1, source_target_pairs={{0,8},{4,12},{8,0},{12,4},{1,9},{5,13},{9,1},{13,5},{2,10},{6,14},... | collective-permute-start | bytes 196616 | tf_op jit(solution)/shard_map/ppermute | solution.py:21
  35.3 0.1 collective-permute-done.17.refs_0_
  35.4 3.5 %collective-permute-done.18.refs_1_ = bf16[4,64,128]{2,1,0:T(8,128)(2,1)S(1)} collective-permute-done((bf16[4,64,128]{2,1,0:T(8,128)(2,1)S(1)}, bf16[4,64,128]{2,1,0:T(8,128)(2,1)S(1)}, u32[]{:S(2)}, u32[]{:S(2)}) %collective-permute-start.18) | collective-permute-done | bytes 65568 | tf_op jit(solution)/shard_map/ppermute | solution.py:21
  38.9 0.0 collective-permute-done.16.refs_1_
  38.9 0.8 %finish.1 = f32[8,64,64]{2,1,0:T(8,128)} custom-call(f32[4,64,128]{2,1,0:T(8,128)S(1)} %get-tuple-element.51.refs_0_, bf16[4,64,128]{2,1,0:T(8,128)(2,1)S(1)} %collective-permute-done.16.refs_1_, f32[4,64,128]{2,1,0:T(8,128)S(1)} %fold.1.refs_2_), custom_call_target="tpu_custom_call" | custom-call | tf_op jit(solution)/shard_map/finish/pallas_call | solution.py:463
  (10 shorter events, 0.2 us)
Async XLA Ops:
  0.6 0.9 %copy-start.1 = (bf16[8,64,64]{2,1,0:T(8,128)(2,1)S(1)}, bf16[8,64,64]{2,1,0:T(8,128)(2,1)}, u32[]{:S(2)}) copy-start(bf16[8,64,64]{2,1,0:T(8,128)(2,1)} %w_ref.1) | copy-start | bytes 196612
  1.6 5.7 %collective-permute-start.2 = (bf16[4,64,128]{2,1,0:T(8,128)(2,1)S(1)}, bf16[4,64,128]{2,1,0:T(8,128)(2,1)S(1)}, u32[]{:S(2)}, u32[]{:S(2)}) collective-permute-start(bf16[4,64,128]{2,1,0:T(8,128)(2,1)S(1)} %get-tuple-element.29), channel_id=1, source_target_pairs={{0,1},{1,0},{2,3},{3,2},{4,5},{5,4},{6,7},{7,6},{8,9},{9,8},{10,11... | collective-permute-start | bytes 196616 | tf_op jit(solution)/shard_map/ppermute | solution.py:21
  4.7 8.6 %collective-permute-start = (bf16[4,64,128]{2,1,0:T(8,128)(2,1)S(1)}, bf16[4,64,128]{2,1,0:T(8,128)(2,1)S(1)}, u32[]{:S(2)}, u32[]{:S(2)}) collective-permute-start(bf16[4,64,128]{2,1,0:T(8,128)(2,1)S(1)} %get-tuple-element.28.refs_0_), channel_id=1, source_target_pairs={{0,2},{1,3},{2,0},{3,1},{4,6},{5,7},{6,4},{7,5},{8,10},{9,11},{10,... | collective-permute-start | bytes 196616 | tf_op jit(solution)/shard_map/ppermute | solution.py:21
  7.3 7.5 %collective-permute-start.1 = (bf16[4,64,128]{2,1,0:T(8,128)(2,1)S(1)}, bf16[4,64,128]{2,1,0:T(8,128)(2,1)S(1)}, u32[]{:S(2)}, u32[]{:S(2)}) collective-permute-start(bf16[4,64,128]{2,1,0:T(8,128)(2,1)S(1)} %get-tuple-element.29), channel_id=1, source_target_pairs={{0,3},{1,2},{2,1},{3,0},{4,7},{5,6},{6,5},{7,4},{8,11},{9,10},{10,... | collective-permute-start | bytes 196616 | tf_op jit(solution)/shard_map/ppermute | solution.py:21
  7.4 1.0 %copy-start = (bf16[2,8,128,64]{2,3,1,0:T(8,128)(2,1)S(1)}, bf16[2,8,128,64]{2,3,1,0:T(8,128)(2,1)}, u32[]{:S(2)}) copy-start(bf16[2,8,128,64]{2,3,1,0:T(8,128)(2,1)} %param.5) | copy-start | bytes 786436
  8.3 9.7 %collective-permute-start.3 = (bf16[4,64,128]{2,1,0:T(8,128)(2,1)S(1)}, bf16[4,64,128]{2,1,0:T(8,128)(2,1)S(1)}, u32[]{:S(2)}, u32[]{:S(2)}) collective-permute-start(bf16[4,64,128]{2,1,0:T(8,128)(2,1)S(1)} %get-tuple-element.32), channel_id=1, source_target_pairs={{0,1},{1,0},{2,3},{3,2},{4,5},{5,4},{6,7},{7,6},{8,9},{9,8},{10,11... | collective-permute-start | bytes 196616 | tf_op jit(solution)/shard_map/ppermute | solution.py:21
  10.1 8.1 %collective-permute-start.4 = (bf16[4,64,128]{2,1,0:T(8,128)(2,1)S(1)}, bf16[4,64,128]{2,1,0:T(8,128)(2,1)S(1)}, u32[]{:S(2)}, u32[]{:S(2)}) collective-permute-start(bf16[4,64,128]{2,1,0:T(8,128)(2,1)S(1)} %get-tuple-element.33), channel_id=1, source_target_pairs={{0,2},{1,3},{2,0},{3,1},{4,6},{5,7},{6,4},{7,5},{8,10},{9,11},{10,... | collective-permute-start | bytes 196616 | tf_op jit(solution)/shard_map/ppermute | solution.py:21
  13.3 6.1 %collective-permute-start.5 = (bf16[4,64,128]{2,1,0:T(8,128)(2,1)S(1)}, bf16[4,64,128]{2,1,0:T(8,128)(2,1)S(1)}, u32[]{:S(2)}, u32[]{:S(2)}) collective-permute-start(bf16[4,64,128]{2,1,0:T(8,128)(2,1)S(1)} %get-tuple-element.34), channel_id=1, source_target_pairs={{0,3},{1,2},{2,1},{3,0},{4,7},{5,6},{6,5},{7,4},{8,11},{9,10},{10,... | collective-permute-start | bytes 196616 | tf_op jit(solution)/shard_map/ppermute | solution.py:21
  13.3 6.2 %collective-permute-start.6 = (bf16[8,64,128]{2,1,0:T(8,128)(2,1)S(1)}, bf16[8,64,128]{2,1,0:T(8,128)(2,1)S(1)}, u32[]{:S(2)}, u32[]{:S(2)}) collective-permute-start(bf16[8,64,128]{2,1,0:T(8,128)(2,1)S(1)} %merge_tile.3.refs_0_.t_ref), channel_id=1, source_target_pairs={{0,8},{4,12},{8,0},{12,4},{1,9},{5,13},{9,1},{13,5},{2,10},{6,14},... | collective-permute-start | bytes 393224 | tf_op jit(solution)/shard_map/ppermute | solution.py:21
  14.8 5.0 %collective-permute-start.7 = (bf16[8,64,128]{2,1,0:T(8,128)(2,1)S(1)}, bf16[8,64,128]{2,1,0:T(8,128)(2,1)S(1)}, u32[]{:S(2)}, u32[]{:S(2)}) collective-permute-start(bf16[8,64,128]{2,1,0:T(8,128)(2,1)S(1)} %merge_tile.2.refs_0_.t_ref.refs_1_), channel_id=1, source_target_pairs={{0,8},{4,12},{8,0},{12,4},{1,9},{5,13},{9,1},{13,5},{2,10},{6,14},... | collective-permute-start | bytes 393224 | tf_op jit(solution)/shard_map/ppermute | solution.py:21
  18.1 2.1 %collective-permute-start.10 = (bf16[8,64,128]{2,1,0:T(8,128)(2,1)S(1)}, bf16[8,64,128]{2,1,0:T(8,128)(2,1)S(1)}, u32[]{:S(2)}, u32[]{:S(2)}) collective-permute-start(bf16[8,64,128]{2,1,0:T(8,128)(2,1)S(1)} %gate.6), channel_id=1, source_target_pairs={{0,4},{4,0},{8,12},{12,8},{1,5},{5,1},{9,13},{13,9},{2,6},{6,2},{1... | collective-permute-start | bytes 393224 | tf_op jit(solution)/shard_map/ppermute | solution.py:21
  18.2 2.0 %collective-permute-start.11 = (bf16[8,64,128]{2,1,0:T(8,128)(2,1)S(1)}, bf16[8,64,128]{2,1,0:T(8,128)(2,1)S(1)}, u32[]{:S(2)}, u32[]{:S(2)}) collective-permute-start(bf16[8,64,128]{2,1,0:T(8,128)(2,1)S(1)} %gate.7), channel_id=1, source_target_pairs={{0,4},{4,0},{8,12},{12,8},{1,5},{5,1},{9,13},{13,9},{2,6},{6,2},{1... | collective-permute-start | bytes 393224 | tf_op jit(solution)/shard_map/ppermute | solution.py:21
  19.5 1.4 %collective-permute-start.8 = (bf16[8,64,128]{2,1,0:T(8,128)(2,1)S(1)}, bf16[8,64,128]{2,1,0:T(8,128)(2,1)S(1)}, u32[]{:S(2)}, u32[]{:S(2)}) collective-permute-start(bf16[8,64,128]{2,1,0:T(8,128)(2,1)S(1)} %gate.4), channel_id=1, source_target_pairs={{0,4},{4,0},{8,12},{12,8},{1,5},{5,1},{9,13},{13,9},{2,6},{6,2},{1... | collective-permute-start | bytes 393224 | tf_op jit(solution)/shard_map/ppermute | solution.py:21
  19.9 1.4 %collective-permute-start.9 = (bf16[8,64,128]{2,1,0:T(8,128)(2,1)S(1)}, bf16[8,64,128]{2,1,0:T(8,128)(2,1)S(1)}, u32[]{:S(2)}, u32[]{:S(2)}) collective-permute-start(bf16[8,64,128]{2,1,0:T(8,128)(2,1)S(1)} %gate.5), channel_id=1, source_target_pairs={{0,4},{4,0},{8,12},{12,8},{1,5},{5,1},{9,13},{13,9},{2,6},{6,2},{1... | collective-permute-start | bytes 393224 | tf_op jit(solution)/shard_map/ppermute | solution.py:21
  22.5 1.6 %collective-permute-start.13 = (bf16[2,8,64,128]{3,2,1,0:T(8,128)(2,1)S(1)}, bf16[2,8,64,128]{3,2,1,0:T(8,128)(2,1)S(1)}, u32[]{:S(2)}, u32[]{:S(2)}) collective-permute-start(bf16[2,8,64,128]{3,2,1,0:T(8,128)(2,1)S(1)} %get-tuple-element.44), channel_id=1, source_target_pairs={{0,4},{4,0},{8,12},{12,8},{1,5},{5,1},{9,13},{13,9},{2,6},{6,2},{1... | collective-permute-start | bytes 786440 | tf_op jit(solution)/shard_map/ppermute | solution.py:21
  22.8 2.8 %collective-permute-start.12 = (bf16[2,8,64,128]{3,2,1,0:T(8,128)(2,1)S(1)}, bf16[2,8,64,128]{3,2,1,0:T(8,128)(2,1)S(1)}, u32[]{:S(2)}, u32[]{:S(2)}) collective-permute-start(bf16[2,8,64,128]{3,2,1,0:T(8,128)(2,1)S(1)} %get-tuple-element.42), channel_id=1, source_target_pairs={{0,4},{4,0},{8,12},{12,8},{1,5},{5,1},{9,13},{13,9},{2,6},{6,2},{1... | collective-permute-start | bytes 786440 | tf_op jit(solution)/shard_map/ppermute | solution.py:21
  24.2 5.7 %collective-permute-start.15 = (bf16[8,64,128]{2,1,0:T(8,128)(2,1)S(1)}, bf16[8,64,128]{2,1,0:T(8,128)(2,1)S(1)}, u32[]{:S(2)}, u32[]{:S(2)}) collective-permute-start(bf16[8,64,128]{2,1,0:T(8,128)(2,1)S(1)} %get-tuple-element.45.refs_0_), channel_id=1, source_target_pairs={{0,8},{4,12},{8,0},{12,4},{1,9},{5,13},{9,1},{13,5},{2,10},{6,14},... | collective-permute-start | bytes 393224 | tf_op jit(solution)/shard_map/ppermute | solution.py:21
  25.7 8.1 %collective-permute-start.14 = (bf16[8,64,128]{2,1,0:T(8,128)(2,1)S(1)}, bf16[8,64,128]{2,1,0:T(8,128)(2,1)S(1)}, u32[]{:S(2)}, u32[]{:S(2)}) collective-permute-start(bf16[8,64,128]{2,1,0:T(8,128)(2,1)S(1)} %get-tuple-element.47), channel_id=1, source_target_pairs={{0,1},{1,0},{2,3},{3,2},{4,5},{5,4},{6,7},{7,6},{8,9},{9,8},{10,11... | collective-permute-start | bytes 393224 | tf_op jit(solution)/shard_map/ppermute | solution.py:21
  30.0 5.4 %collective-permute-start.17 = (bf16[4,64,128]{2,1,0:T(8,128)(2,1)S(1)}, bf16[4,64,128]{2,1,0:T(8,128)(2,1)S(1)}, u32[]{:S(2)}, u32[]{:S(2)}) collective-permute-start(bf16[4,64,128]{2,1,0:T(8,128)(2,1)S(1)} %get-tuple-element.53), channel_id=1, source_target_pairs={{0,2},{1,3},{2,0},{3,1},{4,6},{5,7},{6,4},{7,5},{8,10},{9,11},{10,... | collective-permute-start | bytes 196616 | tf_op jit(solution)/shard_map/ppermute | solution.py:21
  32.8 6.1 %collective-permute-start.18 = (bf16[4,64,128]{2,1,0:T(8,128)(2,1)S(1)}, bf16[4,64,128]{2,1,0:T(8,128)(2,1)S(1)}, u32[]{:S(2)}, u32[]{:S(2)}) collective-permute-start(bf16[4,64,128]{2,1,0:T(8,128)(2,1)S(1)} %get-tuple-element.50.refs_2_), channel_id=1, source_target_pairs={{0,3},{1,2},{2,1},{3,0},{4,7},{5,6},{6,5},{7,4},{8,11},{9,10},{10,... | collective-permute-start | bytes 196616 | tf_op jit(solution)/shard_map/ppermute | solution.py:21
  33.9 5.0 %collective-permute-start.16 = (bf16[4,64,128]{2,1,0:T(8,128)(2,1)S(1)}, bf16[4,64,128]{2,1,0:T(8,128)(2,1)S(1)}, u32[]{:S(2)}, u32[]{:S(2)}) collective-permute-start(bf16[4,64,128]{2,1,0:T(8,128)(2,1)S(1)} %get-tuple-element.52), channel_id=1, source_target_pairs={{0,8},{4,12},{8,0},{12,4},{1,9},{5,13},{9,1},{13,5},{2,10},{6,14},... | collective-permute-start | bytes 196616 | tf_op jit(solution)/shard_map/ppermute | solution.py:21

commit v5 on v4

--- a/solution.py
+++ b/solution.py
@@ -274,8 +274,8 @@
         d_ref, w_ref = refs[-2:]
         me = lax.axis_index("space")
         place(w_ref, refs[:len(flat)], me, start, tiles)
-        for first in range(0, rows, rows // 2):
-            here = slice(first, first + rows // 2)
+        for first in range(0, rows, rows // 4):
+            here = slice(first, first + rows // 4)
             pre = None if own is None else refs[len(flat)][here]
             for q in range(ratio):
                 acc = None
@@ -558,7 +558,7 @@
         far = list(sums[1:]) + far
         came = [fetch(sums[n], "space", pairs(spaces, steps[n])) for n in range(1, len(steps))]
         outs += [(t * ratio + u, part) for u, part in enumerate(add_and_pack(sums[0], came, width, (mark,)))]
-    parts = add_core_near(near[0], crossed[0], width, far[:1])
+    parts = add_core_near(near[0], crossed[0], width, far[:1] + [mark])
     got = [fetch(parts[u], "chan", pairs(chans, u)) for u in range(1, ratio)]
     sums = add_near(parts[0], got, kinds // ratio, [part for _, part in outs[-1:]])
     got = [sums[0]] + [fetch(sums[n], "space", pairs(spaces, steps[n])) for n in range(1, len(steps))]

time: 39.9 us -> 39.9 us (level)
  waiting for transfers between devices: 6.66 us -> 7.41 us
  starting transfers between devices: 21.8 us -> 21.1 us
    ppermute x19, waiting for transfers between devices: 6.66 us -> 7.41 us  [fetch(): return lax.ppermute(x, axis, pairs)]
    ppermute x19, starting transfers between devices: 21.8 us -> 21.1 us  [fetch(): return lax.ppermute(x, axis, pairs)]
  transfers between devices with their start and end apart: 19 -> 19, of which waited for: 8 -> 9; matrix products, arithmetic and copies ran while one was open for 0% -> 0% of each run, Pallas kernels for 16% -> 16%
where the time goes in v5:
time: 39.9 us; the launch traced here: 39.7 us
  starting transfers between devices  21.1 us (53%)
  Pallas kernels  8.55 us (21%)
  waiting for transfers between devices  7.41 us (19%)
  local copies, waits for them, and re-layouts  1.84 us (5%)
  between operations  0.82 us (2%)
    ppermute x19, starting transfers between devices, fetch(): return lax.ppermute(x, axis, pairs)  21.1 us
    ppermute x19, waiting for transfers between devices, fetch(): return lax.ppermute(x, axis, pairs)  7.41 us
    pallas_call x1, Pallas kernels, volume_grad(): pl.pallas_call(body, in_specs=[pl.BlockSpec(memory_space=pltpu.VMEM)] * 2...  2.52 us
    pallas_call x1, Pallas kernels, patch_rows(): pl.pallas_call(body, in_specs=[pl.BlockSpec(memory_space=pltpu.VMEM)] + [...  2.37 us
    unnamed x4, local copies, waits for them, and re-layouts  1.84 us
    pallas_call x2, Pallas kernels, weight_part(): pl.pallas_call(body, out_shape=[jax.ShapeDtypeStruct((len(steps), kinds,...  0.86 us
    pallas_call x1, Pallas kernels, finish(): pl.pallas_call(body, out_shape=jax.ShapeDtypeStruct((kinds, block, width)...  0.81 us
  transfers between devices with their start and end apart: 19, of which 9 were waited for; matrix products, arithmetic and copies ran while one was open for 0% of the time, Pallas kernels for 16%

profile of v5, /device:TPU:0, one launch (start us, length us, event | category | flops | bytes accessed | tf_op | source)
XLA Modules:
  0.0 39.7 jit_solution(711299568536750149)
XLA Ops:
  0.6 0.0 copy-start.1
  0.6 0.9 %copy-done.1 = bf16[8,64,64]{2,1,0:T(8,128)(2,1)S(1)} copy-done((bf16[8,64,64]{2,1,0:T(8,128)(2,1)S(1)}, bf16[8,64,64]{2,1,0:T(8,128)(2,1)}, u32[]{:S(2)}) %copy-start.1) | copy-done | bytes 65560
  1.5 0.1 pack_weight.1
  1.6 3.1 %collective-permute-start.2 = (bf16[4,64,128]{2,1,0:T(8,128)(2,1)S(1)}, bf16[4,64,128]{2,1,0:T(8,128)(2,1)S(1)}, u32[]{:S(2)}, u32[]{:S(2)}) collective-permute-start(bf16[4,64,128]{2,1,0:T(8,128)(2,1)S(1)} %get-tuple-element.29), channel_id=1, source_target_pairs={{0,1},{1,0},{2,3},{3,2},{4,5},{5,4},{6,7},{7,6},{8,9},{9,8},{10,11... | collective-permute-start | bytes 196616 | tf_op jit(solution)/shard_map/ppermute | solution.py:21
  4.7 2.6 %collective-permute-start = (bf16[4,64,128]{2,1,0:T(8,128)(2,1)S(1)}, bf16[4,64,128]{2,1,0:T(8,128)(2,1)S(1)}, u32[]{:S(2)}, u32[]{:S(2)}) collective-permute-start(bf16[4,64,128]{2,1,0:T(8,128)(2,1)S(1)} %get-tuple-element.28.refs_0_), channel_id=1, source_target_pairs={{0,2},{1,3},{2,0},{3,1},{4,6},{5,7},{6,4},{7,5},{8,10},{9,11},{10,... | collective-permute-start | bytes 196616 | tf_op jit(solution)/shard_map/ppermute | solution.py:21
  7.3 0.0 collective-permute-start.1
  7.3 0.0 collective-permute-done.2.refs_1_
  7.4 0.0 copy-start
  7.4 0.9 %copy-done = bf16[2,8,128,64]{2,3,1,0:T(8,128)(2,1)S(1)} copy-done((bf16[2,8,128,64]{2,3,1,0:T(8,128)(2,1)S(1)}, bf16[2,8,128,64]{2,3,1,0:T(8,128)(2,1)}, u32[]{:S(2)}) %copy-start) | copy-done | bytes 262168
  8.3 1.7 %collective-permute-start.3 = (bf16[4,64,128]{2,1,0:T(8,128)(2,1)S(1)}, bf16[4,64,128]{2,1,0:T(8,128)(2,1)S(1)}, u32[]{:S(2)}, u32[]{:S(2)}) collective-permute-start(bf16[4,64,128]{2,1,0:T(8,128)(2,1)S(1)} %get-tuple-element.32), channel_id=1, source_target_pairs={{0,1},{1,0},{2,3},{3,2},{4,5},{5,4},{6,7},{7,6},{8,9},{9,8},{10,11... | collective-permute-start | bytes 196616 | tf_op jit(solution)/shard_map/ppermute | solution.py:21
  10.1 3.2 %collective-permute-start.4 = (bf16[4,64,128]{2,1,0:T(8,128)(2,1)S(1)}, bf16[4,64,128]{2,1,0:T(8,128)(2,1)S(1)}, u32[]{:S(2)}, u32[]{:S(2)}) collective-permute-start(bf16[4,64,128]{2,1,0:T(8,128)(2,1)S(1)} %get-tuple-element.33), channel_id=1, source_target_pairs={{0,2},{1,3},{2,0},{3,1},{4,6},{5,7},{6,4},{7,5},{8,10},{9,11},{10,... | collective-permute-start | bytes 196616 | tf_op jit(solution)/shard_map/ppermute | solution.py:21
  13.3 0.0 collective-permute-start.5
  13.3 0.0 collective-permute-done.refs_0_
  13.3 1.5 %collective-permute-start.6 = (bf16[8,64,128]{2,1,0:T(8,128)(2,1)S(1)}, bf16[8,64,128]{2,1,0:T(8,128)(2,1)S(1)}, u32[]{:S(2)}, u32[]{:S(2)}) collective-permute-start(bf16[8,64,128]{2,1,0:T(8,128)(2,1)S(1)} %merge_tile.3.refs_0_.t_ref), channel_id=1, source_target_pairs={{0,8},{4,12},{8,0},{12,4},{1,9},{5,13},{9,1},{13,5},{2,10},{6,14},... | collective-permute-start | bytes 393224 | tf_op jit(solution)/shard_map/ppermute | solution.py:21
  14.8 0.0 collective-permute-done.1.refs_1_
  14.8 0.8 %collective-permute-start.7 = (bf16[8,64,128]{2,1,0:T(8,128)(2,1)S(1)}, bf16[8,64,128]{2,1,0:T(8,128)(2,1)S(1)}, u32[]{:S(2)}, u32[]{:S(2)}) collective-permute-start(bf16[8,64,128]{2,1,0:T(8,128)(2,1)S(1)} %merge_tile.2.refs_0_.t_ref.refs_1_), channel_id=1, source_target_pairs={{0,8},{4,12},{8,0},{12,4},{1,9},{5,13},{9,1},{13,5},{2,10},{6,14},... | collective-permute-start | bytes 393224 | tf_op jit(solution)/shard_map/ppermute | solution.py:21
  15.6 2.4 %patch_rows.1 = (bf16[8,512,256]{2,1,0:T(8,128)(2,1)S(1)}, bf16[8,256,512]{2,1,0:T(8,128)(2,1)S(1)}) custom-call(bf16[4,4,256,256]{3,2,1,0:T(8,128)(2,1)} %v_ref.1, bf16[8,64,128]{2,1,0:T(8,128)(2,1)S(1)} %merge_tile.2.refs_0_.t_ref.refs_1_), custom_call_target="tpu_custom_call" | custom-call | flops 536870912 | bytes 6291456 | tf_op jit(solution)/shard_map/patch_rows/pallas_call | solution.py:176
  18.1 0.0 collective-permute-done.3.refs_1_
  18.1 0.1 collective-permute-start.10
  18.1 0.0 collective-permute-done.4.refs_2_
  18.2 0.5 %collective-permute-start.11 = (bf16[8,64,128]{2,1,0:T(8,128)(2,1)S(1)}, bf16[8,64,128]{2,1,0:T(8,128)(2,1)S(1)}, u32[]{:S(2)}, u32[]{:S(2)}) collective-permute-start(bf16[8,64,128]{2,1,0:T(8,128)(2,1)S(1)} %gate.7), channel_id=1, source_target_pairs={{0,4},{4,0},{8,12},{12,8},{1,5},{5,1},{9,13},{13,9},{2,6},{6,2},{1... | collective-permute-start | bytes 393224 | tf_op jit(solution)/shard_map/ppermute | solution.py:21
  18.6 0.7 %collective-permute-done.5.refs_3_ = bf16[4,64,128]{2,1,0:T(8,128)(2,1)S(1)} collective-permute-done((bf16[4,64,128]{2,1,0:T(8,128)(2,1)S(1)}, bf16[4,64,128]{2,1,0:T(8,128)(2,1)S(1)}, u32[]{:S(2)}, u32[]{:S(2)}) %collective-permute-start.5) | collective-permute-done | bytes 65568 | tf_op jit(solution)/shard_map/ppermute | solution.py:21
  19.4 0.1 turn_cot.1.refs_0_.u_ref
  19.5 0.0 collective-permute-done.6.t_ref.refs_0_
  19.5 0.1 collective-permute-start.8
  19.6 0.3 collective-permute-done.7.t_ref.refs_1_
  19.9 0.3 collective-permute-start.9
  20.2 0.0 collective-permute-done.10.refs_2_
  20.2 0.0 collective-permute-done.11.refs_3_
  20.2 0.6 %forward_own.1 = (f32[512,256]{1,0:T(8,128)S(1)}, bf16[8,256,256]{2,1,0:T(8,128)(2,1)S(1)}) custom-call(bf16[8,512,256]{2,1,0:T(8,128)(2,1)S(1)} %get-tuple-element.30.refs_0_.p_ref, bf16[8,64,128]{2,1,0:T(8,128)(2,1)S(1)} %merge_tile.3.refs_0_.t_ref, bf16[8,64,128]{2,1,0:T(8,128)(2,1)S(1)} %merge_tile.2.refs_0_.t_ref.refs_1_, ...), custom_call_target="tpu_custom_call" | custom-call | flops 268435456 | bytes 2097152 | tf_op jit(solution)/shard_map/forward_own/pallas_call | solution.py:252
  20.8 0.1 collective-permute-done.8.refs_2_
  20.9 0.4 collective-permute-done.9.refs_3_
  21.3 0.7 %forward.1 = (bf16[2,512,256]{2,1,0:T(8,128)(2,1)S(1)}, bf16[8,256,256]{2,1,0:T(8,128)(2,1)S(1)}) custom-call(bf16[8,512,256]{2,1,0:T(8,128)(2,1)S(1)} %get-tuple-element.30.refs_0_.p_ref, bf16[512,256]{1,0:T(8,128)(2,1)S(1)} %turn_cot.1.refs_0_.u_ref, bf16[8,64,128]{2,1,0:T(8,128)(2,1)S(1)} %collective-permute-done.6.t_ref.refs_0_, ...), custom_call_target="tpu_custom_call", output_to_operand_aliasing={{1}: (7, {})} | custom-call | flops 536870912 | bytes 2097152 | tf_op jit(solution)/shard_map/forward/pallas_call | solution.py:301
  22.0 0.4 %weight_part.3 = (bf16[2,8,64,128]{3,2,1,0:T(8,128)(2,1)S(1)}, bf16[2,8,64,128]{3,2,1,0:T(8,128)(2,1)S(1)}) custom-call(bf16[8,256,512]{2,1,0:T(8,128)(2,1)S(1)} %get-tuple-element.40.t_ref, bf16[2,512,256]{2,1,0:T(8,128)(2,1)S(1)} %get-tuple-element.37.d_ref), custom_call_target="tpu_custom_call" | custom-call | flops 268435456 | bytes 2097152 | tf_op jit(solution)/shard_map/weight_part/pallas_call | solution.py:332
  22.5 0.3 collective-permute-start.13
  22.8 0.3 collective-permute-start.12
  23.0 0.4 %weight_part.2 = (f32[2,8,64,128]{3,2,1,0:T(8,128)S(1)}, f32[2,8,64,128]{3,2,1,0:T(8,128)S(1)}) custom-call(bf16[8,256,512]{2,1,0:T(8,128)(2,1)S(1)} %get-tuple-element.40.t_ref, bf16[2,512,256]{2,1,0:T(8,128)(2,1)S(1)} %get-tuple-element.37.d_ref), custom_call_target="tpu_custom_call" | custom-call | flops 268435456 | bytes 2097152 | tf_op jit(solution)/shard_map/weight_part/pallas_call | solution.py:332
  23.5 0.6 %collective-permute-done.13.b_ref = bf16[2,8,64,128]{3,2,1,0:T(8,128)(2,1)S(1)} collective-permute-done((bf16[2,8,64,128]{3,2,1,0:T(8,128)(2,1)S(1)}, bf16[2,8,64,128]{3,2,1,0:T(8,128)(2,1)S(1)}, u32[]{:S(2)}, u32[]{:S(2)}) %collective-permute-start.13) | collective-permute-done | bytes 262176 | tf_op jit(solution)/shard_map/ppermute | solution.py:21
  24.1 1.4 %collective-permute-start.15 = (bf16[8,64,128]{2,1,0:T(8,128)(2,1)S(1)}, bf16[8,64,128]{2,1,0:T(8,128)(2,1)S(1)}, u32[]{:S(2)}, u32[]{:S(2)}) collective-permute-start(bf16[8,64,128]{2,1,0:T(8,128)(2,1)S(1)} %get-tuple-element.45.refs_0_), channel_id=1, source_target_pairs={{0,8},{4,12},{8,0},{12,4},{1,9},{5,13},{9,1},{13,5},{2,10},{6,14},... | collective-permute-start | bytes 393224 | tf_op jit(solution)/shard_map/ppermute | solution.py:21
  25.6 2.5 %volume_grad.1 = (bf16[4,4,256,256]{3,2,1,0:T(8,128)(2,1)}, f32[8,128]{1,0:T(8,128)S(1)}) custom-call(bf16[2,512,256]{2,1,0:T(8,128)(2,1)S(1)} %get-tuple-element.37.d_ref, bf16[8,256,256]{2,1,0:T(8,128)(2,1)S(1)} %get-tuple-element.38.w_ref), custom_call_target="tpu_custom_call" | custom-call | flops 1073741824 | bytes 2097152 | tf_op jit(solution)/shard_map/volume_grad/pallas_call | solution.py:509
  28.1 0.0 collective-permute-done.12.b_ref
  28.1 0.1 add_core_near.1
  28.2 0.7 %collective-permute-start.14 = (bf16[8,64,128]{2,1,0:T(8,128)(2,1)S(1)}, bf16[8,64,128]{2,1,0:T(8,128)(2,1)S(1)}, u32[]{:S(2)}, u32[]{:S(2)}) collective-permute-start(bf16[8,64,128]{2,1,0:T(8,128)(2,1)S(1)} %get-tuple-element.48), channel_id=1, source_target_pairs={{0,1},{1,0},{2,3},{3,2},{4,5},{5,4},{6,7},{7,6},{8,9},{9,8},{10,11... | collective-permute-start | bytes 393224 | tf_op jit(solution)/shard_map/ppermute | solution.py:21
  28.9 0.9 %collective-permute-done.15.refs_1_ = bf16[8,64,128]{2,1,0:T(8,128)(2,1)S(1)} collective-permute-done((bf16[8,64,128]{2,1,0:T(8,128)(2,1)S(1)}, bf16[8,64,128]{2,1,0:T(8,128)(2,1)S(1)}, u32[]{:S(2)}, u32[]{:S(2)}) %collective-permute-start.15) | collective-permute-done | bytes 131104 | tf_op jit(solution)/shard_map/ppermute | solution.py:21
  29.8 0.1 add_and_pack.1
  29.9 2.9 %collective-permute-start.17 = (bf16[4,64,128]{2,1,0:T(8,128)(2,1)S(1)}, bf16[4,64,128]{2,1,0:T(8,128)(2,1)S(1)}, u32[]{:S(2)}, u32[]{:S(2)}) collective-permute-start(bf16[4,64,128]{2,1,0:T(8,128)(2,1)S(1)} %get-tuple-element.53), channel_id=1, source_target_pairs={{0,2},{1,3},{2,0},{3,1},{4,6},{5,7},{6,4},{7,5},{8,10},{9,11},{10,... | collective-permute-start | bytes 196616 | tf_op jit(solution)/shard_map/ppermute | solution.py:21
  32.8 1.0 %collective-permute-start.18 = (bf16[4,64,128]{2,1,0:T(8,128)(2,1)S(1)}, bf16[4,64,128]{2,1,0:T(8,128)(2,1)S(1)}, u32[]{:S(2)}, u32[]{:S(2)}) collective-permute-start(bf16[4,64,128]{2,1,0:T(8,128)(2,1)S(1)} %get-tuple-element.50.refs_2_), channel_id=1, source_target_pairs={{0,3},{1,2},{2,1},{3,0},{4,7},{5,6},{6,5},{7,4},{8,11},{9,10},{10,... | collective-permute-start | bytes 196616 | tf_op jit(solution)/shard_map/ppermute | solution.py:21
  33.8 0.7 %collective-permute-done.14.refs_1_ = bf16[8,64,128]{2,1,0:T(8,128)(2,1)S(1)} collective-permute-done((bf16[8,64,128]{2,1,0:T(8,128)(2,1)S(1)}, bf16[8,64,128]{2,1,0:T(8,128)(2,1)S(1)}, u32[]{:S(2)}, u32[]{:S(2)}) %collective-permute-start.14) | collective-permute-done | bytes 131104 | tf_op jit(solution)/shard_map/ppermute | solution.py:21
  34.5 0.7 %collective-permute-start.16 = (bf16[4,64,128]{2,1,0:T(8,128)(2,1)S(1)}, bf16[4,64,128]{2,1,0:T(8,128)(2,1)S(1)}, u32[]{:S(2)}, u32[]{:S(2)}) collective-permute-start(bf16[4,64,128]{2,1,0:T(8,128)(2,1)S(1)} %get-tuple-element.52), channel_id=1, source_target_pairs={{0,8},{4,12},{8,0},{12,4},{1,9},{5,13},{9,1},{13,5},{2,10},{6,14},... | collective-permute-start | bytes 196616 | tf_op jit(solution)/shard_map/ppermute | solution.py:21
  35.2 0.9 %collective-permute-done.17.refs_0_ = bf16[4,64,128]{2,1,0:T(8,128)(2,1)S(1)} collective-permute-done((bf16[4,64,128]{2,1,0:T(8,128)(2,1)S(1)}, bf16[4,64,128]{2,1,0:T(8,128)(2,1)S(1)}, u32[]{:S(2)}, u32[]{:S(2)}) %collective-permute-start.17) | collective-permute-done | bytes 65568 | tf_op jit(solution)/shard_map/ppermute | solution.py:21
  36.1 2.8 %collective-permute-done.18.refs_1_ = bf16[4,64,128]{2,1,0:T(8,128)(2,1)S(1)} collective-permute-done((bf16[4,64,128]{2,1,0:T(8,128)(2,1)S(1)}, bf16[4,64,128]{2,1,0:T(8,128)(2,1)S(1)}, u32[]{:S(2)}, u32[]{:S(2)}) %collective-permute-start.18) | collective-permute-done | bytes 65568 | tf_op jit(solution)/shard_map/ppermute | solution.py:21
  38.9 0.0 collective-permute-done.16.refs_1_
  38.9 0.8 %finish.1 = f32[8,64,64]{2,1,0:T(8,128)} custom-call(f32[4,64,128]{2,1,0:T(8,128)S(1)} %get-tuple-element.51.refs_0_, bf16[4,64,128]{2,1,0:T(8,128)(2,1)S(1)} %collective-permute-done.16.refs_1_, f32[4,64,128]{2,1,0:T(8,128)S(1)} %fold.1.refs_2_), custom_call_target="tpu_custom_call" | custom-call | tf_op jit(solution)/shard_map/finish/pallas_call | solution.py:463
  (10 shorter events, 0.2 us)
Async XLA Ops:
  0.6 0.9 %copy-start.1 = (bf16[8,64,64]{2,1,0:T(8,128)(2,1)S(1)}, bf16[8,64,64]{2,1,0:T(8,128)(2,1)}, u32[]{:S(2)}) copy-start(bf16[8,64,64]{2,1,0:T(8,128)(2,1)} %w_ref.1) | copy-start | bytes 196612
  1.6 5.7 %collective-permute-start.2 = (bf16[4,64,128]{2,1,0:T(8,128)(2,1)S(1)}, bf16[4,64,128]{2,1,0:T(8,128)(2,1)S(1)}, u32[]{:S(2)}, u32[]{:S(2)}) collective-permute-start(bf16[4,64,128]{2,1,0:T(8,128)(2,1)S(1)} %get-tuple-element.29), channel_id=1, source_target_pairs={{0,1},{1,0},{2,3},{3,2},{4,5},{5,4},{6,7},{7,6},{8,9},{9,8},{10,11... | collective-permute-start | bytes 196616 | tf_op jit(solution)/shard_map/ppermute | solution.py:21
  4.7 8.6 %collective-permute-start = (bf16[4,64,128]{2,1,0:T(8,128)(2,1)S(1)}, bf16[4,64,128]{2,1,0:T(8,128)(2,1)S(1)}, u32[]{:S(2)}, u32[]{:S(2)}) collective-permute-start(bf16[4,64,128]{2,1,0:T(8,128)(2,1)S(1)} %get-tuple-element.28.refs_0_), channel_id=1, source_target_pairs={{0,2},{1,3},{2,0},{3,1},{4,6},{5,7},{6,4},{7,5},{8,10},{9,11},{10,... | collective-permute-start | bytes 196616 | tf_op jit(solution)/shard_map/ppermute | solution.py:21
  7.3 7.5 %collective-permute-start.1 = (bf16[4,64,128]{2,1,0:T(8,128)(2,1)S(1)}, bf16[4,64,128]{2,1,0:T(8,128)(2,1)S(1)}, u32[]{:S(2)}, u32[]{:S(2)}) collective-permute-start(bf16[4,64,128]{2,1,0:T(8,128)(2,1)S(1)} %get-tuple-element.29), channel_id=1, source_target_pairs={{0,3},{1,2},{2,1},{3,0},{4,7},{5,6},{6,5},{7,4},{8,11},{9,10},{10,... | collective-permute-start | bytes 196616 | tf_op jit(solution)/shard_map/ppermute | solution.py:21
  7.4 1.0 %copy-start = (bf16[2,8,128,64]{2,3,1,0:T(8,128)(2,1)S(1)}, bf16[2,8,128,64]{2,3,1,0:T(8,128)(2,1)}, u32[]{:S(2)}) copy-start(bf16[2,8,128,64]{2,3,1,0:T(8,128)(2,1)} %param.5) | copy-start | bytes 786436
  8.3 9.7 %collective-permute-start.3 = (bf16[4,64,128]{2,1,0:T(8,128)(2,1)S(1)}, bf16[4,64,128]{2,1,0:T(8,128)(2,1)S(1)}, u32[]{:S(2)}, u32[]{:S(2)}) collective-permute-start(bf16[4,64,128]{2,1,0:T(8,128)(2,1)S(1)} %get-tuple-element.32), channel_id=1, source_target_pairs={{0,1},{1,0},{2,3},{3,2},{4,5},{5,4},{6,7},{7,6},{8,9},{9,8},{10,11... | collective-permute-start | bytes 196616 | tf_op jit(solution)/shard_map/ppermute | solution.py:21
  10.1 8.1 %collective-permute-start.4 = (bf16[4,64,128]{2,1,0:T(8,128)(2,1)S(1)}, bf16[4,64,128]{2,1,0:T(8,128)(2,1)S(1)}, u32[]{:S(2)}, u32[]{:S(2)}) collective-permute-start(bf16[4,64,128]{2,1,0:T(8,128)(2,1)S(1)} %get-tuple-element.33), channel_id=1, source_target_pairs={{0,2},{1,3},{2,0},{3,1},{4,6},{5,7},{6,4},{7,5},{8,10},{9,11},{10,... | collective-permute-start | bytes 196616 | tf_op jit(solution)/shard_map/ppermute | solution.py:21
  13.3 6.1 %collective-permute-start.5 = (bf16[4,64,128]{2,1,0:T(8,128)(2,1)S(1)}, bf16[4,64,128]{2,1,0:T(8,128)(2,1)S(1)}, u32[]{:S(2)}, u32[]{:S(2)}) collective-permute-start(bf16[4,64,128]{2,1,0:T(8,128)(2,1)S(1)} %get-tuple-element.34), channel_id=1, source_target_pairs={{0,3},{1,2},{2,1},{3,0},{4,7},{5,6},{6,5},{7,4},{8,11},{9,10},{10,... | collective-permute-start | bytes 196616 | tf_op jit(solution)/shard_map/ppermute | solution.py:21
  13.3 6.2 %collective-permute-start.6 = (bf16[8,64,128]{2,1,0:T(8,128)(2,1)S(1)}, bf16[8,64,128]{2,1,0:T(8,128)(2,1)S(1)}, u32[]{:S(2)}, u32[]{:S(2)}) collective-permute-start(bf16[8,64,128]{2,1,0:T(8,128)(2,1)S(1)} %merge_tile.3.refs_0_.t_ref), channel_id=1, source_target_pairs={{0,8},{4,12},{8,0},{12,4},{1,9},{5,13},{9,1},{13,5},{2,10},{6,14},... | collective-permute-start | bytes 393224 | tf_op jit(solution)/shard_map/ppermute | solution.py:21
  14.8 5.0 %collective-permute-start.7 = (bf16[8,64,128]{2,1,0:T(8,128)(2,1)S(1)}, bf16[8,64,128]{2,1,0:T(8,128)(2,1)S(1)}, u32[]{:S(2)}, u32[]{:S(2)}) collective-permute-start(bf16[8,64,128]{2,1,0:T(8,128)(2,1)S(1)} %merge_tile.2.refs_0_.t_ref.refs_1_), channel_id=1, source_target_pairs={{0,8},{4,12},{8,0},{12,4},{1,9},{5,13},{9,1},{13,5},{2,10},{6,14},... | collective-permute-start | bytes 393224 | tf_op jit(solution)/shard_map/ppermute | solution.py:21
  18.1 2.1 %collective-permute-start.10 = (bf16[8,64,128]{2,1,0:T(8,128)(2,1)S(1)}, bf16[8,64,128]{2,1,0:T(8,128)(2,1)S(1)}, u32[]{:S(2)}, u32[]{:S(2)}) collective-permute-start(bf16[8,64,128]{2,1,0:T(8,128)(2,1)S(1)} %gate.6), channel_id=1, source_target_pairs={{0,4},{4,0},{8,12},{12,8},{1,5},{5,1},{9,13},{13,9},{2,6},{6,2},{1... | collective-permute-start | bytes 393224 | tf_op jit(solution)/shard_map/ppermute | solution.py:21
  18.2 2.0 %collective-permute-start.11 = (bf16[8,64,128]{2,1,0:T(8,128)(2,1)S(1)}, bf16[8,64,128]{2,1,0:T(8,128)(2,1)S(1)}, u32[]{:S(2)}, u32[]{:S(2)}) collective-permute-start(bf16[8,64,128]{2,1,0:T(8,128)(2,1)S(1)} %gate.7), channel_id=1, source_target_pairs={{0,4},{4,0},{8,12},{12,8},{1,5},{5,1},{9,13},{13,9},{2,6},{6,2},{1... | collective-permute-start | bytes 393224 | tf_op jit(solution)/shard_map/ppermute | solution.py:21
  19.5 1.4 %collective-permute-start.8 = (bf16[8,64,128]{2,1,0:T(8,128)(2,1)S(1)}, bf16[8,64,128]{2,1,0:T(8,128)(2,1)S(1)}, u32[]{:S(2)}, u32[]{:S(2)}) collective-permute-start(bf16[8,64,128]{2,1,0:T(8,128)(2,1)S(1)} %gate.4), channel_id=1, source_target_pairs={{0,4},{4,0},{8,12},{12,8},{1,5},{5,1},{9,13},{13,9},{2,6},{6,2},{1... | collective-permute-start | bytes 393224 | tf_op jit(solution)/shard_map/ppermute | solution.py:21
  19.9 1.4 %collective-permute-start.9 = (bf16[8,64,128]{2,1,0:T(8,128)(2,1)S(1)}, bf16[8,64,128]{2,1,0:T(8,128)(2,1)S(1)}, u32[]{:S(2)}, u32[]{:S(2)}) collective-permute-start(bf16[8,64,128]{2,1,0:T(8,128)(2,1)S(1)} %gate.5), channel_id=1, source_target_pairs={{0,4},{4,0},{8,12},{12,8},{1,5},{5,1},{9,13},{13,9},{2,6},{6,2},{1... | collective-permute-start | bytes 393224 | tf_op jit(solution)/shard_map/ppermute | solution.py:21
  22.5 1.6 %collective-permute-start.13 = (bf16[2,8,64,128]{3,2,1,0:T(8,128)(2,1)S(1)}, bf16[2,8,64,128]{3,2,1,0:T(8,128)(2,1)S(1)}, u32[]{:S(2)}, u32[]{:S(2)}) collective-permute-start(bf16[2,8,64,128]{3,2,1,0:T(8,128)(2,1)S(1)} %get-tuple-element.44), channel_id=1, source_target_pairs={{0,4},{4,0},{8,12},{12,8},{1,5},{5,1},{9,13},{13,9},{2,6},{6,2},{1... | collective-permute-start | bytes 786440 | tf_op jit(solution)/shard_map/ppermute | solution.py:21
  22.8 5.3 %collective-permute-start.12 = (bf16[2,8,64,128]{3,2,1,0:T(8,128)(2,1)S(1)}, bf16[2,8,64,128]{3,2,1,0:T(8,128)(2,1)S(1)}, u32[]{:S(2)}, u32[]{:S(2)}) collective-permute-start(bf16[2,8,64,128]{3,2,1,0:T(8,128)(2,1)S(1)} %get-tuple-element.42), channel_id=1, source_target_pairs={{0,4},{4,0},{8,12},{12,8},{1,5},{5,1},{9,13},{13,9},{2,6},{6,2},{1... | collective-permute-start | bytes 786440 | tf_op jit(solution)/shard_map/ppermute | solution.py:21
  24.1 5.7 %collective-permute-start.15 = (bf16[8,64,128]{2,1,0:T(8,128)(2,1)S(1)}, bf16[8,64,128]{2,1,0:T(8,128)(2,1)S(1)}, u32[]{:S(2)}, u32[]{:S(2)}) collective-permute-start(bf16[8,64,128]{2,1,0:T(8,128)(2,1)S(1)} %get-tuple-element.45.refs_0_), channel_id=1, source_target_pairs={{0,8},{4,12},{8,0},{12,4},{1,9},{5,13},{9,1},{13,5},{2,10},{6,14},... | collective-permute-start | bytes 393224 | tf_op jit(solution)/shard_map/ppermute | solution.py:21
  28.2 6.3 %collective-permute-start.14 = (bf16[8,64,128]{2,1,0:T(8,128)(2,1)S(1)}, bf16[8,64,128]{2,1,0:T(8,128)(2,1)S(1)}, u32[]{:S(2)}, u32[]{:S(2)}) collective-permute-start(bf16[8,64,128]{2,1,0:T(8,128)(2,1)S(1)} %get-tuple-element.48), channel_id=1, source_target_pairs={{0,1},{1,0},{2,3},{3,2},{4,5},{5,4},{6,7},{7,6},{8,9},{9,8},{10,11... | collective-permute-start | bytes 393224 | tf_op jit(solution)/shard_map/ppermute | solution.py:21
  29.9 6.1 %collective-permute-start.17 = (bf16[4,64,128]{2,1,0:T(8,128)(2,1)S(1)}, bf16[4,64,128]{2,1,0:T(8,128)(2,1)S(1)}, u32[]{:S(2)}, u32[]{:S(2)}) collective-permute-start(bf16[4,64,128]{2,1,0:T(8,128)(2,1)S(1)} %get-tuple-element.53), channel_id=1, source_target_pairs={{0,2},{1,3},{2,0},{3,1},{4,6},{5,7},{6,4},{7,5},{8,10},{9,11},{10,... | collective-permute-start | bytes 196616 | tf_op jit(solution)/shard_map/ppermute | solution.py:21
  32.8 6.1 %collective-permute-start.18 = (bf16[4,64,128]{2,1,0:T(8,128)(2,1)S(1)}, bf16[4,64,128]{2,1,0:T(8,128)(2,1)S(1)}, u32[]{:S(2)}, u32[]{:S(2)}) collective-permute-start(bf16[4,64,128]{2,1,0:T(8,128)(2,1)S(1)} %get-tuple-element.50.refs_2_), channel_id=1, source_target_pairs={{0,3},{1,2},{2,1},{3,0},{4,7},{5,6},{6,5},{7,4},{8,11},{9,10},{10,... | collective-permute-start | bytes 196616 | tf_op jit(solution)/shard_map/ppermute | solution.py:21
  34.5 4.4 %collective-permute-start.16 = (bf16[4,64,128]{2,1,0:T(8,128)(2,1)S(1)}, bf16[4,64,128]{2,1,0:T(8,128)(2,1)S(1)}, u32[]{:S(2)}, u32[]{:S(2)}) collective-permute-start(bf16[4,64,128]{2,1,0:T(8,128)(2,1)S(1)} %get-tuple-element.52), channel_id=1, source_target_pairs={{0,8},{4,12},{8,0},{12,4},{1,9},{5,13},{9,1},{13,5},{2,10},{6,14},... | collective-permute-start | bytes 196616 | tf_op jit(solution)/shard_map/ppermute | solution.py:21

commit v6 on v5

--- a/solution.py
+++ b/solution.py
@@ -290,7 +290,7 @@
                 acc = swap_groups(acc, width, q)
                 pre = acc if pre is None else pre + acc
             up = u_ref[here].astype(F32)
-            squash = 1.0 / (1.0 + jnp.exp(-pre))
+            squash = 0.5 + 0.5 * jnp.tanh(0.5 * pre)
             slopes = squash * (1.0 + pre * (1.0 - squash))
             delta = (up * slopes).astype(BF16)
             d_ref[0, here] = delta

time: 39.9 us -> 39.9 us (level)
  no operation moved by 1% of the time
where the time goes in v6:
time: 39.9 us; the launch traced here: 39.7 us
  starting transfers between devices  21.1 us (53%)
  Pallas kernels  8.56 us (21%)
  waiting for transfers between devices  7.36 us (18%)
  local copies, waits for them, and re-layouts  1.84 us (5%)
  between operations  0.82 us (2%)
    ppermute x19, starting transfers between devices, fetch(): return lax.ppermute(x, axis, pairs)  21.1 us
    ppermute x19, waiting for transfers between devices, fetch(): return lax.ppermute(x, axis, pairs)  7.36 us
    pallas_call x1, Pallas kernels, volume_grad(): pl.pallas_call(body, in_specs=[pl.BlockSpec(memory_space=pltpu.VMEM)] * 2...  2.52 us
    pallas_call x1, Pallas kernels, patch_rows(): pl.pallas_call(body, in_specs=[pl.BlockSpec(memory_space=pltpu.VMEM)] + [...  2.37 us
    unnamed x4, local copies, waits for them, and re-layouts  1.84 us
    pallas_call x2, Pallas kernels, weight_part(): pl.pallas_call(body, out_shape=[jax.ShapeDtypeStruct((len(steps), kinds,...  0.87 us
    pallas_call x1, Pallas kernels, finish(): pl.pallas_call(body, out_shape=jax.ShapeDtypeStruct((kinds, block, width)...  0.81 us
  transfers between devices with their start and end apart: 19, of which 9 were waited for; matrix products, arithmetic and copies ran while one was open for 0% of the time, Pallas kernels for 16%

profile of v6, /device:TPU:0, one launch (start us, length us, event | category | flops | bytes accessed | tf_op | source)
XLA Modules:
  0.0 39.7 jit_solution(3558398515740239084)
XLA Ops:
  0.6 0.0 copy-start.1
  0.6 0.9 %copy-done.1 = bf16[8,64,64]{2,1,0:T(8,128)(2,1)S(1)} copy-done((bf16[8,64,64]{2,1,0:T(8,128)(2,1)S(1)}, bf16[8,64,64]{2,1,0:T(8,128)(2,1)}, u32[]{:S(2)}) %copy-start.1) | copy-done | bytes 65560
  1.5 0.1 pack_weight.1
  1.6 3.1 %collective-permute-start.2 = (bf16[4,64,128]{2,1,0:T(8,128)(2,1)S(1)}, bf16[4,64,128]{2,1,0:T(8,128)(2,1)S(1)}, u32[]{:S(2)}, u32[]{:S(2)}) collective-permute-start(bf16[4,64,128]{2,1,0:T(8,128)(2,1)S(1)} %get-tuple-element.29), channel_id=1, source_target_pairs={{0,1},{1,0},{2,3},{3,2},{4,5},{5,4},{6,7},{7,6},{8,9},{9,8},{10,11... | collective-permute-start | bytes 196616 | tf_op jit(solution)/shard_map/ppermute | solution.py:21
  4.7 2.6 %collective-permute-start = (bf16[4,64,128]{2,1,0:T(8,128)(2,1)S(1)}, bf16[4,64,128]{2,1,0:T(8,128)(2,1)S(1)}, u32[]{:S(2)}, u32[]{:S(2)}) collective-permute-start(bf16[4,64,128]{2,1,0:T(8,128)(2,1)S(1)} %get-tuple-element.28.refs_0_), channel_id=1, source_target_pairs={{0,2},{1,3},{2,0},{3,1},{4,6},{5,7},{6,4},{7,5},{8,10},{9,11},{10,... | collective-permute-start | bytes 196616 | tf_op jit(solution)/shard_map/ppermute | solution.py:21
  7.3 0.0 collective-permute-start.1
  7.3 0.0 collective-permute-done.2.refs_1_
  7.4 0.0 copy-start
  7.4 0.9 %copy-done = bf16[2,8,128,64]{2,3,1,0:T(8,128)(2,1)S(1)} copy-done((bf16[2,8,128,64]{2,3,1,0:T(8,128)(2,1)S(1)}, bf16[2,8,128,64]{2,3,1,0:T(8,128)(2,1)}, u32[]{:S(2)}) %copy-start) | copy-done | bytes 262168
  8.3 1.7 %collective-permute-start.3 = (bf16[4,64,128]{2,1,0:T(8,128)(2,1)S(1)}, bf16[4,64,128]{2,1,0:T(8,128)(2,1)S(1)}, u32[]{:S(2)}, u32[]{:S(2)}) collective-permute-start(bf16[4,64,128]{2,1,0:T(8,128)(2,1)S(1)} %get-tuple-element.32), channel_id=1, source_target_pairs={{0,1},{1,0},{2,3},{3,2},{4,5},{5,4},{6,7},{7,6},{8,9},{9,8},{10,11... | collective-permute-start | bytes 196616 | tf_op jit(solution)/shard_map/ppermute | solution.py:21
  10.1 3.2 %collective-permute-start.4 = (bf16[4,64,128]{2,1,0:T(8,128)(2,1)S(1)}, bf16[4,64,128]{2,1,0:T(8,128)(2,1)S(1)}, u32[]{:S(2)}, u32[]{:S(2)}) collective-permute-start(bf16[4,64,128]{2,1,0:T(8,128)(2,1)S(1)} %get-tuple-element.33), channel_id=1, source_target_pairs={{0,2},{1,3},{2,0},{3,1},{4,6},{5,7},{6,4},{7,5},{8,10},{9,11},{10,... | collective-permute-start | bytes 196616 | tf_op jit(solution)/shard_map/ppermute | solution.py:21
  13.3 0.0 collective-permute-start.5
  13.3 0.0 collective-permute-done.refs_0_
  13.3 1.5 %collective-permute-start.6 = (bf16[8,64,128]{2,1,0:T(8,128)(2,1)S(1)}, bf16[8,64,128]{2,1,0:T(8,128)(2,1)S(1)}, u32[]{:S(2)}, u32[]{:S(2)}) collective-permute-start(bf16[8,64,128]{2,1,0:T(8,128)(2,1)S(1)} %merge_tile.3.refs_0_.t_ref), channel_id=1, source_target_pairs={{0,8},{4,12},{8,0},{12,4},{1,9},{5,13},{9,1},{13,5},{2,10},{6,14},... | collective-permute-start | bytes 393224 | tf_op jit(solution)/shard_map/ppermute | solution.py:21
  14.8 0.0 collective-permute-done.1.refs_1_
  14.8 0.8 %collective-permute-start.7 = (bf16[8,64,128]{2,1,0:T(8,128)(2,1)S(1)}, bf16[8,64,128]{2,1,0:T(8,128)(2,1)S(1)}, u32[]{:S(2)}, u32[]{:S(2)}) collective-permute-start(bf16[8,64,128]{2,1,0:T(8,128)(2,1)S(1)} %merge_tile.2.refs_0_.t_ref.refs_1_), channel_id=1, source_target_pairs={{0,8},{4,12},{8,0},{12,4},{1,9},{5,13},{9,1},{13,5},{2,10},{6,14},... | collective-permute-start | bytes 393224 | tf_op jit(solution)/shard_map/ppermute | solution.py:21
  15.6 2.4 %patch_rows.1 = (bf16[8,512,256]{2,1,0:T(8,128)(2,1)S(1)}, bf16[8,256,512]{2,1,0:T(8,128)(2,1)S(1)}) custom-call(bf16[4,4,256,256]{3,2,1,0:T(8,128)(2,1)} %v_ref.1, bf16[8,64,128]{2,1,0:T(8,128)(2,1)S(1)} %merge_tile.2.refs_0_.t_ref.refs_1_), custom_call_target="tpu_custom_call" | custom-call | flops 536870912 | bytes 6291456 | tf_op jit(solution)/shard_map/patch_rows/pallas_call | solution.py:176
  18.1 0.0 collective-permute-done.3.refs_1_
  18.1 0.1 collective-permute-start.10
  18.1 0.0 collective-permute-done.4.refs_2_
  18.2 0.5 %collective-permute-start.11 = (bf16[8,64,128]{2,1,0:T(8,128)(2,1)S(1)}, bf16[8,64,128]{2,1,0:T(8,128)(2,1)S(1)}, u32[]{:S(2)}, u32[]{:S(2)}) collective-permute-start(bf16[8,64,128]{2,1,0:T(8,128)(2,1)S(1)} %gate.7), channel_id=1, source_target_pairs={{0,4},{4,0},{8,12},{12,8},{1,5},{5,1},{9,13},{13,9},{2,6},{6,2},{1... | collective-permute-start | bytes 393224 | tf_op jit(solution)/shard_map/ppermute | solution.py:21
  18.6 0.7 %collective-permute-done.5.refs_3_ = bf16[4,64,128]{2,1,0:T(8,128)(2,1)S(1)} collective-permute-done((bf16[4,64,128]{2,1,0:T(8,128)(2,1)S(1)}, bf16[4,64,128]{2,1,0:T(8,128)(2,1)S(1)}, u32[]{:S(2)}, u32[]{:S(2)}) %collective-permute-start.5) | collective-permute-done | bytes 65568 | tf_op jit(solution)/shard_map/ppermute | solution.py:21
  19.4 0.1 turn_cot.1.refs_0_.u_ref
  19.5 0.0 collective-permute-done.6.t_ref.refs_0_
  19.5 0.1 collective-permute-start.8
  19.6 0.3 collective-permute-done.7.t_ref.refs_1_
  19.9 0.3 collective-permute-start.9
  20.2 0.0 collective-permute-done.10.refs_2_
  20.2 0.0 collective-permute-done.11.refs_3_
  20.2 0.6 %forward_own.1 = (f32[512,256]{1,0:T(8,128)S(1)}, bf16[8,256,256]{2,1,0:T(8,128)(2,1)S(1)}) custom-call(bf16[8,512,256]{2,1,0:T(8,128)(2,1)S(1)} %get-tuple-element.30.refs_0_.p_ref, bf16[8,64,128]{2,1,0:T(8,128)(2,1)S(1)} %merge_tile.3.refs_0_.t_ref, bf16[8,64,128]{2,1,0:T(8,128)(2,1)S(1)} %merge_tile.2.refs_0_.t_ref.refs_1_, ...), custom_call_target="tpu_custom_call" | custom-call | flops 268435456 | bytes 2097152 | tf_op jit(solution)/shard_map/forward_own/pallas_call | solution.py:252
  20.8 0.1 collective-permute-done.8.refs_2_
  20.9 0.4 collective-permute-done.9.refs_3_
  21.3 0.7 %forward.1 = (bf16[2,512,256]{2,1,0:T(8,128)(2,1)S(1)}, bf16[8,256,256]{2,1,0:T(8,128)(2,1)S(1)}) custom-call(bf16[8,512,256]{2,1,0:T(8,128)(2,1)S(1)} %get-tuple-element.30.refs_0_.p_ref, bf16[512,256]{1,0:T(8,128)(2,1)S(1)} %turn_cot.1.refs_0_.u_ref, bf16[8,64,128]{2,1,0:T(8,128)(2,1)S(1)} %collective-permute-done.6.t_ref.refs_0_, ...), custom_call_target="tpu_custom_call", output_to_operand_aliasing={{1}: (7, {})} | custom-call | flops 536870912 | bytes 2097152 | tf_op jit(solution)/shard_map/forward/pallas_call | solution.py:301
  22.0 0.4 %weight_part.3 = (bf16[2,8,64,128]{3,2,1,0:T(8,128)(2,1)S(1)}, bf16[2,8,64,128]{3,2,1,0:T(8,128)(2,1)S(1)}) custom-call(bf16[8,256,512]{2,1,0:T(8,128)(2,1)S(1)} %get-tuple-element.40.t_ref, bf16[2,512,256]{2,1,0:T(8,128)(2,1)S(1)} %get-tuple-element.37.d_ref), custom_call_target="tpu_custom_call" | custom-call | flops 268435456 | bytes 2097152 | tf_op jit(solution)/shard_map/weight_part/pallas_call | solution.py:332
  22.5 0.3 collective-permute-start.13
  22.8 0.3 collective-permute-start.12
  23.0 0.4 %weight_part.2 = (f32[2,8,64,128]{3,2,1,0:T(8,128)S(1)}, f32[2,8,64,128]{3,2,1,0:T(8,128)S(1)}) custom-call(bf16[8,256,512]{2,1,0:T(8,128)(2,1)S(1)} %get-tuple-element.40.t_ref, bf16[2,512,256]{2,1,0:T(8,128)(2,1)S(1)} %get-tuple-element.37.d_ref), custom_call_target="tpu_custom_call" | custom-call | flops 268435456 | bytes 2097152 | tf_op jit(solution)/shard_map/weight_part/pallas_call | solution.py:332
  23.5 0.6 %collective-permute-done.13.b_ref = bf16[2,8,64,128]{3,2,1,0:T(8,128)(2,1)S(1)} collective-permute-done((bf16[2,8,64,128]{3,2,1,0:T(8,128)(2,1)S(1)}, bf16[2,8,64,128]{3,2,1,0:T(8,128)(2,1)S(1)}, u32[]{:S(2)}, u32[]{:S(2)}) %collective-permute-start.13) | collective-permute-done | bytes 262176 | tf_op jit(solution)/shard_map/ppermute | solution.py:21
  24.1 1.4 %collective-permute-start.15 = (bf16[8,64,128]{2,1,0:T(8,128)(2,1)S(1)}, bf16[8,64,128]{2,1,0:T(8,128)(2,1)S(1)}, u32[]{:S(2)}, u32[]{:S(2)}) collective-permute-start(bf16[8,64,128]{2,1,0:T(8,128)(2,1)S(1)} %get-tuple-element.45.refs_0_), channel_id=1, source_target_pairs={{0,8},{4,12},{8,0},{12,4},{1,9},{5,13},{9,1},{13,5},{2,10},{6,14},... | collective-permute-start | bytes 393224 | tf_op jit(solution)/shard_map/ppermute | solution.py:21
  25.5 2.5 %volume_grad.1 = (bf16[4,4,256,256]{3,2,1,0:T(8,128)(2,1)}, f32[8,128]{1,0:T(8,128)S(1)}) custom-call(bf16[2,512,256]{2,1,0:T(8,128)(2,1)S(1)} %get-tuple-element.37.d_ref, bf16[8,256,256]{2,1,0:T(8,128)(2,1)S(1)} %get-tuple-element.38.w_ref), custom_call_target="tpu_custom_call" | custom-call | flops 1073741824 | bytes 2097152 | tf_op jit(solution)/shard_map/volume_grad/pallas_call | solution.py:509
  28.1 0.0 collective-permute-done.12.b_ref
  28.1 0.1 add_core_near.1
  28.2 0.7 %collective-permute-start.14 = (bf16[8,64,128]{2,1,0:T(8,128)(2,1)S(1)}, bf16[8,64,128]{2,1,0:T(8,128)(2,1)S(1)}, u32[]{:S(2)}, u32[]{:S(2)}) collective-permute-start(bf16[8,64,128]{2,1,0:T(8,128)(2,1)S(1)} %get-tuple-element.48), channel_id=1, source_target_pairs={{0,1},{1,0},{2,3},{3,2},{4,5},{5,4},{6,7},{7,6},{8,9},{9,8},{10,11... | collective-permute-start | bytes 393224 | tf_op jit(solution)/shard_map/ppermute | solution.py:21
  28.9 0.9 %collective-permute-done.15.refs_1_ = bf16[8,64,128]{2,1,0:T(8,128)(2,1)S(1)} collective-permute-done((bf16[8,64,128]{2,1,0:T(8,128)(2,1)S(1)}, bf16[8,64,128]{2,1,0:T(8,128)(2,1)S(1)}, u32[]{:S(2)}, u32[]{:S(2)}) %collective-permute-start.15) | collective-permute-done | bytes 131104 | tf_op jit(solution)/shard_map/ppermute | solution.py:21
  29.8 0.1 add_and_pack.1
  29.9 2.8 %collective-permute-start.17 = (bf16[4,64,128]{2,1,0:T(8,128)(2,1)S(1)}, bf16[4,64,128]{2,1,0:T(8,128)(2,1)S(1)}, u32[]{:S(2)}, u32[]{:S(2)}) collective-permute-start(bf16[4,64,128]{2,1,0:T(8,128)(2,1)S(1)} %get-tuple-element.53), channel_id=1, source_target_pairs={{0,2},{1,3},{2,0},{3,1},{4,6},{5,7},{6,4},{7,5},{8,10},{9,11},{10,... | collective-permute-start | bytes 196616 | tf_op jit(solution)/shard_map/ppermute | solution.py:21
  32.8 1.0 %collective-permute-start.18 = (bf16[4,64,128]{2,1,0:T(8,128)(2,1)S(1)}, bf16[4,64,128]{2,1,0:T(8,128)(2,1)S(1)}, u32[]{:S(2)}, u32[]{:S(2)}) collective-permute-start(bf16[4,64,128]{2,1,0:T(8,128)(2,1)S(1)} %get-tuple-element.50.refs_2_), channel_id=1, source_target_pairs={{0,3},{1,2},{2,1},{3,0},{4,7},{5,6},{6,5},{7,4},{8,11},{9,10},{10,... | collective-permute-start | bytes 196616 | tf_op jit(solution)/shard_map/ppermute | solution.py:21
  33.8 0.6 %collective-permute-done.14.refs_1_ = bf16[8,64,128]{2,1,0:T(8,128)(2,1)S(1)} collective-permute-done((bf16[8,64,128]{2,1,0:T(8,128)(2,1)S(1)}, bf16[8,64,128]{2,1,0:T(8,128)(2,1)S(1)}, u32[]{:S(2)}, u32[]{:S(2)}) %collective-permute-start.14) | collective-permute-done | bytes 131104 | tf_op jit(solution)/shard_map/ppermute | solution.py:21
  34.5 0.7 %collective-permute-start.16 = (bf16[4,64,128]{2,1,0:T(8,128)(2,1)S(1)}, bf16[4,64,128]{2,1,0:T(8,128)(2,1)S(1)}, u32[]{:S(2)}, u32[]{:S(2)}) collective-permute-start(bf16[4,64,128]{2,1,0:T(8,128)(2,1)S(1)} %get-tuple-element.52), channel_id=1, source_target_pairs={{0,8},{4,12},{8,0},{12,4},{1,9},{5,13},{9,1},{13,5},{2,10},{6,14},... | collective-permute-start | bytes 196616 | tf_op jit(solution)/shard_map/ppermute | solution.py:21
  35.2 0.9 %collective-permute-done.17.refs_0_ = bf16[4,64,128]{2,1,0:T(8,128)(2,1)S(1)} collective-permute-done((bf16[4,64,128]{2,1,0:T(8,128)(2,1)S(1)}, bf16[4,64,128]{2,1,0:T(8,128)(2,1)S(1)}, u32[]{:S(2)}, u32[]{:S(2)}) %collective-permute-start.17) | collective-permute-done | bytes 65568 | tf_op jit(solution)/shard_map/ppermute | solution.py:21
  36.1 2.8 %collective-permute-done.18.refs_1_ = bf16[4,64,128]{2,1,0:T(8,128)(2,1)S(1)} collective-permute-done((bf16[4,64,128]{2,1,0:T(8,128)(2,1)S(1)}, bf16[4,64,128]{2,1,0:T(8,128)(2,1)S(1)}, u32[]{:S(2)}, u32[]{:S(2)}) %collective-permute-start.18) | collective-permute-done | bytes 65568 | tf_op jit(solution)/shard_map/ppermute | solution.py:21
  38.9 0.0 collective-permute-done.16.refs_1_
  38.9 0.8 %finish.1 = f32[8,64,64]{2,1,0:T(8,128)} custom-call(f32[4,64,128]{2,1,0:T(8,128)S(1)} %get-tuple-element.51.refs_0_, bf16[4,64,128]{2,1,0:T(8,128)(2,1)S(1)} %collective-permute-done.16.refs_1_, f32[4,64,128]{2,1,0:T(8,128)S(1)} %fold.1.refs_2_), custom_call_target="tpu_custom_call" | custom-call | tf_op jit(solution)/shard_map/finish/pallas_call | solution.py:463
  (10 shorter events, 0.2 us)
Async XLA Ops:
  0.6 0.9 %copy-start.1 = (bf16[8,64,64]{2,1,0:T(8,128)(2,1)S(1)}, bf16[8,64,64]{2,1,0:T(8,128)(2,1)}, u32[]{:S(2)}) copy-start(bf16[8,64,64]{2,1,0:T(8,128)(2,1)} %w_ref.1) | copy-start | bytes 196612
  1.6 5.7 %collective-permute-start.2 = (bf16[4,64,128]{2,1,0:T(8,128)(2,1)S(1)}, bf16[4,64,128]{2,1,0:T(8,128)(2,1)S(1)}, u32[]{:S(2)}, u32[]{:S(2)}) collective-permute-start(bf16[4,64,128]{2,1,0:T(8,128)(2,1)S(1)} %get-tuple-element.29), channel_id=1, source_target_pairs={{0,1},{1,0},{2,3},{3,2},{4,5},{5,4},{6,7},{7,6},{8,9},{9,8},{10,11... | collective-permute-start | bytes 196616 | tf_op jit(solution)/shard_map/ppermute | solution.py:21
  4.7 8.6 %collective-permute-start = (bf16[4,64,128]{2,1,0:T(8,128)(2,1)S(1)}, bf16[4,64,128]{2,1,0:T(8,128)(2,1)S(1)}, u32[]{:S(2)}, u32[]{:S(2)}) collective-permute-start(bf16[4,64,128]{2,1,0:T(8,128)(2,1)S(1)} %get-tuple-element.28.refs_0_), channel_id=1, source_target_pairs={{0,2},{1,3},{2,0},{3,1},{4,6},{5,7},{6,4},{7,5},{8,10},{9,11},{10,... | collective-permute-start | bytes 196616 | tf_op jit(solution)/shard_map/ppermute | solution.py:21
  7.3 7.5 %collective-permute-start.1 = (bf16[4,64,128]{2,1,0:T(8,128)(2,1)S(1)}, bf16[4,64,128]{2,1,0:T(8,128)(2,1)S(1)}, u32[]{:S(2)}, u32[]{:S(2)}) collective-permute-start(bf16[4,64,128]{2,1,0:T(8,128)(2,1)S(1)} %get-tuple-element.29), channel_id=1, source_target_pairs={{0,3},{1,2},{2,1},{3,0},{4,7},{5,6},{6,5},{7,4},{8,11},{9,10},{10,... | collective-permute-start | bytes 196616 | tf_op jit(solution)/shard_map/ppermute | solution.py:21
  7.4 1.0 %copy-start = (bf16[2,8,128,64]{2,3,1,0:T(8,128)(2,1)S(1)}, bf16[2,8,128,64]{2,3,1,0:T(8,128)(2,1)}, u32[]{:S(2)}) copy-start(bf16[2,8,128,64]{2,3,1,0:T(8,128)(2,1)} %param.5) | copy-start | bytes 786436
  8.3 9.7 %collective-permute-start.3 = (bf16[4,64,128]{2,1,0:T(8,128)(2,1)S(1)}, bf16[4,64,128]{2,1,0:T(8,128)(2,1)S(1)}, u32[]{:S(2)}, u32[]{:S(2)}) collective-permute-start(bf16[4,64,128]{2,1,0:T(8,128)(2,1)S(1)} %get-tuple-element.32), channel_id=1, source_target_pairs={{0,1},{1,0},{2,3},{3,2},{4,5},{5,4},{6,7},{7,6},{8,9},{9,8},{10,11... | collective-permute-start | bytes 196616 | tf_op jit(solution)/shard_map/ppermute | solution.py:21
  10.1 8.1 %collective-permute-start.4 = (bf16[4,64,128]{2,1,0:T(8,128)(2,1)S(1)}, bf16[4,64,128]{2,1,0:T(8,128)(2,1)S(1)}, u32[]{:S(2)}, u32[]{:S(2)}) collective-permute-start(bf16[4,64,128]{2,1,0:T(8,128)(2,1)S(1)} %get-tuple-element.33), channel_id=1, source_target_pairs={{0,2},{1,3},{2,0},{3,1},{4,6},{5,7},{6,4},{7,5},{8,10},{9,11},{10,... | collective-permute-start | bytes 196616 | tf_op jit(solution)/shard_map/ppermute | solution.py:21
  13.3 6.1 %collective-permute-start.5 = (bf16[4,64,128]{2,1,0:T(8,128)(2,1)S(1)}, bf16[4,64,128]{2,1,0:T(8,128)(2,1)S(1)}, u32[]{:S(2)}, u32[]{:S(2)}) collective-permute-start(bf16[4,64,128]{2,1,0:T(8,128)(2,1)S(1)} %get-tuple-element.34), channel_id=1, source_target_pairs={{0,3},{1,2},{2,1},{3,0},{4,7},{5,6},{6,5},{7,4},{8,11},{9,10},{10,... | collective-permute-start | bytes 196616 | tf_op jit(solution)/shard_map/ppermute | solution.py:21
  13.3 6.2 %collective-permute-start.6 = (bf16[8,64,128]{2,1,0:T(8,128)(2,1)S(1)}, bf16[8,64,128]{2,1,0:T(8,128)(2,1)S(1)}, u32[]{:S(2)}, u32[]{:S(2)}) collective-permute-start(bf16[8,64,128]{2,1,0:T(8,128)(2,1)S(1)} %merge_tile.3.refs_0_.t_ref), channel_id=1, source_target_pairs={{0,8},{4,12},{8,0},{12,4},{1,9},{5,13},{9,1},{13,5},{2,10},{6,14},... | collective-permute-start | bytes 393224 | tf_op jit(solution)/shard_map/ppermute | solution.py:21
  14.8 5.0 %collective-permute-start.7 = (bf16[8,64,128]{2,1,0:T(8,128)(2,1)S(1)}, bf16[8,64,128]{2,1,0:T(8,128)(2,1)S(1)}, u32[]{:S(2)}, u32[]{:S(2)}) collective-permute-start(bf16[8,64,128]{2,1,0:T(8,128)(2,1)S(1)} %merge_tile.2.refs_0_.t_ref.refs_1_), channel_id=1, source_target_pairs={{0,8},{4,12},{8,0},{12,4},{1,9},{5,13},{9,1},{13,5},{2,10},{6,14},... | collective-permute-start | bytes 393224 | tf_op jit(solution)/shard_map/ppermute | solution.py:21
  18.1 2.1 %collective-permute-start.10 = (bf16[8,64,128]{2,1,0:T(8,128)(2,1)S(1)}, bf16[8,64,128]{2,1,0:T(8,128)(2,1)S(1)}, u32[]{:S(2)}, u32[]{:S(2)}) collective-permute-start(bf16[8,64,128]{2,1,0:T(8,128)(2,1)S(1)} %gate.6), channel_id=1, source_target_pairs={{0,4},{4,0},{8,12},{12,8},{1,5},{5,1},{9,13},{13,9},{2,6},{6,2},{1... | collective-permute-start | bytes 393224 | tf_op jit(solution)/shard_map/ppermute | solution.py:21
  18.2 2.0 %collective-permute-start.11 = (bf16[8,64,128]{2,1,0:T(8,128)(2,1)S(1)}, bf16[8,64,128]{2,1,0:T(8,128)(2,1)S(1)}, u32[]{:S(2)}, u32[]{:S(2)}) collective-permute-start(bf16[8,64,128]{2,1,0:T(8,128)(2,1)S(1)} %gate.7), channel_id=1, source_target_pairs={{0,4},{4,0},{8,12},{12,8},{1,5},{5,1},{9,13},{13,9},{2,6},{6,2},{1... | collective-permute-start | bytes 393224 | tf_op jit(solution)/shard_map/ppermute | solution.py:21
  19.5 1.4 %collective-permute-start.8 = (bf16[8,64,128]{2,1,0:T(8,128)(2,1)S(1)}, bf16[8,64,128]{2,1,0:T(8,128)(2,1)S(1)}, u32[]{:S(2)}, u32[]{:S(2)}) collective-permute-start(bf16[8,64,128]{2,1,0:T(8,128)(2,1)S(1)} %gate.4), channel_id=1, source_target_pairs={{0,4},{4,0},{8,12},{12,8},{1,5},{5,1},{9,13},{13,9},{2,6},{6,2},{1... | collective-permute-start | bytes 393224 | tf_op jit(solution)/shard_map/ppermute | solution.py:21
  19.9 1.4 %collective-permute-start.9 = (bf16[8,64,128]{2,1,0:T(8,128)(2,1)S(1)}, bf16[8,64,128]{2,1,0:T(8,128)(2,1)S(1)}, u32[]{:S(2)}, u32[]{:S(2)}) collective-permute-start(bf16[8,64,128]{2,1,0:T(8,128)(2,1)S(1)} %gate.5), channel_id=1, source_target_pairs={{0,4},{4,0},{8,12},{12,8},{1,5},{5,1},{9,13},{13,9},{2,6},{6,2},{1... | collective-permute-start | bytes 393224 | tf_op jit(solution)/shard_map/ppermute | solution.py:21
  22.5 1.6 %collective-permute-start.13 = (bf16[2,8,64,128]{3,2,1,0:T(8,128)(2,1)S(1)}, bf16[2,8,64,128]{3,2,1,0:T(8,128)(2,1)S(1)}, u32[]{:S(2)}, u32[]{:S(2)}) collective-permute-start(bf16[2,8,64,128]{3,2,1,0:T(8,128)(2,1)S(1)} %get-tuple-element.44), channel_id=1, source_target_pairs={{0,4},{4,0},{8,12},{12,8},{1,5},{5,1},{9,13},{13,9},{2,6},{6,2},{1... | collective-permute-start | bytes 786440 | tf_op jit(solution)/shard_map/ppermute | solution.py:21
  22.8 5.3 %collective-permute-start.12 = (bf16[2,8,64,128]{3,2,1,0:T(8,128)(2,1)S(1)}, bf16[2,8,64,128]{3,2,1,0:T(8,128)(2,1)S(1)}, u32[]{:S(2)}, u32[]{:S(2)}) collective-permute-start(bf16[2,8,64,128]{3,2,1,0:T(8,128)(2,1)S(1)} %get-tuple-element.42), channel_id=1, source_target_pairs={{0,4},{4,0},{8,12},{12,8},{1,5},{5,1},{9,13},{13,9},{2,6},{6,2},{1... | collective-permute-start | bytes 786440 | tf_op jit(solution)/shard_map/ppermute | solution.py:21
  24.1 5.7 %collective-permute-start.15 = (bf16[8,64,128]{2,1,0:T(8,128)(2,1)S(1)}, bf16[8,64,128]{2,1,0:T(8,128)(2,1)S(1)}, u32[]{:S(2)}, u32[]{:S(2)}) collective-permute-start(bf16[8,64,128]{2,1,0:T(8,128)(2,1)S(1)} %get-tuple-element.45.refs_0_), channel_id=1, source_target_pairs={{0,8},{4,12},{8,0},{12,4},{1,9},{5,13},{9,1},{13,5},{2,10},{6,14},... | collective-permute-start | bytes 393224 | tf_op jit(solution)/shard_map/ppermute | solution.py:21
  28.2 6.2 %collective-permute-start.14 = (bf16[8,64,128]{2,1,0:T(8,128)(2,1)S(1)}, bf16[8,64,128]{2,1,0:T(8,128)(2,1)S(1)}, u32[]{:S(2)}, u32[]{:S(2)}) collective-permute-start(bf16[8,64,128]{2,1,0:T(8,128)(2,1)S(1)} %get-tuple-element.48), channel_id=1, source_target_pairs={{0,1},{1,0},{2,3},{3,2},{4,5},{5,4},{6,7},{7,6},{8,9},{9,8},{10,11... | collective-permute-start | bytes 393224 | tf_op jit(solution)/shard_map/ppermute | solution.py:21
  29.9 6.1 %collective-permute-start.17 = (bf16[4,64,128]{2,1,0:T(8,128)(2,1)S(1)}, bf16[4,64,128]{2,1,0:T(8,128)(2,1)S(1)}, u32[]{:S(2)}, u32[]{:S(2)}) collective-permute-start(bf16[4,64,128]{2,1,0:T(8,128)(2,1)S(1)} %get-tuple-element.53), channel_id=1, source_target_pairs={{0,2},{1,3},{2,0},{3,1},{4,6},{5,7},{6,4},{7,5},{8,10},{9,11},{10,... | collective-permute-start | bytes 196616 | tf_op jit(solution)/shard_map/ppermute | solution.py:21
  32.8 6.1 %collective-permute-start.18 = (bf16[4,64,128]{2,1,0:T(8,128)(2,1)S(1)}, bf16[4,64,128]{2,1,0:T(8,128)(2,1)S(1)}, u32[]{:S(2)}, u32[]{:S(2)}) collective-permute-start(bf16[4,64,128]{2,1,0:T(8,128)(2,1)S(1)} %get-tuple-element.50.refs_2_), channel_id=1, source_target_pairs={{0,3},{1,2},{2,1},{3,0},{4,7},{5,6},{6,5},{7,4},{8,11},{9,10},{10,... | collective-permute-start | bytes 196616 | tf_op jit(solution)/shard_map/ppermute | solution.py:21
  34.5 4.4 %collective-permute-start.16 = (bf16[4,64,128]{2,1,0:T(8,128)(2,1)S(1)}, bf16[4,64,128]{2,1,0:T(8,128)(2,1)S(1)}, u32[]{:S(2)}, u32[]{:S(2)}) collective-permute-start(bf16[4,64,128]{2,1,0:T(8,128)(2,1)S(1)} %get-tuple-element.52), channel_id=1, source_target_pairs={{0,8},{4,12},{8,0},{12,4},{1,9},{5,13},{9,1},{13,5},{2,10},{6,14},... | collective-permute-start | bytes 196616 | tf_op jit(solution)/shard_map/ppermute | solution.py:21

commit v7 on v5

--- a/solution.py
+++ b/solution.py
@@ -241,8 +241,8 @@
         pre_ref, w_ref = refs[-2:]
         me = lax.axis_index("space")
         place(w_ref, refs[:-2], me, 0, tiles)
-        for first in range(0, rows, rows // 2):
-            here = slice(first, first + rows // 2)
+        for first in range(0, rows, rows // 4):
+            here = slice(first, first + rows // 4)
             pre = None
             for q in range(ratio):
                 acc = swap_groups(chip_part(p_ref, w_ref, here, me, 0, block, ratio, q), width, q)

time: 39.9 us -> 39.9 us (level)
  no operation moved by 1% of the time
where the time goes in v7:
time: 39.9 us; the launch traced here: 39.7 us
  starting transfers between devices  21.1 us (53%)
  Pallas kernels  8.56 us (21%)
  waiting for transfers between devices  7.41 us (19%)
  local copies, waits for them, and re-layouts  1.84 us (5%)
  between operations  0.82 us (2%)
    ppermute x19, starting transfers between devices, fetch(): return lax.ppermute(x, axis, pairs)  21.1 us
    ppermute x19, waiting for transfers between devices, fetch(): return lax.ppermute(x, axis, pairs)  7.41 us
    pallas_call x1, Pallas kernels, volume_grad(): pl.pallas_call(body, in_specs=[pl.BlockSpec(memory_space=pltpu.VMEM)] * 2...  2.52 us
    pallas_call x1, Pallas kernels, patch_rows(): pl.pallas_call(body, in_specs=[pl.BlockSpec(memory_space=pltpu.VMEM)] + [...  2.37 us
    unnamed x4, local copies, waits for them, and re-layouts  1.84 us
    pallas_call x2, Pallas kernels, weight_part(): pl.pallas_call(body, out_shape=[jax.ShapeDtypeStruct((len(steps), kinds,...  0.86 us
    pallas_call x1, Pallas kernels, finish(): pl.pallas_call(body, out_shape=jax.ShapeDtypeStruct((kinds, block, width)...  0.81 us
  transfers between devices with their start and end apart: 19, of which 9 were waited for; matrix products, arithmetic and copies ran while one was open for 0% of the time, Pallas kernels for 16%

profile of v7, /device:TPU:0, one launch (start us, length us, event | category | flops | bytes accessed | tf_op | source)
XLA Modules:
  0.0 39.7 jit_solution(3928160267348467028)
XLA Ops:
  0.6 0.0 copy-start.1
  0.6 0.9 %copy-done.1 = bf16[8,64,64]{2,1,0:T(8,128)(2,1)S(1)} copy-done((bf16[8,64,64]{2,1,0:T(8,128)(2,1)S(1)}, bf16[8,64,64]{2,1,0:T(8,128)(2,1)}, u32[]{:S(2)}) %copy-start.1) | copy-done | bytes 65560
  1.5 0.1 pack_weight.1
  1.6 3.1 %collective-permute-start.2 = (bf16[4,64,128]{2,1,0:T(8,128)(2,1)S(1)}, bf16[4,64,128]{2,1,0:T(8,128)(2,1)S(1)}, u32[]{:S(2)}, u32[]{:S(2)}) collective-permute-start(bf16[4,64,128]{2,1,0:T(8,128)(2,1)S(1)} %get-tuple-element.29), channel_id=1, source_target_pairs={{0,1},{1,0},{2,3},{3,2},{4,5},{5,4},{6,7},{7,6},{8,9},{9,8},{10,11... | collective-permute-start | bytes 196616 | tf_op jit(solution)/shard_map/ppermute | solution.py:21
  4.7 2.6 %collective-permute-start = (bf16[4,64,128]{2,1,0:T(8,128)(2,1)S(1)}, bf16[4,64,128]{2,1,0:T(8,128)(2,1)S(1)}, u32[]{:S(2)}, u32[]{:S(2)}) collective-permute-start(bf16[4,64,128]{2,1,0:T(8,128)(2,1)S(1)} %get-tuple-element.28.refs_0_), channel_id=1, source_target_pairs={{0,2},{1,3},{2,0},{3,1},{4,6},{5,7},{6,4},{7,5},{8,10},{9,11},{10,... | collective-permute-start | bytes 196616 | tf_op jit(solution)/shard_map/ppermute | solution.py:21
  7.3 0.0 collective-permute-start.1
  7.3 0.0 collective-permute-done.2.refs_1_
  7.4 0.0 copy-start
  7.4 0.9 %copy-done = bf16[2,8,128,64]{2,3,1,0:T(8,128)(2,1)S(1)} copy-done((bf16[2,8,128,64]{2,3,1,0:T(8,128)(2,1)S(1)}, bf16[2,8,128,64]{2,3,1,0:T(8,128)(2,1)}, u32[]{:S(2)}) %copy-start) | copy-done | bytes 262168
  8.3 1.7 %collective-permute-start.3 = (bf16[4,64,128]{2,1,0:T(8,128)(2,1)S(1)}, bf16[4,64,128]{2,1,0:T(8,128)(2,1)S(1)}, u32[]{:S(2)}, u32[]{:S(2)}) collective-permute-start(bf16[4,64,128]{2,1,0:T(8,128)(2,1)S(1)} %get-tuple-element.32), channel_id=1, source_target_pairs={{0,1},{1,0},{2,3},{3,2},{4,5},{5,4},{6,7},{7,6},{8,9},{9,8},{10,11... | collective-permute-start | bytes 196616 | tf_op jit(solution)/shard_map/ppermute | solution.py:21
  10.1 3.2 %collective-permute-start.4 = (bf16[4,64,128]{2,1,0:T(8,128)(2,1)S(1)}, bf16[4,64,128]{2,1,0:T(8,128)(2,1)S(1)}, u32[]{:S(2)}, u32[]{:S(2)}) collective-permute-start(bf16[4,64,128]{2,1,0:T(8,128)(2,1)S(1)} %get-tuple-element.33), channel_id=1, source_target_pairs={{0,2},{1,3},{2,0},{3,1},{4,6},{5,7},{6,4},{7,5},{8,10},{9,11},{10,... | collective-permute-start | bytes 196616 | tf_op jit(solution)/shard_map/ppermute | solution.py:21
  13.3 0.0 collective-permute-start.5
  13.3 0.0 collective-permute-done.refs_0_
  13.3 1.5 %collective-permute-start.6 = (bf16[8,64,128]{2,1,0:T(8,128)(2,1)S(1)}, bf16[8,64,128]{2,1,0:T(8,128)(2,1)S(1)}, u32[]{:S(2)}, u32[]{:S(2)}) collective-permute-start(bf16[8,64,128]{2,1,0:T(8,128)(2,1)S(1)} %merge_tile.3.refs_0_.t_ref), channel_id=1, source_target_pairs={{0,8},{4,12},{8,0},{12,4},{1,9},{5,13},{9,1},{13,5},{2,10},{6,14},... | collective-permute-start | bytes 393224 | tf_op jit(solution)/shard_map/ppermute | solution.py:21
  14.8 0.0 collective-permute-done.1.refs_1_
  14.8 0.8 %collective-permute-start.7 = (bf16[8,64,128]{2,1,0:T(8,128)(2,1)S(1)}, bf16[8,64,128]{2,1,0:T(8,128)(2,1)S(1)}, u32[]{:S(2)}, u32[]{:S(2)}) collective-permute-start(bf16[8,64,128]{2,1,0:T(8,128)(2,1)S(1)} %merge_tile.2.refs_0_.t_ref.refs_1_), channel_id=1, source_target_pairs={{0,8},{4,12},{8,0},{12,4},{1,9},{5,13},{9,1},{13,5},{2,10},{6,14},... | collective-permute-start | bytes 393224 | tf_op jit(solution)/shard_map/ppermute | solution.py:21
  15.6 2.4 %patch_rows.1 = (bf16[8,512,256]{2,1,0:T(8,128)(2,1)S(1)}, bf16[8,256,512]{2,1,0:T(8,128)(2,1)S(1)}) custom-call(bf16[4,4,256,256]{3,2,1,0:T(8,128)(2,1)} %v_ref.1, bf16[8,64,128]{2,1,0:T(8,128)(2,1)S(1)} %merge_tile.2.refs_0_.t_ref.refs_1_), custom_call_target="tpu_custom_call" | custom-call | flops 536870912 | bytes 6291456 | tf_op jit(solution)/shard_map/patch_rows/pallas_call | solution.py:176
  18.1 0.0 collective-permute-done.3.refs_1_
  18.1 0.1 collective-permute-start.10
  18.1 0.0 collective-permute-done.4.refs_2_
  18.2 0.5 %collective-permute-start.11 = (bf16[8,64,128]{2,1,0:T(8,128)(2,1)S(1)}, bf16[8,64,128]{2,1,0:T(8,128)(2,1)S(1)}, u32[]{:S(2)}, u32[]{:S(2)}) collective-permute-start(bf16[8,64,128]{2,1,0:T(8,128)(2,1)S(1)} %gate.7), channel_id=1, source_target_pairs={{0,4},{4,0},{8,12},{12,8},{1,5},{5,1},{9,13},{13,9},{2,6},{6,2},{1... | collective-permute-start | bytes 393224 | tf_op jit(solution)/shard_map/ppermute | solution.py:21
  18.6 0.7 %collective-permute-done.5.refs_3_ = bf16[4,64,128]{2,1,0:T(8,128)(2,1)S(1)} collective-permute-done((bf16[4,64,128]{2,1,0:T(8,128)(2,1)S(1)}, bf16[4,64,128]{2,1,0:T(8,128)(2,1)S(1)}, u32[]{:S(2)}, u32[]{:S(2)}) %collective-permute-start.5) | collective-permute-done | bytes 65568 | tf_op jit(solution)/shard_map/ppermute | solution.py:21
  19.4 0.1 turn_cot.1.refs_0_.u_ref
  19.5 0.0 collective-permute-done.6.t_ref.refs_0_
  19.5 0.1 collective-permute-start.8
  19.6 0.3 collective-permute-done.7.t_ref.refs_1_
  19.9 0.3 collective-permute-start.9
  20.2 0.0 collective-permute-done.10.refs_2_
  20.2 0.0 collective-permute-done.11.refs_3_
  20.2 0.6 %forward_own.1 = (f32[512,256]{1,0:T(8,128)S(1)}, bf16[8,256,256]{2,1,0:T(8,128)(2,1)S(1)}) custom-call(bf16[8,512,256]{2,1,0:T(8,128)(2,1)S(1)} %get-tuple-element.30.refs_0_.p_ref, bf16[8,64,128]{2,1,0:T(8,128)(2,1)S(1)} %merge_tile.3.refs_0_.t_ref, bf16[8,64,128]{2,1,0:T(8,128)(2,1)S(1)} %merge_tile.2.refs_0_.t_ref.refs_1_, ...), custom_call_target="tpu_custom_call" | custom-call | flops 268435456 | bytes 2097152 | tf_op jit(solution)/shard_map/forward_own/pallas_call | solution.py:252
  20.8 0.1 collective-permute-done.8.refs_2_
  20.9 0.4 collective-permute-done.9.refs_3_
  21.3 0.7 %forward.1 = (bf16[2,512,256]{2,1,0:T(8,128)(2,1)S(1)}, bf16[8,256,256]{2,1,0:T(8,128)(2,1)S(1)}) custom-call(bf16[8,512,256]{2,1,0:T(8,128)(2,1)S(1)} %get-tuple-element.30.refs_0_.p_ref, bf16[512,256]{1,0:T(8,128)(2,1)S(1)} %turn_cot.1.refs_0_.u_ref, bf16[8,64,128]{2,1,0:T(8,128)(2,1)S(1)} %collective-permute-done.6.t_ref.refs_0_, ...), custom_call_target="tpu_custom_call", output_to_operand_aliasing={{1}: (7, {})} | custom-call | flops 536870912 | bytes 2097152 | tf_op jit(solution)/shard_map/forward/pallas_call | solution.py:301
  22.0 0.4 %weight_part.3 = (bf16[2,8,64,128]{3,2,1,0:T(8,128)(2,1)S(1)}, bf16[2,8,64,128]{3,2,1,0:T(8,128)(2,1)S(1)}) custom-call(bf16[8,256,512]{2,1,0:T(8,128)(2,1)S(1)} %get-tuple-element.40.t_ref, bf16[2,512,256]{2,1,0:T(8,128)(2,1)S(1)} %get-tuple-element.37.d_ref), custom_call_target="tpu_custom_call" | custom-call | flops 268435456 | bytes 2097152 | tf_op jit(solution)/shard_map/weight_part/pallas_call | solution.py:332
  22.5 0.3 collective-permute-start.13
  22.8 0.3 collective-permute-start.12
  23.0 0.4 %weight_part.2 = (f32[2,8,64,128]{3,2,1,0:T(8,128)S(1)}, f32[2,8,64,128]{3,2,1,0:T(8,128)S(1)}) custom-call(bf16[8,256,512]{2,1,0:T(8,128)(2,1)S(1)} %get-tuple-element.40.t_ref, bf16[2,512,256]{2,1,0:T(8,128)(2,1)S(1)} %get-tuple-element.37.d_ref), custom_call_target="tpu_custom_call" | custom-call | flops 268435456 | bytes 2097152 | tf_op jit(solution)/shard_map/weight_part/pallas_call | solution.py:332
  23.5 0.6 %collective-permute-done.13.b_ref = bf16[2,8,64,128]{3,2,1,0:T(8,128)(2,1)S(1)} collective-permute-done((bf16[2,8,64,128]{3,2,1,0:T(8,128)(2,1)S(1)}, bf16[2,8,64,128]{3,2,1,0:T(8,128)(2,1)S(1)}, u32[]{:S(2)}, u32[]{:S(2)}) %collective-permute-start.13) | collective-permute-done | bytes 262176 | tf_op jit(solution)/shard_map/ppermute | solution.py:21
  24.1 1.4 %collective-permute-start.15 = (bf16[8,64,128]{2,1,0:T(8,128)(2,1)S(1)}, bf16[8,64,128]{2,1,0:T(8,128)(2,1)S(1)}, u32[]{:S(2)}, u32[]{:S(2)}) collective-permute-start(bf16[8,64,128]{2,1,0:T(8,128)(2,1)S(1)} %get-tuple-element.45.refs_0_), channel_id=1, source_target_pairs={{0,8},{4,12},{8,0},{12,4},{1,9},{5,13},{9,1},{13,5},{2,10},{6,14},... | collective-permute-start | bytes 393224 | tf_op jit(solution)/shard_map/ppermute | solution.py:21
  25.6 2.5 %volume_grad.1 = (bf16[4,4,256,256]{3,2,1,0:T(8,128)(2,1)}, f32[8,128]{1,0:T(8,128)S(1)}) custom-call(bf16[2,512,256]{2,1,0:T(8,128)(2,1)S(1)} %get-tuple-element.37.d_ref, bf16[8,256,256]{2,1,0:T(8,128)(2,1)S(1)} %get-tuple-element.38.w_ref), custom_call_target="tpu_custom_call" | custom-call | flops 1073741824 | bytes 2097152 | tf_op jit(solution)/shard_map/volume_grad/pallas_call | solution.py:509
  28.1 0.0 collective-permute-done.12.b_ref
  28.1 0.1 add_core_near.1
  28.2 0.7 %collective-permute-start.14 = (bf16[8,64,128]{2,1,0:T(8,128)(2,1)S(1)}, bf16[8,64,128]{2,1,0:T(8,128)(2,1)S(1)}, u32[]{:S(2)}, u32[]{:S(2)}) collective-permute-start(bf16[8,64,128]{2,1,0:T(8,128)(2,1)S(1)} %get-tuple-element.48), channel_id=1, source_target_pairs={{0,1},{1,0},{2,3},{3,2},{4,5},{5,4},{6,7},{7,6},{8,9},{9,8},{10,11... | collective-permute-start | bytes 393224 | tf_op jit(solution)/shard_map/ppermute | solution.py:21
  28.9 0.9 %collective-permute-done.15.refs_1_ = bf16[8,64,128]{2,1,0:T(8,128)(2,1)S(1)} collective-permute-done((bf16[8,64,128]{2,1,0:T(8,128)(2,1)S(1)}, bf16[8,64,128]{2,1,0:T(8,128)(2,1)S(1)}, u32[]{:S(2)}, u32[]{:S(2)}) %collective-permute-start.15) | collective-permute-done | bytes 131104 | tf_op jit(solution)/shard_map/ppermute | solution.py:21
  29.8 0.1 add_and_pack.1
  29.9 2.9 %collective-permute-start.17 = (bf16[4,64,128]{2,1,0:T(8,128)(2,1)S(1)}, bf16[4,64,128]{2,1,0:T(8,128)(2,1)S(1)}, u32[]{:S(2)}, u32[]{:S(2)}) collective-permute-start(bf16[4,64,128]{2,1,0:T(8,128)(2,1)S(1)} %get-tuple-element.53), channel_id=1, source_target_pairs={{0,2},{1,3},{2,0},{3,1},{4,6},{5,7},{6,4},{7,5},{8,10},{9,11},{10,... | collective-permute-start | bytes 196616 | tf_op jit(solution)/shard_map/ppermute | solution.py:21
  32.8 1.0 %collective-permute-start.18 = (bf16[4,64,128]{2,1,0:T(8,128)(2,1)S(1)}, bf16[4,64,128]{2,1,0:T(8,128)(2,1)S(1)}, u32[]{:S(2)}, u32[]{:S(2)}) collective-permute-start(bf16[4,64,128]{2,1,0:T(8,128)(2,1)S(1)} %get-tuple-element.50.refs_2_), channel_id=1, source_target_pairs={{0,3},{1,2},{2,1},{3,0},{4,7},{5,6},{6,5},{7,4},{8,11},{9,10},{10,... | collective-permute-start | bytes 196616 | tf_op jit(solution)/shard_map/ppermute | solution.py:21
  33.8 0.7 %collective-permute-done.14.refs_1_ = bf16[8,64,128]{2,1,0:T(8,128)(2,1)S(1)} collective-permute-done((bf16[8,64,128]{2,1,0:T(8,128)(2,1)S(1)}, bf16[8,64,128]{2,1,0:T(8,128)(2,1)S(1)}, u32[]{:S(2)}, u32[]{:S(2)}) %collective-permute-start.14) | collective-permute-done | bytes 131104 | tf_op jit(solution)/shard_map/ppermute | solution.py:21
  34.5 0.7 %collective-permute-start.16 = (bf16[4,64,128]{2,1,0:T(8,128)(2,1)S(1)}, bf16[4,64,128]{2,1,0:T(8,128)(2,1)S(1)}, u32[]{:S(2)}, u32[]{:S(2)}) collective-permute-start(bf16[4,64,128]{2,1,0:T(8,128)(2,1)S(1)} %get-tuple-element.52), channel_id=1, source_target_pairs={{0,8},{4,12},{8,0},{12,4},{1,9},{5,13},{9,1},{13,5},{2,10},{6,14},... | collective-permute-start | bytes 196616 | tf_op jit(solution)/shard_map/ppermute | solution.py:21
  35.2 0.9 %collective-permute-done.17.refs_0_ = bf16[4,64,128]{2,1,0:T(8,128)(2,1)S(1)} collective-permute-done((bf16[4,64,128]{2,1,0:T(8,128)(2,1)S(1)}, bf16[4,64,128]{2,1,0:T(8,128)(2,1)S(1)}, u32[]{:S(2)}, u32[]{:S(2)}) %collective-permute-start.17) | collective-permute-done | bytes 65568 | tf_op jit(solution)/shard_map/ppermute | solution.py:21
  36.1 2.8 %collective-permute-done.18.refs_1_ = bf16[4,64,128]{2,1,0:T(8,128)(2,1)S(1)} collective-permute-done((bf16[4,64,128]{2,1,0:T(8,128)(2,1)S(1)}, bf16[4,64,128]{2,1,0:T(8,128)(2,1)S(1)}, u32[]{:S(2)}, u32[]{:S(2)}) %collective-permute-start.18) | collective-permute-done | bytes 65568 | tf_op jit(solution)/shard_map/ppermute | solution.py:21
  38.9 0.0 collective-permute-done.16.refs_1_
  38.9 0.8 %finish.1 = f32[8,64,64]{2,1,0:T(8,128)} custom-call(f32[4,64,128]{2,1,0:T(8,128)S(1)} %get-tuple-element.51.refs_0_, bf16[4,64,128]{2,1,0:T(8,128)(2,1)S(1)} %collective-permute-done.16.refs_1_, f32[4,64,128]{2,1,0:T(8,128)S(1)} %fold.1.refs_2_), custom_call_target="tpu_custom_call" | custom-call | tf_op jit(solution)/shard_map/finish/pallas_call | solution.py:463
  (10 shorter events, 0.2 us)
Async XLA Ops:
  0.6 0.9 %copy-start.1 = (bf16[8,64,64]{2,1,0:T(8,128)(2,1)S(1)}, bf16[8,64,64]{2,1,0:T(8,128)(2,1)}, u32[]{:S(2)}) copy-start(bf16[8,64,64]{2,1,0:T(8,128)(2,1)} %w_ref.1) | copy-start | bytes 196612
  1.6 5.7 %collective-permute-start.2 = (bf16[4,64,128]{2,1,0:T(8,128)(2,1)S(1)}, bf16[4,64,128]{2,1,0:T(8,128)(2,1)S(1)}, u32[]{:S(2)}, u32[]{:S(2)}) collective-permute-start(bf16[4,64,128]{2,1,0:T(8,128)(2,1)S(1)} %get-tuple-element.29), channel_id=1, source_target_pairs={{0,1},{1,0},{2,3},{3,2},{4,5},{5,4},{6,7},{7,6},{8,9},{9,8},{10,11... | collective-permute-start | bytes 196616 | tf_op jit(solution)/shard_map/ppermute | solution.py:21
  4.7 8.6 %collective-permute-start = (bf16[4,64,128]{2,1,0:T(8,128)(2,1)S(1)}, bf16[4,64,128]{2,1,0:T(8,128)(2,1)S(1)}, u32[]{:S(2)}, u32[]{:S(2)}) collective-permute-start(bf16[4,64,128]{2,1,0:T(8,128)(2,1)S(1)} %get-tuple-element.28.refs_0_), channel_id=1, source_target_pairs={{0,2},{1,3},{2,0},{3,1},{4,6},{5,7},{6,4},{7,5},{8,10},{9,11},{10,... | collective-permute-start | bytes 196616 | tf_op jit(solution)/shard_map/ppermute | solution.py:21
  7.3 7.5 %collective-permute-start.1 = (bf16[4,64,128]{2,1,0:T(8,128)(2,1)S(1)}, bf16[4,64,128]{2,1,0:T(8,128)(2,1)S(1)}, u32[]{:S(2)}, u32[]{:S(2)}) collective-permute-start(bf16[4,64,128]{2,1,0:T(8,128)(2,1)S(1)} %get-tuple-element.29), channel_id=1, source_target_pairs={{0,3},{1,2},{2,1},{3,0},{4,7},{5,6},{6,5},{7,4},{8,11},{9,10},{10,... | collective-permute-start | bytes 196616 | tf_op jit(solution)/shard_map/ppermute | solution.py:21
  7.4 1.0 %copy-start = (bf16[2,8,128,64]{2,3,1,0:T(8,128)(2,1)S(1)}, bf16[2,8,128,64]{2,3,1,0:T(8,128)(2,1)}, u32[]{:S(2)}) copy-start(bf16[2,8,128,64]{2,3,1,0:T(8,128)(2,1)} %param.5) | copy-start | bytes 786436
  8.3 9.7 %collective-permute-start.3 = (bf16[4,64,128]{2,1,0:T(8,128)(2,1)S(1)}, bf16[4,64,128]{2,1,0:T(8,128)(2,1)S(1)}, u32[]{:S(2)}, u32[]{:S(2)}) collective-permute-start(bf16[4,64,128]{2,1,0:T(8,128)(2,1)S(1)} %get-tuple-element.32), channel_id=1, source_target_pairs={{0,1},{1,0},{2,3},{3,2},{4,5},{5,4},{6,7},{7,6},{8,9},{9,8},{10,11... | collective-permute-start | bytes 196616 | tf_op jit(solution)/shard_map/ppermute | solution.py:21
  10.1 8.1 %collective-permute-start.4 = (bf16[4,64,128]{2,1,0:T(8,128)(2,1)S(1)}, bf16[4,64,128]{2,1,0:T(8,128)(2,1)S(1)}, u32[]{:S(2)}, u32[]{:S(2)}) collective-permute-start(bf16[4,64,128]{2,1,0:T(8,128)(2,1)S(1)} %get-tuple-element.33), channel_id=1, source_target_pairs={{0,2},{1,3},{2,0},{3,1},{4,6},{5,7},{6,4},{7,5},{8,10},{9,11},{10,... | collective-permute-start | bytes 196616 | tf_op jit(solution)/shard_map/ppermute | solution.py:21
  13.3 6.1 %collective-permute-start.5 = (bf16[4,64,128]{2,1,0:T(8,128)(2,1)S(1)}, bf16[4,64,128]{2,1,0:T(8,128)(2,1)S(1)}, u32[]{:S(2)}, u32[]{:S(2)}) collective-permute-start(bf16[4,64,128]{2,1,0:T(8,128)(2,1)S(1)} %get-tuple-element.34), channel_id=1, source_target_pairs={{0,3},{1,2},{2,1},{3,0},{4,7},{5,6},{6,5},{7,4},{8,11},{9,10},{10,... | collective-permute-start | bytes 196616 | tf_op jit(solution)/shard_map/ppermute | solution.py:21
  13.3 6.2 %collective-permute-start.6 = (bf16[8,64,128]{2,1,0:T(8,128)(2,1)S(1)}, bf16[8,64,128]{2,1,0:T(8,128)(2,1)S(1)}, u32[]{:S(2)}, u32[]{:S(2)}) collective-permute-start(bf16[8,64,128]{2,1,0:T(8,128)(2,1)S(1)} %merge_tile.3.refs_0_.t_ref), channel_id=1, source_target_pairs={{0,8},{4,12},{8,0},{12,4},{1,9},{5,13},{9,1},{13,5},{2,10},{6,14},... | collective-permute-start | bytes 393224 | tf_op jit(solution)/shard_map/ppermute | solution.py:21
  14.8 5.0 %collective-permute-start.7 = (bf16[8,64,128]{2,1,0:T(8,128)(2,1)S(1)}, bf16[8,64,128]{2,1,0:T(8,128)(2,1)S(1)}, u32[]{:S(2)}, u32[]{:S(2)}) collective-permute-start(bf16[8,64,128]{2,1,0:T(8,128)(2,1)S(1)} %merge_tile.2.refs_0_.t_ref.refs_1_), channel_id=1, source_target_pairs={{0,8},{4,12},{8,0},{12,4},{1,9},{5,13},{9,1},{13,5},{2,10},{6,14},... | collective-permute-start | bytes 393224 | tf_op jit(solution)/shard_map/ppermute | solution.py:21
  18.1 2.1 %collective-permute-start.10 = (bf16[8,64,128]{2,1,0:T(8,128)(2,1)S(1)}, bf16[8,64,128]{2,1,0:T(8,128)(2,1)S(1)}, u32[]{:S(2)}, u32[]{:S(2)}) collective-permute-start(bf16[8,64,128]{2,1,0:T(8,128)(2,1)S(1)} %gate.6), channel_id=1, source_target_pairs={{0,4},{4,0},{8,12},{12,8},{1,5},{5,1},{9,13},{13,9},{2,6},{6,2},{1... | collective-permute-start | bytes 393224 | tf_op jit(solution)/shard_map/ppermute | solution.py:21
  18.2 2.0 %collective-permute-start.11 = (bf16[8,64,128]{2,1,0:T(8,128)(2,1)S(1)}, bf16[8,64,128]{2,1,0:T(8,128)(2,1)S(1)}, u32[]{:S(2)}, u32[]{:S(2)}) collective-permute-start(bf16[8,64,128]{2,1,0:T(8,128)(2,1)S(1)} %gate.7), channel_id=1, source_target_pairs={{0,4},{4,0},{8,12},{12,8},{1,5},{5,1},{9,13},{13,9},{2,6},{6,2},{1... | collective-permute-start | bytes 393224 | tf_op jit(solution)/shard_map/ppermute | solution.py:21
  19.5 1.4 %collective-permute-start.8 = (bf16[8,64,128]{2,1,0:T(8,128)(2,1)S(1)}, bf16[8,64,128]{2,1,0:T(8,128)(2,1)S(1)}, u32[]{:S(2)}, u32[]{:S(2)}) collective-permute-start(bf16[8,64,128]{2,1,0:T(8,128)(2,1)S(1)} %gate.4), channel_id=1, source_target_pairs={{0,4},{4,0},{8,12},{12,8},{1,5},{5,1},{9,13},{13,9},{2,6},{6,2},{1... | collective-permute-start | bytes 393224 | tf_op jit(solution)/shard_map/ppermute | solution.py:21
  19.9 1.4 %collective-permute-start.9 = (bf16[8,64,128]{2,1,0:T(8,128)(2,1)S(1)}, bf16[8,64,128]{2,1,0:T(8,128)(2,1)S(1)}, u32[]{:S(2)}, u32[]{:S(2)}) collective-permute-start(bf16[8,64,128]{2,1,0:T(8,128)(2,1)S(1)} %gate.5), channel_id=1, source_target_pairs={{0,4},{4,0},{8,12},{12,8},{1,5},{5,1},{9,13},{13,9},{2,6},{6,2},{1... | collective-permute-start | bytes 393224 | tf_op jit(solution)/shard_map/ppermute | solution.py:21
  22.5 1.6 %collective-permute-start.13 = (bf16[2,8,64,128]{3,2,1,0:T(8,128)(2,1)S(1)}, bf16[2,8,64,128]{3,2,1,0:T(8,128)(2,1)S(1)}, u32[]{:S(2)}, u32[]{:S(2)}) collective-permute-start(bf16[2,8,64,128]{3,2,1,0:T(8,128)(2,1)S(1)} %get-tuple-element.44), channel_id=1, source_target_pairs={{0,4},{4,0},{8,12},{12,8},{1,5},{5,1},{9,13},{13,9},{2,6},{6,2},{1... | collective-permute-start | bytes 786440 | tf_op jit(solution)/shard_map/ppermute | solution.py:21
  22.8 5.3 %collective-permute-start.12 = (bf16[2,8,64,128]{3,2,1,0:T(8,128)(2,1)S(1)}, bf16[2,8,64,128]{3,2,1,0:T(8,128)(2,1)S(1)}, u32[]{:S(2)}, u32[]{:S(2)}) collective-permute-start(bf16[2,8,64,128]{3,2,1,0:T(8,128)(2,1)S(1)} %get-tuple-element.42), channel_id=1, source_target_pairs={{0,4},{4,0},{8,12},{12,8},{1,5},{5,1},{9,13},{13,9},{2,6},{6,2},{1... | collective-permute-start | bytes 786440 | tf_op jit(solution)/shard_map/ppermute | solution.py:21
  24.1 5.7 %collective-permute-start.15 = (bf16[8,64,128]{2,1,0:T(8,128)(2,1)S(1)}, bf16[8,64,128]{2,1,0:T(8,128)(2,1)S(1)}, u32[]{:S(2)}, u32[]{:S(2)}) collective-permute-start(bf16[8,64,128]{2,1,0:T(8,128)(2,1)S(1)} %get-tuple-element.45.refs_0_), channel_id=1, source_target_pairs={{0,8},{4,12},{8,0},{12,4},{1,9},{5,13},{9,1},{13,5},{2,10},{6,14},... | collective-permute-start | bytes 393224 | tf_op jit(solution)/shard_map/ppermute | solution.py:21
  28.2 6.3 %collective-permute-start.14 = (bf16[8,64,128]{2,1,0:T(8,128)(2,1)S(1)}, bf16[8,64,128]{2,1,0:T(8,128)(2,1)S(1)}, u32[]{:S(2)}, u32[]{:S(2)}) collective-permute-start(bf16[8,64,128]{2,1,0:T(8,128)(2,1)S(1)} %get-tuple-element.48), channel_id=1, source_target_pairs={{0,1},{1,0},{2,3},{3,2},{4,5},{5,4},{6,7},{7,6},{8,9},{9,8},{10,11... | collective-permute-start | bytes 393224 | tf_op jit(solution)/shard_map/ppermute | solution.py:21
  29.9 6.1 %collective-permute-start.17 = (bf16[4,64,128]{2,1,0:T(8,128)(2,1)S(1)}, bf16[4,64,128]{2,1,0:T(8,128)(2,1)S(1)}, u32[]{:S(2)}, u32[]{:S(2)}) collective-permute-start(bf16[4,64,128]{2,1,0:T(8,128)(2,1)S(1)} %get-tuple-element.53), channel_id=1, source_target_pairs={{0,2},{1,3},{2,0},{3,1},{4,6},{5,7},{6,4},{7,5},{8,10},{9,11},{10,... | collective-permute-start | bytes 196616 | tf_op jit(solution)/shard_map/ppermute | solution.py:21
  32.8 6.1 %collective-permute-start.18 = (bf16[4,64,128]{2,1,0:T(8,128)(2,1)S(1)}, bf16[4,64,128]{2,1,0:T(8,128)(2,1)S(1)}, u32[]{:S(2)}, u32[]{:S(2)}) collective-permute-start(bf16[4,64,128]{2,1,0:T(8,128)(2,1)S(1)} %get-tuple-element.50.refs_2_), channel_id=1, source_target_pairs={{0,3},{1,2},{2,1},{3,0},{4,7},{5,6},{6,5},{7,4},{8,11},{9,10},{10,... | collective-permute-start | bytes 196616 | tf_op jit(solution)/shard_map/ppermute | solution.py:21
  34.5 4.4 %collective-permute-start.16 = (bf16[4,64,128]{2,1,0:T(8,128)(2,1)S(1)}, bf16[4,64,128]{2,1,0:T(8,128)(2,1)S(1)}, u32[]{:S(2)}, u32[]{:S(2)}) collective-permute-start(bf16[4,64,128]{2,1,0:T(8,128)(2,1)S(1)} %get-tuple-element.52), channel_id=1, source_target_pairs={{0,8},{4,12},{8,0},{12,4},{1,9},{5,13},{9,1},{13,5},{2,10},{6,14},... | collective-permute-start | bytes 196616 | tf_op jit(solution)/shard_map/ppermute | solution.py:21
